TPU v7x, 128 devices: a whole 4x4x4 slice. The times are simulated.
128 devices in a mesh: ctx: 16 (over y, z), mp: 8 (over x, core).
Axes of the slice: x: 4, y: 4, z: 4, core: 2. Of those that a mesh axis runs over, the one named last changes fastest.
Arguments:
- block_entry_states: bfloat16 [16384, 2304], P('ctx'), may hold values from -6 to 6
- dispatch_preference: float32 [16384], P('ctx'), may hold values from -8 to 8
- chosen_positions: int32 [4096], P('ctx'), may hold values from 0 to 1023, as said below
- occupied_places: int32 [16], P('ctx'), may hold values from 64 to 256, as said below
- premix_rescaling_vector: float32 [2304], replicated, may hold values from 0.1 to 1.9
- asking_matrix: bfloat16 [2304, 4096], P(None, 'mp'), may hold values from -0.125 to 0.125
- lookup_matrix: bfloat16 [2304, 2048], P(None, 'mp'), may hold values from -0.125 to 0.125
- content_matrix: bfloat16 [2304, 2048], P(None, 'mp'), may hold values from -0.125 to 0.125
- final_mixing_matrix: bfloat16 [4096, 2304], P('mp'), may hold values from -0.09375 to 0.09375
- sharpness_coefficient: float32 [32], P('mp'), may hold values from 0.5 to 64
- premlp_rescaling_vector: float32 [2304], replicated, may hold values from 0.1 to 1.9
- switch_matrix: bfloat16 [2304, 18432], P('ctx', 'mp'), may hold values from -0.125 to 0.125
- expand_matrix: bfloat16 [2304, 18432], P('ctx', 'mp'), may hold values from -0.125 to 0.125
- contract_matrix: bfloat16 [2304, 18432], P('ctx', 'mp'), may hold values from -0.046875 to 0.046875
Outputs:
- residual_out: bfloat16 [16384, 2304], P('ctx')
Inputs may be any that keep to these rules, and one draw needn't show every extreme that they name: `chosen_positions`: in each shard's block of 256 slots the first occupied_places entries are distinct positions within the shard in rising order; the remaining entries are other distinct positions of the shard and mean nothing. `occupied_places`: in every draw one shard has all 256 slots live.
All inputs are finite; a program needn't handle non-finite values.
Results may differ from a plain program's by a relative error of at most 0.0065.
Values may be sent and summed in bfloat16 or wider, within the bound.
No kernel may reach another device: no remote copies, remote signals or barrier semaphores. Data moves between devices by JAX's collectives and lax.ppermute only.
A program may use at most 128 MiB of HBM per device.

v0:
```python
import math

import jax
import jax.numpy as jnp
from jax import lax
from jax.sharding import PartitionSpec as P

PER_HEAD_DIM = 128


epsilon = 1e-06
far_position = 1073741824


def normalize(inputs, scaling):
    values = inputs.astype(jnp.float32)
    dot_product_divisor = lax.rsqrt(jnp.mean(values * values, axis=-1, keepdims=True) + epsilon)
    return (values * dot_product_divisor * scaling).astype(jnp.bfloat16)


def rotate(values, positions):
    half_dim = values.shape[-1] // 2
    frequency = 10000.0 ** (-jnp.arange(half_dim, dtype=jnp.float32) / half_dim)
    angles = positions.astype(jnp.float32)[:, None] * frequency[None, :]
    cosine = jnp.cos(angles)[:, None, :]
    sine_part = jnp.sin(angles)[:, None, :]
    front_half = values[..., :half_dim]
    back_half = values[..., half_dim:]
    return jnp.concatenate(
        [front_half * cosine - back_half * sine_part, back_half * cosine + front_half * sine_part],
        axis=-1,
    )


def project(normed, weight, positions, turned):
    values = jnp.dot(normed, weight, preferred_element_type=jnp.float32)
    values = values.reshape(normed.shape[0], weight.shape[1] // PER_HEAD_DIM, PER_HEAD_DIM)
    if turned:
        values = rotate(values, positions)
    return values.astype(jnp.bfloat16)


def local(
    block_entry_states,
    dispatch_preference,
    chosen_positions,
    occupied_places,
    premix_rescaling_vector,
    asking_matrix,
    lookup_matrix,
    content_matrix,
    final_mixing_matrix,
    sharpness_coefficient,
    premlp_rescaling_vector,
    switch_matrix,
    expand_matrix,
    contract_matrix,
):
    seq_dev = block_entry_states.shape[0]
    model_width = block_entry_states.shape[1]
    capacity = chosen_positions.shape[0]
    shard_id = lax.axis_index("ctx")
    slot_ids = jnp.arange(capacity, dtype=jnp.int32)
    live_slot = slot_ids < occupied_places[0]
    positions = shard_id * seq_dev + chosen_positions
    key_position = jnp.where(live_slot, positions, far_position)
    picked = block_entry_states[chosen_positions]
    router_gate = jax.nn.sigmoid(dispatch_preference[chosen_positions])
    normed = normalize(picked, premix_rescaling_vector)
    queries = project(normed, asking_matrix, positions, True)
    keys = project(normed, lookup_matrix, positions, True)
    values = project(normed, content_matrix, positions, False)
    head_count = queries.shape[1]
    memory_branch_number = keys.shape[1]
    askers_per_memory = head_count // memory_branch_number
    packed = jnp.stack([keys, values], axis=1)
    grouped = queries.reshape(capacity, memory_branch_number, askers_per_memory, PER_HEAD_DIM)
    dot_product_divisor = (sharpness_coefficient / math.sqrt(PER_HEAD_DIM)).reshape(
        memory_branch_number, askers_per_memory
    )[:, :, None, None]
    running_max = jnp.full((memory_branch_number, askers_per_memory, capacity), -1e30, jnp.float32)
    kv_block = lax.all_gather(packed, "ctx", axis=0, tiled=True)
    block_position = lax.all_gather(key_position, "ctx", axis=0, tiled=True)
    key_block = kv_block[:, 0]
    value_block = kv_block[:, 1]
    scores = (
        jnp.einsum("sgrd,tgd->grst", grouped, key_block, preferred_element_type=jnp.float32)
        * dot_product_divisor
    )
    allowed = block_position[None, None, None, :] <= positions[None, None, :, None]
    scores = jnp.where(allowed, scores, -1e30)
    new_max = jnp.maximum(running_max, jnp.max(scores, axis=-1))
    weights = jnp.exp(scores - new_max[..., None])
    running_sum = jnp.sum(weights, axis=-1)
    added = jnp.einsum(
        "grst,tgd->grsd",
        weights.astype(jnp.bfloat16),
        value_block,
        preferred_element_type=jnp.float32,
    )
    running_out = added
    running_max, running_sum, running_out = (new_max, running_sum, running_out)
    mixed_out = (running_out / running_sum[..., None]).astype(jnp.bfloat16)
    mixed_out = mixed_out.transpose(2, 0, 1, 3).reshape(capacity, head_count * PER_HEAD_DIM)
    partial_value = jnp.dot(mixed_out, final_mixing_matrix, preferred_element_type=jnp.float32)
    piece_width = model_width // lax.axis_size("mp")
    col_start = lax.axis_index("mp") * piece_width
    own_cols = lax.dynamic_slice_in_dim(picked, col_start, piece_width, 1).astype(jnp.float32)
    attention = lax.psum_scatter(
        partial_value.astype(jnp.bfloat16), "mp", scatter_dimension=1, tiled=True
    ).astype(jnp.float32)
    mid_state = lax.all_gather(
        (own_cols + attention).astype(jnp.bfloat16), "mp", axis=1, tiled=True
    )
    ffn_normed = normalize(mid_state, premlp_rescaling_vector)
    gate_act = jnp.dot(
        ffn_normed,
        lax.all_gather(switch_matrix, "ctx", axis=0, tiled=True),
        preferred_element_type=jnp.float32,
    )
    up_act = jnp.dot(
        ffn_normed,
        lax.all_gather(expand_matrix, "ctx", axis=0, tiled=True),
        preferred_element_type=jnp.float32,
    )
    hidden = (jax.nn.silu(gate_act) * up_act).astype(jnp.bfloat16)
    feed_out = lax.psum_scatter(
        lax.dot_general(
            hidden,
            lax.all_gather(contract_matrix, "ctx", axis=0, tiled=True),
            (((1,), (1,)), ((), ())),
            preferred_element_type=jnp.float32,
        ).astype(jnp.bfloat16),
        "mp",
        scatter_dimension=1,
        tiled=True,
    ).astype(jnp.float32)
    result_cols = (own_cols + router_gate[:, None] * (attention + feed_out)).astype(jnp.bfloat16)
    result = lax.all_gather(result_cols, "mp", axis=1, tiled=True)
    target = jnp.where(live_slot, chosen_positions, seq_dev)
    return block_entry_states.at[target].set(result, mode="drop")


def solution(mesh):
    return jax.shard_map(
        local,
        mesh=mesh,
        in_specs=(
            P("ctx", None),
            P("ctx"),
            P("ctx"),
            P("ctx"),
            P(),
            P(None, "mp"),
            P(None, "mp"),
            P(None, "mp"),
            P("mp", None),
            P("mp"),
            P(),
            P("ctx", "mp"),
            P("ctx", "mp"),
            P("ctx", "mp"),
        ),
        out_specs=P("ctx", None),
        check_vma=False,
    )
```

profile of v0, /device:TPU:1, one launch (start us, length us, event | category | flops | bytes accessed | tf_op | source)
XLA Modules:
  0.0 499.6 jit_solution(1045636341385218684)
XLA Ops:
  6.5 5.0 copy.53
  13.3 5.5 %gather_fusion = bf16[256,2304]{1,0:T(8,128)(2,1)S(1)} fusion(bf16[1024,2304]{1,0:T(8,128)(2,1)} %copy.53, s32[1024]{0:T(1024)S(1)} %pad_clamp_fusion), kind=kCustom, calls=%fused_computation | custom fusion | bytes 2360320 | tf_op jit(solution)/shard_map/gather | solution.py:67
  19.1 2.0 fusion.42
  21.9 1.8 copy.48
  25.4 2.7 convolution_convert_fusion.2
  34.4 3.3 fusion.39
  37.7 2.0 reshape.170
  44.8 21.1 %all-gather = s32[16,1,256]{2,1,0:T(1,128)S(1)} all-gather(s32[1,1,256]{2,1,0:T(1,128)S(1)} %bitcast.70), channel_id=1, replica_groups=mesh['ctx'=16,'mp'=8] {'ctx'}, dimensions={0}, use_global_device_ids=true | all-gather | bytes 17408 | tf_op jit(solution)/shard_map/all_gather | solution.py:83
  65.9 2.7 broadcast_compare_fusion
  68.6 20.8 %all-gather.8.cloned.1.call-done = bf16[4096,2,2,128]{3,0,2,1:T(8,128)(2,1)} async-done(((bf16[256,2,2,128]{3,0,2,1:T(8,128)(2,1)}), bf16[4096,2,2,128]{3,0,2,1:T(8,128)(2,1)}) %all-gather.8.cloned.1.call-update) | async-done | bytes 4194320 | tf_op jit(solution)/shard_map/all_gather | solution.py:82
  89.4 4.6 fusion.2
  94.1 3.9 fusion
  97.9 6.6 %fusion.20 = bf16[256,2,2,128]{0,3,2,1:T(8,128)(2,1)S(1)} fusion(bf16[4096,2,2,128]{3,0,2,1:T(8,128)(2,1)} %all-gather.8.cloned.1.call-done, f32[2,4096,256,2]{2,1,3,0:T(8,128)S(1)} %get-tuple-element.18, f32[2,2,256]{2,1,0:T(2,128)S(1)} %broadcast_maximum_fusion, f32[2,2]{1,0:T(2,128)S(1)} %copy-done.10, pred[256,4096]{0,1:T(8,128)(4,1)} %broadcast_compare_fusion, ...), kind=kOutput, calls=%fused_computation.31 | convolution fusion | flops 1090781184 | bytes 20193296 | tf_op jit(solution)/shard_map/grst,tgd->grsd/dot_general | solution.py:95
  104.6 2.1 convolution_convert_fusion.1
  107.0 28.6 %reduce-scatter.3.cloned.1.call-done = bf16[256,288]{0,1:T(8,128)(2,1)} async-done(((bf16[256,2304]{0,1:T(8,128)(2,1)}), bf16[256,288]{0,1:T(8,128)(2,1)}) %reduce-scatter.3.cloned.1.call-update) | async-done | bytes 147472 | tf_op jit(solution)/shard_map/reduce_scatter | solution.py:109
  139.3 23.8 %all-gather.10.cloned.1.call-done = bf16[256,2304]{0,1:T(8,128)(2,1)} async-done(((bf16[256,288]{0,1:T(8,128)(2,1)}), bf16[256,2304]{0,1:T(8,128)(2,1)}) %all-gather.10.cloned.1.call-update) | async-done | bytes 1179664 | tf_op jit(solution)/shard_map/all_gather | solution.py:112
  164.8 81.2 %all-gather.12.cloned.1.call-done = bf16[2304,2304]{1,0:T(8,128)(2,1)} async-done(((bf16[144,2304]{1,0:T(8,128)(2,1)}), bf16[2304,2304]{1,0:T(8,128)(2,1)}) %all-gather.12.cloned.1.call-update) | async-done | bytes 10616848 | tf_op jit(solution)/shard_map/all_gather | solution.py:118
  246.0 8.5 %fusion.25 = f32[256,2304]{1,0:T(8,128)} fusion(bf16[2304,2304]{1,0:T(8,128)(2,1)} %all-gather.12.cloned.1.call-done, bf16[256,2304]{0,1:T(8,128)(2,1)S(1)} %copy-done.3, f32[2304]{0:T(1024)S(1)} %copy-done.8, f32[256]{0:T(256)S(1)} %add_rsqrt_fusion), kind=kOutput, calls=%fused_computation.37 | convolution fusion | flops 2720268288 | bytes 14166016 | tf_op jit(solution)/shard_map/dot_general | solution.py:116
  254.4 74.3 %all-gather.14.cloned.1.call-done = bf16[2304,2304]{1,0:T(8,128)(2,1)} async-done(((bf16[144,2304]{1,0:T(8,128)(2,1)}), bf16[2304,2304]{1,0:T(8,128)(2,1)}) %all-gather.14.cloned.1.call-update) | async-done | bytes 10616848 | tf_op jit(solution)/shard_map/all_gather | solution.py:123
  328.7 82.8 %all-gather.16.cloned.1.call-done = bf16[2304,2304]{1,0:T(8,128)(2,1)} async-done(((bf16[144,2304]{1,0:T(8,128)(2,1)}), bf16[2304,2304]{1,0:T(8,128)(2,1)}) %all-gather.16.cloned.1.call-update) | async-done | bytes 10616848 | tf_op jit(solution)/shard_map/all_gather | solution.py:130
  411.5 15.3 %convolution_convert_fusion = bf16[256,2304]{0,1:T(8,128)(2,1)} fusion(bf16[2304,2304]{1,0:T(8,128)(2,1)} %all-gather.16.cloned.1.call-done, bf16[2304,2304]{1,0:T(8,128)(2,1)} %all-gather.14.cloned.1.call-done, f32[256,2304]{1,0:T(8,128)} %fusion.25, bf16[256,2304]{0,1:T(8,128)(2,1)S(1)} %copy-done.3, f32[2304]{0:T(1024)S(1)} %copy-done.8, ...), kind=kOutput, calls=%fused_computation.11 | convolution fusion | flops 5442306048 | bytes 25962496 | tf_op jit(solution)/shard_map/dot_general | solution.py:128
  428.5 27.3 %reduce-scatter.5.cloned.1.call-done = bf16[256,288]{0,1:T(8,128)(2,1)} async-done(((bf16[256,2304]{0,1:T(8,128)(2,1)}), bf16[256,288]{0,1:T(8,128)(2,1)}) %reduce-scatter.5.cloned.1.call-update) | async-done | bytes 147472 | tf_op jit(solution)/shard_map/reduce_scatter | solution.py:127
  457.5 25.8 %all-gather.18.cloned.1.call-done = bf16[256,2304]{0,1:T(8,128)(2,1)} async-done(((bf16[256,288]{0,1:T(8,128)(2,1)}), bf16[256,2304]{0,1:T(8,128)(2,1)}) %all-gather.18.cloned.1.call-update) | async-done | bytes 1179664 | tf_op jit(solution)/shard_map/all_gather | solution.py:139
  484.9 7.8 %scatter_fusion = bf16[1024,2304]{1,0:T(8,128)(2,1)} fusion(bf16[1024,2304]{1,0:T(8,128)(2,1)} %copy.53, s32[256]{0:T(256)S(1)} %get-tuple-element.16, bf16[256,2304]{1,0:T(8,128)(2,1)S(1)} %copy.41), kind=kCustom, calls=%fused_computation.2 | custom fusion | bytes 3539968 | tf_op jit(solution)/shard_map/scatter | solution.py:141
  (71 shorter events, 25.8 us)
Async XLA Ops:
  6.5 98.1 %copy-start = (bf16[512,2304]{1,0:T(8,128)(2,1)S(1)}, bf16[512,2304]{1,0:T(8,128)(2,1)}, u32[]{:S(2)}) copy-start(bf16[512,2304]{1,0:T(8,128)(2,1)} %param.22) | copy-start | bytes 7077892
  6.5 82.9 %all-gather.8.cloned.1.call-start = ((), (), s32[]{:S(2)}) async-start(), calls=%async_computation.2 | async-start | bytes 4456448 | tf_op jit(solution)/shard_map/all_gather | solution.py:82
  6.5 6.1 %copy-start.12 = (s32[256]{0:T(256)S(1)}, s32[256]{0:T(256)}, u32[]{:S(2)}) copy-start(s32[256]{0:T(256)} %param.16) | copy-start | bytes 3076
  19.1 2.8 copy-start.11
  30.8 0.7 copy-start.5
  30.8 1.8 copy-start.6
  34.3 101.3 %reduce-scatter.3.cloned.1.call-start = ((), (), s32[]{:S(2)}) async-start(), calls=%async_computation.3 | async-start | bytes 1327104 | tf_op jit(solution)/shard_map/reduce_scatter | solution.py:109
  37.7 7.1 %copy-start.9 = (s32[256]{0:T(256)S(1)}, s32[256]{0:T(256)}, u32[]{:S(2)}) copy-start(s32[256]{0:T(256)} %get-tuple-element.5) | copy-start | bytes 3076
  39.7 3.2 copy-start.13
  89.4 4.6 copy-start.4
  89.4 4.6 copy-start.10
  106.7 139.3 %copy-start.8 = (f32[2304]{0:T(1024)S(1)}, f32[2304]{0:T(1024)}, u32[]{:S(2)}) copy-start(f32[2304]{0:T(1024)} %param.24) | copy-start | bytes 27652
  106.7 56.4 %all-gather.10.cloned.1.call-start = ((), (), s32[]{:S(2)}) async-start(), calls=%async_computation.4 | async-start | bytes 1327104 | tf_op jit(solution)/shard_map/all_gather | solution.py:112
  137.3 108.7 %all-gather.12.cloned.1.call-start = ((), (), s32[]{:S(2)}) async-start(), calls=%async_computation.5 | async-start | bytes 11280384 | tf_op jit(solution)/shard_map/all_gather | solution.py:118
  137.9 190.9 %all-gather.14.cloned.1.call-start = ((), (), s32[]{:S(2)}) async-start(), calls=%async_computation.6 | async-start | bytes 11280384 | tf_op jit(solution)/shard_map/all_gather | solution.py:123
  138.5 273.0 %all-gather.16.cloned.1.call-start = ((), (), s32[]{:S(2)}) async-start(), calls=%async_computation.7 | async-start | bytes 11280384 | tf_op jit(solution)/shard_map/all_gather | solution.py:130
  139.0 316.8 %reduce-scatter.5.cloned.1.call-start = ((), (), s32[]{:S(2)}) async-start(), calls=%async_computation.8 | async-start | bytes 1327104 | tf_op jit(solution)/shard_map/reduce_scatter | solution.py:127
  163.1 82.9 %copy-start.3 = (bf16[256,2304]{0,1:T(8,128)(2,1)S(1)}, bf16[256,2304]{0,1:T(8,128)(2,1)}, u32[]{:S(2)}) copy-start(bf16[256,2304]{0,1:T(8,128)(2,1)} %all-gather.10.cloned.1.call-done) | copy-start | bytes 3538948
  254.4 172.7 %copy-start.2 = (f32[1024]{0:T(1024)S(1)}, f32[1024]{0:T(1024)}, u32[]{:S(2)}) copy-start(f32[1024]{0:T(1024)} %param.15) | copy-start | bytes 12292
  254.4 201.4 %copy-start.7 = (bf16[256,288]{0,1:T(8,128)(2,1)S(1)}, bf16[256,288]{0,1:T(8,128)(2,1)}, u32[]{:S(2)}) copy-start(bf16[256,288]{0,1:T(8,128)(2,1)} %reduce-scatter.3.cloned.1.call-done) | copy-start | bytes 442372
  426.8 56.5 %all-gather.18.cloned.1.call-start = ((), (), s32[]{:S(2)}) async-start(), calls=%async_computation.9 | async-start | bytes 1327104 | tf_op jit(solution)/shard_map/all_gather | solution.py:139
  484.9 7.8 %copy-start.1 = (bf16[512,2304]{1,0:T(8,128)(2,1)S(1)}, bf16[512,2304]{1,0:T(8,128)(2,1)}, u32[]{:S(2)}) copy-start(bf16[512,2304]{1,0:T(8,128)(2,1)} %param.22) | copy-start | bytes 7077892
Sparse Core Ops, SparseCore 0:
  34.5 54.9 all-gather.7
  106.8 28.8 reduce-scatter.2
  137.4 25.6 all-gather.9
  165.1 80.7 all-gather.11
  248.0 80.6 all-gather.13
  330.8 80.6 all-gather.15
  427.0 28.8 reduce-scatter.4
  457.7 25.6 all-gather.17
where the time goes:
time: 500 us
  waiting for transfers between devices  366 us (73%)
  matrix products  45.1 us (9%)
  local copies, waits for them, and re-layouts  32.8 us (7%)
  blocking collectives  21.1 us (4%)
  other arithmetic  19.2 us (4%)
  between operations  14.4 us (3%)
    all_gather x1, waiting for transfers between devices, local(): lax.all_gather(contract_matrix, 'ctx', axis=0, tiled=True)  82.8 us
    all_gather x1, waiting for transfers between devices, local(): lax.all_gather(switch_matrix, 'ctx', axis=0, tiled=True)  81.2 us
    all_gather x1, waiting for transfers between devices, local(): lax.all_gather(expand_matrix, 'ctx', axis=0, tiled=True)  74.3 us
    reduce_scatter x1, waiting for transfers between devices, local(): lax.psum_scatter(partial_value.astype(jnp.bfloat16), 'mp', scatter_dimens...  28.6 us
    reduce_scatter x1, waiting for transfers between devices, local(): lax.psum_scatter(lax.dot_general(hidden, lax.all_gather(contract_matrix,...  27.3 us
    all_gather x1, waiting for transfers between devices, local(): result = lax.all_gather(result_cols, 'mp', axis=1, tiled=True)  25.8 us
    all_gather x1, waiting for transfers between devices, local(): lax.all_gather((own_cols + attention).astype(jnp.bfloat16), 'mp', axis=1,...  23.8 us
    all_gather x1, blocking collectives, local(): block_position = lax.all_gather(key_position, 'ctx', axis=0, tiled=True)  21.1 us
  transfers between devices with their start and end apart: 8, of which 8 were waited for; matrix products, arithmetic and copies ran while one was open for 5% of the time, Pallas kernels for 0%

commit v1 on v0

v1 whole, which is shorter than its diff:
```python
import functools
import math

import jax
import jax.numpy as jnp
from jax import lax
from jax.experimental import pallas as pl
from jax.experimental.pallas import tpu as pltpu
from jax.sharding import Mesh, PartitionSpec as P

D = 2304
CAP = 256
SEQ_DEV = 1024
HD = 128
FF_DEV = 1152
ROWS = 144
OWN = 32
EPS = 1e-06
NEG = -1e30
LOG2E = 1.4426950408889634
MB = 1024 * 1024
F32 = jnp.float32
BF16 = jnp.bfloat16


def vmem_spec():
    return pl.BlockSpec(memory_space=pltpu.VMEM)


def smem_spec():
    return pl.BlockSpec(memory_space=pltpu.SMEM)


def any_spec():
    return pl.BlockSpec(memory_space=pl.ANY)


def params(mib):
    return pltpu.CompilerParams(vmem_limit_bytes=mib * MB)


def project_body(info, block, chosen, gain, cosine, sine, wq_hbm, wk_hbm, wv_hbm,
                 q_out, kv_out, own_out, picked, normed, wq, wk, wv, sems):
    copies = [pltpu.make_async_copy(src, dst, sems.at[i])
              for i, (src, dst) in enumerate(((wq_hbm, wq), (wk_hbm, wk), (wv_hbm, wv)))]
    for copy in copies:
        copy.start()
    lanes = lax.broadcasted_iota(jnp.int32, (CAP, SEQ_DEV), 1)
    one_hot = jnp.where(lanes == chosen[...], 1.0, 0.0).astype(BF16)

    def pick(i, total):
        cols = pl.ds(pl.multiple_of(i * 256, 256), 256)
        part = jnp.dot(one_hot, block[:, cols], preferred_element_type=F32)
        picked[:, cols] = part.astype(BF16)
        return total + part * part

    total = lax.fori_loop(0, D // 256, pick, jnp.zeros((CAP, 256), F32))
    inv = lax.rsqrt(jnp.sum(total, axis=1, keepdims=True) / D + EPS)
    for i in range(D // 256):
        cols = slice(i * 256, (i + 1) * 256)
        normed[:, cols] = (picked[:, cols].astype(F32) * inv * gain[:, cols]).astype(BF16)
    own_out[...] = picked[pl.ds(pl.multiple_of(info[0], OWN), OWN), :]

    def turn(values):
        return values * cosine[...] + pltpu.roll(values, HD // 2, 1) * sine[...]

    copies[1].wait()
    keys = jnp.dot(normed[...], wk[...], preferred_element_type=F32)
    for h in range(2):
        kv_out[0:CAP, h * HD:(h + 1) * HD] = turn(keys[:, h * HD:(h + 1) * HD]).astype(BF16)
    copies[2].wait()
    kv_out[0:CAP, 256:512] = jnp.dot(normed[...], wv[...], preferred_element_type=F32).astype(BF16)
    kv_out[CAP:CAP + 16, :] = jnp.full((16, 512), info[1].astype(F32), F32).astype(BF16)
    copies[0].wait()
    for j in range(2):
        part = jnp.dot(normed[...], wq[:, j * 256:(j + 1) * 256], preferred_element_type=F32)
        for h in range(2):
            at = j * 256 + h * HD
            q_out[:, at:at + HD] = turn(part[:, h * HD:(h + 1) * HD]).astype(BF16)


def project(info, block, chosen, gain, cosine, sine, wq, wk, wv):
    return pl.pallas_call(
        project_body,
        out_shape=(jax.ShapeDtypeStruct((CAP, 512), BF16),
                   jax.ShapeDtypeStruct((CAP + 16, 512), BF16),
                   jax.ShapeDtypeStruct((OWN, D), BF16)),
        in_specs=[smem_spec()] + [vmem_spec()] * 5 + [any_spec()] * 3,
        out_specs=(vmem_spec(),) * 3,
        scratch_shapes=[pltpu.VMEM((CAP, D), BF16), pltpu.VMEM((CAP, D), BF16),
                        pltpu.VMEM((D, 512), BF16), pltpu.VMEM((D, 256), BF16),
                        pltpu.VMEM((D, 256), BF16), pltpu.SemaphoreType.DMA((3,))],
        compiler_params=params(28),
        name="project",
    )(info, block, chosen, gain, cosine, sine, wq, wk, wv)


def attend_body(diagonal, allow, scale, q, kv0, kv1, kv2, kv3, out, stats, values):
    kvs = (kv0, kv1, kv2, kv3)
    lane = lax.broadcasted_iota(jnp.int32, (1, CAP), 1).astype(F32)
    bias = []
    for j, kv in enumerate(kvs):
        count = kv[CAP:CAP + 16, 0:CAP].astype(F32)[0:1, :]
        live = (lane < count) & (allow[j] > 0)
        bias.append(jnp.where(live, 0.0, NEG))
    for g in range(2):
        for h in range(2):
            head = 2 * g + h
            for r in range(2):
                rows = slice(r * 128, (r + 1) * 128)
                query = q[rows, head * HD:(head + 1) * HD]
                scores = []
                for j, kv in enumerate(kvs):
                    part = lax.dot_general(query, kv[0:CAP, g * HD:(g + 1) * HD],
                                           (((1,), (1,)), ((), ())), preferred_element_type=F32)
                    part = part * scale[head] + bias[j]
                    if diagonal and j == 0:
                        slot = lax.broadcasted_iota(jnp.int32, (128, CAP), 0) + r * 128
                        key = lax.broadcasted_iota(jnp.int32, (128, CAP), 1)
                        part = jnp.where(key <= slot, part, NEG)
                    scores.append(part)
                top = functools.reduce(jnp.maximum, scores)
                top = jnp.max(top, axis=1, keepdims=True)
                total = jnp.zeros((128, CAP), F32)
                mixed = jnp.zeros((128, HD), F32)
                for j, kv in enumerate(kvs):
                    weight = jnp.exp2(scores[j] - top)
                    total = total + weight
                    mixed = mixed + jnp.dot(weight.astype(BF16),
                                            kv[0:CAP, 256 + g * HD:256 + (g + 1) * HD],
                                            preferred_element_type=F32)
                total = jnp.sum(total, axis=1, keepdims=True)
                out[rows, head * HD:(head + 1) * HD] = (mixed / total).astype(BF16)
                log_sum = top + jnp.log2(total)
                first = log_sum.astype(BF16).astype(F32)
                second = (log_sum - first).astype(BF16).astype(F32)
                third = log_sum - first - second
                stats[rows, head:head + 1] = first
                stats[rows, 4 + head:5 + head] = second
                stats[rows, 8 + head:9 + head] = third
    lanes = lax.broadcasted_iota(jnp.int32, (CAP, 128), 1)
    clean = jnp.where(lanes < 12, stats[...], 0.0)
    out[CAP:CAP + 16, 0:CAP] = jnp.transpose(clean)[0:16, :].astype(BF16)
    out[CAP:CAP + 16, CAP:512] = jnp.zeros((16, 512 - CAP), BF16)


def attend(diagonal, allow, scale, q, kvs):
    return pl.pallas_call(
        functools.partial(attend_body, diagonal),
        out_shape=jax.ShapeDtypeStruct((CAP + 16, 512), BF16),
        in_specs=[smem_spec(), smem_spec()] + [vmem_spec()] * 5,
        out_specs=vmem_spec(),
        scratch_shapes=[pltpu.VMEM((CAP, 128), F32), pltpu.VMEM((8, 128), F32)],
        compiler_params=params(16),
        name="attend",
    )(allow, scale, q, *kvs)


def mix_body(info, p0, p1, p2, p3, wo, keep, send, mixed):
    parts = (p0, p1, p2, p3)
    logs = []
    for part in parts:
        rows = part[CAP:CAP + 16, 0:CAP].astype(F32)
        rows = jnp.concatenate([rows, jnp.zeros((112, CAP), F32)], axis=0)
        logs.append(jnp.transpose(rows))
    for head in range(4):
        cols = slice(head * HD, (head + 1) * HD)
        each = [log[:, head:head + 1] + log[:, 4 + head:5 + head] + log[:, 8 + head:9 + head] for log in logs]
        top = functools.reduce(jnp.maximum, each)
        weights = [jnp.exp2(one - top) for one in each]
        total = functools.reduce(jnp.add, weights)
        value = functools.reduce(jnp.add, [w * part[0:CAP, cols].astype(F32) for w, part in zip(weights, parts)])
        mixed[:, cols] = (value / total).astype(BF16)
    core = info[2]
    mine = mixed[pl.ds(pl.multiple_of(core * 128, 128), 128), :]
    other = mixed[pl.ds(pl.multiple_of((1 - core) * 128, 128), 128), :]

    @pl.loop(0, D // 256)
    def _(i):
        cols = pl.ds(pl.multiple_of(i * 256, 256), 256)
        send[:, cols] = jnp.dot(other, wo[:, cols], preferred_element_type=F32).astype(BF16)
        keep[:, cols] = jnp.dot(mine, wo[:, cols], preferred_element_type=F32)


def mix(info, parts, wo):
    return pl.pallas_call(
        mix_body,
        out_shape=(jax.ShapeDtypeStruct((128, D), F32), jax.ShapeDtypeStruct((128, D), BF16)),
        in_specs=[smem_spec()] + [vmem_spec()] * 5,
        out_specs=(vmem_spec(),) * 2,
        scratch_shapes=[pltpu.VMEM((CAP, 512), BF16)],
        compiler_params=params(16),
        name="mix",
    )(info, *parts, wo)


def split_body(info, keep, got, own, s1, s2, s3):
    x = info[3]
    for d, ref in enumerate((own, s1, s2, s3)):
        rows = pl.ds(pl.multiple_of(lax.rem(x + d, 4) * OWN, OWN), OWN)
        ref[...] = (keep[rows, :] + got[rows, :].astype(F32)).astype(ref.dtype)


def split(info, keep, got):
    piece = jax.ShapeDtypeStruct((OWN, D), BF16)
    return pl.pallas_call(
        split_body,
        out_shape=(jax.ShapeDtypeStruct((OWN, D), F32), piece, piece, piece),
        in_specs=[smem_spec()] + [vmem_spec()] * 2,
        out_specs=(vmem_spec(),) * 4,
        compiler_params=params(16),
        name="split",
    )(info, keep, got)


def middle_body(picked, own, r1, r2, r3, gain, attention, normed):
    total = own[...] + r1[...].astype(F32) + r2[...].astype(F32) + r3[...].astype(F32)
    attention[...] = total
    mid = (picked[...].astype(F32) + total).astype(BF16).astype(F32)
    inv = lax.rsqrt(jnp.mean(mid * mid, axis=1, keepdims=True) + EPS)
    normed[...] = (mid * inv * gain[...]).astype(BF16)


def middle(picked, own, got, gain):
    return pl.pallas_call(
        middle_body,
        out_shape=(jax.ShapeDtypeStruct((OWN, D), F32), jax.ShapeDtypeStruct((OWN, D), BF16)),
        in_specs=[vmem_spec()] * 6,
        out_specs=(vmem_spec(),) * 2,
        compiler_params=params(16),
        name="middle",
    )(picked, own, *got, gain)


def feed_body(*refs):
    place = refs[0]
    xs = refs[1:17]
    pieces = refs[17:33]
    outs = refs[33:49]
    tokens, gate_up, down, hidden, sems = refs[49:]
    first = [pltpu.make_async_copy(piece.at[:, 0:D],
                                   gate_up.at[pl.ds(pl.multiple_of(place[i] * ROWS, 16), ROWS), :],
                                   sems.at[i])
             for i, piece in enumerate(pieces)]
    second = [pltpu.make_async_copy(piece.at[:, D:D + FF_DEV],
                                    down.at[pl.ds(pl.multiple_of(place[i] * ROWS, 16), ROWS), :],
                                    sems.at[16 + i])
              for i, piece in enumerate(pieces)]
    for copy in first + second:
        copy.start()
    for i, x in enumerate(xs):
        tokens[i * OWN:(i + 1) * OWN, :] = x[...]
    for copy in first:
        copy.wait()

    @pl.loop(0, FF_DEV // 128)
    def _(j):
        both = jnp.dot(tokens[...], gate_up[:, pl.ds(pl.multiple_of(j * 256, 256), 256)],
                       preferred_element_type=F32)
        gate = both[:, 0:128]
        up = both[:, 128:256]
        hidden[:, pl.ds(pl.multiple_of(j * 128, 128), 128)] = (
            gate / (1.0 + jnp.exp(-gate)) * up).astype(BF16)

    for copy in second:
        copy.wait()

    @pl.loop(0, D // 256)
    def _(n):
        rows = pl.ds(pl.multiple_of(n * 256, 256), 256)
        part = lax.dot_general(hidden[...], down[rows, :], (((1,), (1,)), ((), ())),
                               preferred_element_type=F32).astype(BF16)
        for i, out in enumerate(outs):
            out[:, rows] = part[i * OWN:(i + 1) * OWN, :]


def feed(place, xs, pieces):
    return pl.pallas_call(
        feed_body,
        out_shape=(jax.ShapeDtypeStruct((OWN, D), BF16),) * 16,
        in_specs=[smem_spec()] + [vmem_spec()] * 16 + [any_spec()] * 16,
        out_specs=(vmem_spec(),) * 16,
        scratch_shapes=[pltpu.VMEM((512, D), BF16), pltpu.VMEM((D, D), BF16),
                        pltpu.VMEM((D, FF_DEV), BF16), pltpu.VMEM((512, FF_DEV), BF16),
                        pltpu.SemaphoreType.DMA((32,))],
        compiler_params=params(36),
        name="feed",
    )(place, *xs, *pieces)


def finish_body(picked, attention, gate, *refs):
    total = attention[...]
    for ref in refs[:16]:
        total = total + ref[...].astype(F32)
    refs[16][...] = (picked[...].astype(F32) + gate[...] * total).astype(BF16)


def finish(picked, attention, gate, parts):
    return pl.pallas_call(
        finish_body,
        out_shape=jax.ShapeDtypeStruct((OWN, D), BF16),
        in_specs=[vmem_spec()] * 19,
        out_specs=vmem_spec(),
        compiler_params=params(16),
        name="finish",
    )(picked, attention, gate, *parts)


def place_body(info, chosen, block, *refs):
    pieces = refs[:8]
    out = refs[8]
    rows = refs[9]

    @pl.when(pl.program_id(0) == 0)
    def _():
        for i, piece in enumerate(pieces):
            rows[pl.ds(pl.multiple_of(info[8 + i] * OWN, OWN), OWN), :] = piece[...]

    position = lax.broadcasted_iota(jnp.int32, (128, CAP), 0) + pl.program_id(0) * 128
    slot = lax.broadcasted_iota(jnp.int32, (128, CAP), 1)
    hit = jnp.where((position == chosen[...]) & (slot < info[1]), 1.0, 0.0)
    taken = jnp.sum(hit, axis=1, keepdims=True) > 0.5
    hit = hit.astype(BF16)
    for n in range(D // 256):
        cols = slice(n * 256, (n + 1) * 256)
        new = jnp.dot(hit, rows[:, cols], preferred_element_type=F32).astype(BF16)
        out[:, cols] = jnp.where(taken, new, block[:, cols])


def put_back(info, chosen, block, pieces):
    return pl.pallas_call(
        place_body,
        grid=(SEQ_DEV // 128,),
        out_shape=jax.ShapeDtypeStruct((SEQ_DEV, D), BF16),
        in_specs=[smem_spec(), pl.BlockSpec((1, CAP), lambda i: (0, 0)),
                  pl.BlockSpec((128, D), lambda i: (i, 0))]
        + [pl.BlockSpec((OWN, D), lambda i: (0, 0))] * 8,
        out_specs=pl.BlockSpec((128, D), lambda i: (i, 0)),
        scratch_shapes=[pltpu.VMEM((CAP, D), BF16)],
        compiler_params=params(16),
        name="put_back",
    )(info, chosen, block, *pieces)


def shift(value, axis, step, size=4):
    return lax.ppermute(value, axis, [(i, (i + step) % size) for i in range(size)])


def shift2(value, dy, dx):
    pairs = [(4 * y + x, 4 * ((y + dy) % 4) + (x + dx) % 4) for y in range(4) for x in range(4)]
    return lax.ppermute(value, ("y", "x"), pairs)


def shift_mp(value, dx, dc):
    pairs = [(2 * x + c, 2 * ((x + dx) % 4) + (c + dc) % 2) for x in range(4) for c in range(2)]
    return lax.ppermute(value, ("x", "c"), pairs)


def weight_pieces(y, z, c, gate, up, down):
    packs = []
    for half in range(2):
        cols = slice(half * FF_DEV, (half + 1) * FF_DEV)
        both = jnp.stack([gate[:, cols].reshape(ROWS, 9, 128), up[:, cols].reshape(ROWS, 9, 128)], axis=2)
        packs.append(jnp.concatenate([both.reshape(ROWS, D), down[:, cols]], axis=1))
    got = []
    for s in range(2):
        pairs = []
        for sy in range(4):
            for sc in range(2):
                target = 2 * sc + (sy + s) % 2
                pairs.append((2 * sy + sc, 2 * target + sy // 2))
        send = jnp.where((y + s) % 2 == 0, packs[0], packs[1])
        got.append(lax.ppermute(send, ("y", "c"), pairs))
    ahead = [shift(piece, "z", 1) for piece in got]
    back = [shift(piece, "z", 3) for piece in got]
    far = [shift(ahead[0], "z", 1), shift(back[1], "z", 3)]
    mine = [(got, z), (ahead, (z + 3) % 4), (back, (z + 1) % 4), (far, (z + 2) % 4)]
    pieces, place = [], []
    for core in range(2):
        for four, source_z in mine:
            for s, piece in enumerate(four):
                if core == 0:
                    pieces.append(piece)
                    source_y = 2 * c + (y + s) % 2
                else:
                    pieces.append(shift(piece, "c", 1, 2))
                    source_y = 2 * (1 - c) + (y + s) % 2
                place.append(4 * source_y + source_z)
    return pieces, jnp.stack(place).astype(jnp.int32)


def local(block, preference, chosen, occupied, gain1, wq, wk, wv, wo, sharpness, gain2, gate_w, up_w, down_w):
    y, z, x, c = (lax.axis_index(n) for n in ("y", "z", "x", "c"))
    own_at = c * 128 + x * OWN
    order = [2 * 0 + 0] * 0
    for dx in range(4):
        for dc in range(2):
            order.append(((c + dc) % 2) * 4 + (x - dx) % 4)
    info = jnp.stack([own_at, occupied[0], c, x, y, z, y * 0, y * 0] + order).astype(jnp.int32)
    pieces, place = weight_pieces(y, z, c, gate_w, up_w, down_w)

    positions = (4 * y + z) * SEQ_DEV + chosen
    half = HD // 2
    frequency = 10000.0 ** (-jnp.arange(half, dtype=F32) / half)
    angles = positions.astype(F32)[:, None] * frequency[None, :]
    cosine, sine = jnp.cos(angles), jnp.sin(angles)
    cosine = jnp.concatenate([cosine, cosine], axis=1)
    sine = jnp.concatenate([-sine, sine], axis=1)
    q, kv, picked = project(info, block, chosen[:, None], gain1[None, :], cosine, sine, wq, wk, wv)

    kvs = [kv] + [shift(kv, "z", d) for d in (1, 2, 3)]
    scale = sharpness * (LOG2E / math.sqrt(HD))
    parts = []
    for d in (1, 2, 3):
        asked = shift(q, "y", d)
        allow = jnp.broadcast_to(((y - d) % 4 > y).astype(jnp.int32), (4,))
        parts.append(shift(attend(False, allow, scale, asked, kvs), "y", 4 - d))
    allow = jnp.stack([z >= 0] + [(z - d) % 4 < z for d in (1, 2, 3)]).astype(jnp.int32)
    parts.append(attend(True, allow, scale, q, kvs))

    keep, send = mix(info, parts, wo)
    own, s1, s2, s3 = split(info, keep, shift(send, "c", 1, 2))
    got = [shift(s, "x", d) for d, s in ((1, s1), (2, s2), (3, s3))]
    attention, normed = middle(picked, own, got, gain2[None, :])

    offsets = [(dy, dx) for dy in range(4) for dx in range(4)]
    xs = [normed] + [shift2(normed, dy, dx) for dy, dx in offsets[1:]]
    outs = feed(place, xs, pieces)
    back = [outs[0]] + [shift2(o, -dy, -dx) for o, (dy, dx) in zip(outs[1:], offsets[1:])]

    mine = lax.dynamic_slice_in_dim(chosen, own_at, OWN, 0)
    hit = mine[:, None] == jnp.arange(SEQ_DEV, dtype=jnp.int32)[None, :]
    router = jax.nn.sigmoid(jnp.sum(jnp.where(hit, preference[None, :], 0.0), axis=1, keepdims=True))
    result = finish(picked, attention, router, back)
    rows = [result if dx == 0 and dc == 0 else shift_mp(result, dx, dc) for dx in range(4) for dc in range(2)]
    return put_back(info, chosen[None, :], block, rows)


def solution(mesh):
    grid = Mesh(mesh.devices.reshape(4, 4, 4, 2), ("y", "z", "x", "c"))
    ctx, mp = ("y", "z"), ("x", "c")
    return jax.shard_map(
        local,
        mesh=grid,
        in_specs=(P(ctx, None), P(ctx), P(ctx), P(ctx), P(), P(None, mp), P(None, mp), P(None, mp),
                  P(mp, None), P(mp), P(), P(ctx, mp), P(ctx, mp), P(ctx, mp)),
        out_specs=P(ctx, None),
        check_vma=False,
    )
```

time: 500 us -> 340 us (0.68)
  the two profiles are of different devices: /device:TPU:1 before, /device:TPU:39 now
where the time goes in v1:
time: 340 us; the launch traced here: 333 us
  starting transfers between devices  123 us (36%)
  waiting for transfers between devices  91.1 us (27%)
  local copies, waits for them, and re-layouts  59.6 us (18%)
  Pallas kernels  51.6 us (15%)
  other arithmetic  7.08 us (2%)
    ppermute x30, starting transfers between devices, shift2(): return lax.ppermute(value, ('y', 'x'), pairs)  58.6 us
    ppermute x30, waiting for transfers between devices, shift2(): return lax.ppermute(value, ('y', 'x'), pairs)  46.9 us
    unnamed x134, local copies, waits for them, and re-layouts  45.1 us
    ppermute x27, starting transfers between devices, shift(): lax.ppermute(value, axis, [(i, (i + step) % size) for i in range(size)])  41.6 us
    ppermute x27, waiting for transfers between devices, shift(): lax.ppermute(value, axis, [(i, (i + step) % size) for i in range(size)])  31.5 us
    pallas_call x1, Pallas kernels, feed(): pl.pallas_call(feed_body, out_shape=(jax.ShapeDtypeStruct((OWN, D), BF16)...  16.7 us
    pallas_call x4, Pallas kernels, attend(): pl.pallas_call(functools.partial(attend_body, diagonal), out_shape=jax.Sh...  16.4 us
    ppermute x7, starting transfers between devices, shift_mp(): return lax.ppermute(value, ('x', 'c'), pairs)  13.9 us
  transfers between devices with their start and end apart: 66, of which 25 were waited for; matrix products, arithmetic and copies ran while one was open for 6% of the time, Pallas kernels for 7%

profile of v1, /device:TPU:39, one launch (start us, length us, event | category | flops | bytes accessed | tf_op | source)
XLA Modules:
  0.0 333.3 jit_solution(193050875423035480)
XLA Ops:
  9.1 7.1 %project.1 = (bf16[256,512]{1,0:T(8,128)(2,1)S(1)}, bf16[272,512]{1,0:T(8,128)(2,1)S(1)}, bf16[32,2304]{1,0:T(8,128)(2,1)S(1)}) custom-call(s32[16]{0:T(128)S(1)} %stack.127.info, bf16[1024,2304]{1,0:T(8,128)(2,1)S(1)} %copy-done, s32[256,1]{1,0:T(8,128)S(1)} %copy.24.chosen, f32[1,2304]{1,0:T(1,128)S(1)} %broadcast_in_dim.41.gain, ...), custom_call_target="tpu_custom_call" | custom-call | tf_op jit(solution)/shard_map/project/pallas_call | solution.py:83
  41.6 4.3 %attend.6 = bf16[272,512]{1,0:T(8,128)(2,1)} custom-call(s32[4]{0:T(128)S(1)} %broadcast_in_dim.44.allow, f32[4]{0:T(128)S(1)} %broadcast_multiply_fusion.scale, bf16[256,512]{1,0:T(8,128)(2,1)S(1)} %collective-permute-done.7.q, bf16[272,512]{1,0:T(8,128)(2,1)S(1)} %get-tuple-element.34.kv0, bf16[272,512]{1,0:T(8,128)(2,1)S(1)} %collective-permute-done.1.kv1, ...), custom_call_target="tpu_custom_call" | custom-call | tf_op jit(solution)/shard_map/attend/pallas_call | solution.py:148
  47.5 4.3 %attend.5 = bf16[272,512]{1,0:T(8,128)(2,1)} custom-call(s32[4]{0:T(128)S(1)} %broadcast_in_dim.43.allow, f32[4]{0:T(128)S(1)} %broadcast_multiply_fusion.scale, bf16[256,512]{1,0:T(8,128)(2,1)S(1)} %collective-permute-done.5.q, bf16[272,512]{1,0:T(8,128)(2,1)S(1)} %get-tuple-element.34.kv0, bf16[272,512]{1,0:T(8,128)(2,1)S(1)} %collective-permute-done.1.kv1, ...), custom_call_target="tpu_custom_call" | custom-call | tf_op jit(solution)/shard_map/attend/pallas_call | solution.py:148
  53.3 4.3 %attend.4 = bf16[272,512]{1,0:T(8,128)(2,1)} custom-call(s32[4]{0:T(128)S(1)} %broadcast_in_dim.42.allow, f32[4]{0:T(128)S(1)} %broadcast_multiply_fusion.scale, bf16[256,512]{1,0:T(8,128)(2,1)S(1)} %collective-permute-done.q, bf16[272,512]{1,0:T(8,128)(2,1)S(1)} %get-tuple-element.34.kv0, bf16[272,512]{1,0:T(8,128)(2,1)S(1)} %collective-permute-done.1.kv1, ...), custom_call_target="tpu_custom_call" | custom-call | tf_op jit(solution)/shard_map/attend/pallas_call | solution.py:148
  60.1 7.3 %collective-permute-start.28 = (bf16[144,3456]{1,0:T(8,128)(2,1)}, bf16[144,3456]{1,0:T(8,128)(2,1)}, u32[]{:S(2)}, u32[]{:S(2)}) collective-permute-start(bf16[144,3456]{1,0:T(8,128)(2,1)} %get-tuple-element.60), channel_id=1, source_target_pairs={{0,0},{1,64},{32,32},{33,96},{64,1},{65,65},{96,33},{97,97},{2,2},... | collective-permute-start | bytes 2985992 | tf_op jit(solution)/shard_map/ppermute | solution.py:373
  69.6 3.6 %attend.7.p3 = bf16[272,512]{1,0:T(8,128)(2,1)S(1)} custom-call(s32[4]{0:T(128)S(1)} %add_convert_fusion.allow, f32[4]{0:T(128)S(1)} %broadcast_multiply_fusion.scale, bf16[256,512]{1,0:T(8,128)(2,1)S(1)} %copy-done.15, bf16[272,512]{1,0:T(8,128)(2,1)S(1)} %get-tuple-element.34.kv0, bf16[272,512]{1,0:T(8,128)(2,1)S(1)} %collective-permute-done.1.kv1, ...), custom_call_target="tpu_custom_call" | custom-call | tf_op jit(solution)/shard_map/attend/pallas_call | solution.py:148
  73.2 4.4 %mix.1 = (f32[128,2304]{1,0:T(8,128)S(1)}, bf16[128,2304]{1,0:T(8,128)(2,1)S(1)}) custom-call(s32[16]{0:T(128)S(1)} %stack.127.info, bf16[272,512]{1,0:T(8,128)(2,1)} %collective-permute-done.4.p0, bf16[272,512]{1,0:T(8,128)(2,1)} %collective-permute-done.6.p1, bf16[272,512]{1,0:T(8,128)(2,1)} %collective-permute-done.8.p2, bf16[272,512]{1,0:T(8,128)(2,1)S(1)} %attend.7.p3, ...), custom_call_target="tpu_custom_call" | custom-call | tf_op jit(solution)/shard_map/mix/pallas_call | solution.py:186
  77.6 7.8 %collective-permute-start.9 = (bf16[128,2304]{1,0:T(8,128)(2,1)S(1)}, bf16[128,2304]{1,0:T(8,128)(2,1)S(1)}, u32[]{:S(2)}, u32[]{:S(2)}) collective-permute-start(bf16[128,2304]{1,0:T(8,128)(2,1)S(1)} %get-tuple-element.36), channel_id=1, source_target_pairs={{0,1},{1,0},{2,3},{3,2},{4,5},{5,4},{6,7},{7,6},{8,9},{9,8},{10,11... | collective-permute-start | bytes 1769480 | tf_op jit(solution)/shard_map/ppermute | solution.py:346
  94.2 3.6 %collective-permute-done.12.r3 = bf16[32,2304]{1,0:T(8,128)(2,1)S(1)} collective-permute-done((bf16[32,2304]{1,0:T(8,128)(2,1)S(1)}, bf16[32,2304]{1,0:T(8,128)(2,1)S(1)}, u32[]{:S(2)}, u32[]{:S(2)}) %collective-permute-start.12) | collective-permute-done | bytes 147488 | tf_op jit(solution)/shard_map/ppermute | solution.py:346
  117.7 6.9 %collective-permute-done.20.refs_9_ = bf16[32,2304]{1,0:T(8,128)(2,1)S(1)} collective-permute-done((bf16[32,2304]{1,0:T(8,128)(2,1)S(1)}, bf16[32,2304]{1,0:T(8,128)(2,1)S(1)}, u32[]{:S(2)}, u32[]{:S(2)}) %collective-permute-start.20) | collective-permute-done | bytes 147488 | tf_op jit(solution)/shard_map/ppermute | solution.py:351
  127.4 7.1 %collective-permute-done.22.refs_11_ = bf16[32,2304]{1,0:T(8,128)(2,1)S(1)} collective-permute-done((bf16[32,2304]{1,0:T(8,128)(2,1)S(1)}, bf16[32,2304]{1,0:T(8,128)(2,1)S(1)}, u32[]{:S(2)}, u32[]{:S(2)}) %collective-permute-start.22) | collective-permute-done | bytes 147488 | tf_op jit(solution)/shard_map/ppermute | solution.py:351
  135.6 7.2 %collective-permute-done.23.refs_12_ = bf16[32,2304]{1,0:T(8,128)(2,1)S(1)} collective-permute-done((bf16[32,2304]{1,0:T(8,128)(2,1)S(1)}, bf16[32,2304]{1,0:T(8,128)(2,1)S(1)}, u32[]{:S(2)}, u32[]{:S(2)}) %collective-permute-start.23) | collective-permute-done | bytes 147488 | tf_op jit(solution)/shard_map/ppermute | solution.py:351
  143.5 5.4 %collective-permute-done.24.refs_13_ = bf16[32,2304]{1,0:T(8,128)(2,1)S(1)} collective-permute-done((bf16[32,2304]{1,0:T(8,128)(2,1)S(1)}, bf16[32,2304]{1,0:T(8,128)(2,1)S(1)}, u32[]{:S(2)}, u32[]{:S(2)}) %collective-permute-start.24) | collective-permute-done | bytes 147488 | tf_op jit(solution)/shard_map/ppermute | solution.py:351
  162.1 4.9 %collective-permute-start.27 = (bf16[32,2304]{1,0:T(8,128)(2,1)S(1)}, bf16[32,2304]{1,0:T(8,128)(2,1)S(1)}, u32[]{:S(2)}, u32[]{:S(2)}) collective-permute-start(bf16[32,2304]{1,0:T(8,128)(2,1)S(1)} %get-tuple-element.42.refs_1_), channel_id=1, source_target_pairs={{0,102},{2,96},{4,98},{6,100},{32,6},{34,0},{36,2},{38,4},{64,38},... | collective-permute-start | bytes 442376 | tf_op jit(solution)/shard_map/ppermute | solution.py:351
  170.0 11.5 %collective-permute-start.36 = (bf16[144,3456]{1,0:T(8,128)(2,1)}, bf16[144,3456]{1,0:T(8,128)(2,1)S(1)}, u32[]{:S(2)}, u32[]{:S(2)}) collective-permute-start(bf16[144,3456]{1,0:T(8,128)(2,1)} %collective-permute-done.28.refs_17_), channel_id=1, source_target_pairs={{0,1},{1,0},{2,3},{3,2},{4,5},{5,4},{6,7},{7,6},{8,9},{9,8},{10,11... | collective-permute-start | bytes 2985992 | tf_op jit(solution)/shard_map/ppermute | solution.py:346
  186.7 18.1 %collective-permute-done.34.refs_23_ = bf16[144,3456]{1,0:T(8,128)(2,1)} collective-permute-done((bf16[144,3456]{1,0:T(8,128)(2,1)S(1)}, bf16[144,3456]{1,0:T(8,128)(2,1)}, u32[]{:S(2)}, u32[]{:S(2)}) %collective-permute-start.34) | collective-permute-done | bytes 995360 | tf_op jit(solution)/shard_map/ppermute | solution.py:346
  229.8 16.7 %feed.1 = (bf16[32,2304]{1,0:T(8,128)(2,1)S(1)}, bf16[32,2304]{1,0:T(8,128)(2,1)S(1)}, bf16[32,2304]{1,0:T(8,128)(2,1)S(1)}, bf16[32,2304]{1,0:T(8,128)(2,1)S(1)...) custom-call(s32[16]{0:T(128)S(1)} %stack.149.refs_0_, ...), custom_call_target="tpu_custom_call" | custom-call | tf_op jit(solution)/shard_map/feed/pallas_call | solution.py:278
  260.7 3.9 %collective-permute-start.50 = (bf16[32,2304]{1,0:T(8,128)(2,1)}, bf16[32,2304]{1,0:T(8,128)(2,1)S(1)}, u32[]{:S(2)}, u32[]{:S(2)}) collective-permute-start(bf16[32,2304]{1,0:T(8,128)(2,1)} %get-tuple-element.50), channel_id=1, source_target_pairs={{0,98},{2,100},{4,102},{6,96},{32,2},{34,4},{36,6},{38,0},{64,34},... | collective-permute-start | bytes 442376 | tf_op jit(solution)/shard_map/ppermute | solution.py:351
  272.9 10.3 %collective-permute-start.55 = (bf16[32,2304]{1,0:T(8,128)(2,1)}, bf16[32,2304]{1,0:T(8,128)(2,1)S(1)}, u32[]{:S(2)}, u32[]{:S(2)}) collective-permute-start(bf16[32,2304]{1,0:T(8,128)(2,1)} %copy-done.54), channel_id=1, source_target_pairs={{0,32},{2,34},{4,36},{6,38},{32,64},{34,66},{36,68},{38,70},{64,96... | collective-permute-start | bytes 442376 | tf_op jit(solution)/shard_map/ppermute | solution.py:351
  285.7 9.1 %collective-permute-done.56.refs_13_ = bf16[32,2304]{1,0:T(8,128)(2,1)S(1)} collective-permute-done((bf16[32,2304]{1,0:T(8,128)(2,1)}, bf16[32,2304]{1,0:T(8,128)(2,1)S(1)}, u32[]{:S(2)}, u32[]{:S(2)}) %collective-permute-start.56) | collective-permute-done | bytes 147488 | tf_op jit(solution)/shard_map/ppermute | solution.py:351
  298.5 4.5 %collective-permute-start.59 = (bf16[32,2304]{1,0:T(8,128)(2,1)S(1)}, bf16[32,2304]{1,0:T(8,128)(2,1)S(1)}, u32[]{:S(2)}, u32[]{:S(2)}) collective-permute-start(bf16[32,2304]{1,0:T(8,128)(2,1)S(1)} %finish.1.refs_0_), channel_id=1, source_target_pairs={{0,1},{1,0},{2,3},{3,2},{4,5},{5,4},{6,7},{7,6},{8,9},{9,8},{10,11... | collective-permute-start | bytes 442376 | tf_op jit(solution)/shard_map/ppermute | solution.py:356
  304.7 3.6 %collective-permute-start.61 = (bf16[32,2304]{1,0:T(8,128)(2,1)S(1)}, bf16[32,2304]{1,0:T(8,128)(2,1)S(1)}, u32[]{:S(2)}, u32[]{:S(2)}) collective-permute-start(bf16[32,2304]{1,0:T(8,128)(2,1)S(1)} %finish.1.refs_0_), channel_id=1, source_target_pairs={{0,3},{1,2},{2,5},{3,4},{4,7},{5,6},{6,1},{7,0},{8,11},{9,10},{10,... | collective-permute-start | bytes 442376 | tf_op jit(solution)/shard_map/ppermute | solution.py:356
  315.2 4.1 %collective-permute-done.63.refs_5_ = bf16[32,2304]{1,0:T(8,128)(2,1)S(1)} collective-permute-done((bf16[32,2304]{1,0:T(8,128)(2,1)S(1)}, bf16[32,2304]{1,0:T(8,128)(2,1)S(1)}, u32[]{:S(2)}, u32[]{:S(2)}) %collective-permute-start.63) | collective-permute-done | bytes 147488 | tf_op jit(solution)/shard_map/ppermute | solution.py:356
  327.5 5.6 %put_back.1 = bf16[1024,2304]{1,0:T(8,128)(2,1)} custom-call(s32[16]{0:T(128)S(1)} %stack.127.info, s32[1,256]{1,0:T(1,128)S(1)} %bitcast.38, bf16[1024,2304]{1,0:T(8,128)(2,1)S(1)} %copy-done.1, bf16[32,2304]{1,0:T(8,128)(2,1)S(1)} %finish.1.refs_0_, bf16[32,2304]{1,0:T(8,128)(2,1)S(1)} %collective-permute-done.59.refs_1_, ...), custom_call_target="tpu_custom_call" | custom-call | tf_op jit(solution)/shard_map/put_back/pallas_call | solution.py:331
  (286 shorter events, 166.3 us)
Async XLA Ops:
  16.2 25.3 %collective-permute-start.1 = (bf16[272,512]{1,0:T(8,128)(2,1)S(1)}, bf16[272,512]{1,0:T(8,128)(2,1)S(1)}, u32[]{:S(2)}, u32[]{:S(2)}) collective-permute-start(bf16[272,512]{1,0:T(8,128)(2,1)S(1)} %get-tuple-element.34.kv0), channel_id=1, source_target_pairs={{0,8},{8,16},{16,24},{24,0},{1,9},{9,17},{17,25},{25,1},{2,10},{10... | collective-permute-start | bytes 835592 | tf_op jit(solution)/shard_map/ppermute | solution.py:346
  17.9 23.6 %collective-permute-start.2 = (bf16[272,512]{1,0:T(8,128)(2,1)S(1)}, bf16[272,512]{1,0:T(8,128)(2,1)S(1)}, u32[]{:S(2)}, u32[]{:S(2)}) collective-permute-start(bf16[272,512]{1,0:T(8,128)(2,1)S(1)} %get-tuple-element.34.kv0), channel_id=1, source_target_pairs={{0,16},{8,24},{16,0},{24,8},{1,17},{9,25},{17,1},{25,9},{2,18},{10... | collective-permute-start | bytes 835592 | tf_op jit(solution)/shard_map/ppermute | solution.py:346
  19.1 22.5 %collective-permute-start.3 = (bf16[272,512]{1,0:T(8,128)(2,1)S(1)}, bf16[272,512]{1,0:T(8,128)(2,1)S(1)}, u32[]{:S(2)}, u32[]{:S(2)}) collective-permute-start(bf16[272,512]{1,0:T(8,128)(2,1)S(1)} %get-tuple-element.34.kv0), channel_id=1, source_target_pairs={{0,24},{8,0},{16,8},{24,16},{1,25},{9,1},{17,9},{25,17},{2,26},{10... | collective-permute-start | bytes 835592 | tf_op jit(solution)/shard_map/ppermute | solution.py:346
  23.8 23.7 %collective-permute-start.5 = (bf16[256,512]{1,0:T(8,128)(2,1)S(1)}, bf16[256,512]{1,0:T(8,128)(2,1)S(1)}, u32[]{:S(2)}, u32[]{:S(2)}) collective-permute-start(bf16[256,512]{1,0:T(8,128)(2,1)S(1)} %get-tuple-element.33.q), channel_id=1, source_target_pairs={{0,64},{32,96},{64,0},{96,32},{1,65},{33,97},{65,1},{97,33},{2,66}... | collective-permute-start | bytes 786440 | tf_op jit(solution)/shard_map/ppermute | solution.py:346
  32.6 20.7 %collective-permute-start = (bf16[256,512]{1,0:T(8,128)(2,1)S(1)}, bf16[256,512]{1,0:T(8,128)(2,1)S(1)}, u32[]{:S(2)}, u32[]{:S(2)}) collective-permute-start(bf16[256,512]{1,0:T(8,128)(2,1)S(1)} %get-tuple-element.33.q), channel_id=1, source_target_pairs={{0,32},{32,64},{64,96},{96,0},{1,33},{33,65},{65,97},{97,1},{2,34}... | collective-permute-start | bytes 786440 | tf_op jit(solution)/shard_map/ppermute | solution.py:346
  45.8 27.3 %collective-permute-start.8 = (bf16[272,512]{1,0:T(8,128)(2,1)}, bf16[272,512]{1,0:T(8,128)(2,1)}, u32[]{:S(2)}, u32[]{:S(2)}) collective-permute-start(bf16[272,512]{1,0:T(8,128)(2,1)} %attend.6), channel_id=1, source_target_pairs={{0,32},{32,64},{64,96},{96,0},{1,33},{33,65},{65,97},{97,1},{2,34}... | collective-permute-start | bytes 835592 | tf_op jit(solution)/shard_map/ppermute | solution.py:346
  51.7 21.4 %collective-permute-start.6 = (bf16[272,512]{1,0:T(8,128)(2,1)}, bf16[272,512]{1,0:T(8,128)(2,1)}, u32[]{:S(2)}, u32[]{:S(2)}) collective-permute-start(bf16[272,512]{1,0:T(8,128)(2,1)} %attend.5), channel_id=1, source_target_pairs={{0,64},{32,96},{64,0},{96,32},{1,65},{33,97},{65,1},{97,33},{2,66}... | collective-permute-start | bytes 835592 | tf_op jit(solution)/shard_map/ppermute | solution.py:346
  57.6 15.6 %collective-permute-start.4 = (bf16[272,512]{1,0:T(8,128)(2,1)}, bf16[272,512]{1,0:T(8,128)(2,1)}, u32[]{:S(2)}, u32[]{:S(2)}) collective-permute-start(bf16[272,512]{1,0:T(8,128)(2,1)} %attend.4), channel_id=1, source_target_pairs={{0,96},{32,0},{64,32},{96,64},{1,97},{33,1},{65,33},{97,65},{2,98}... | collective-permute-start | bytes 835592 | tf_op jit(solution)/shard_map/ppermute | solution.py:346
  60.1 40.2 %collective-permute-start.28 = (bf16[144,3456]{1,0:T(8,128)(2,1)}, bf16[144,3456]{1,0:T(8,128)(2,1)}, u32[]{:S(2)}, u32[]{:S(2)}) collective-permute-start(bf16[144,3456]{1,0:T(8,128)(2,1)} %get-tuple-element.60), channel_id=1, source_target_pairs={{0,0},{1,64},{32,32},{33,96},{64,1},{65,65},{96,33},{97,97},{2,2},... | collective-permute-start | bytes 2985992 | tf_op jit(solution)/shard_map/ppermute | solution.py:373
  67.5 34.5 %collective-permute-start.29 = (bf16[144,3456]{1,0:T(8,128)(2,1)}, bf16[144,3456]{1,0:T(8,128)(2,1)}, u32[]{:S(2)}, u32[]{:S(2)}) collective-permute-start(bf16[144,3456]{1,0:T(8,128)(2,1)} %get-tuple-element.59), channel_id=1, source_target_pairs={{0,32},{1,96},{32,0},{33,64},{64,33},{65,97},{96,1},{97,65},{2,34}... | collective-permute-start | bytes 2985992 | tf_op jit(solution)/shard_map/ppermute | solution.py:373
  109.6 15.0 %collective-permute-start.20 = (bf16[32,2304]{1,0:T(8,128)(2,1)S(1)}, bf16[32,2304]{1,0:T(8,128)(2,1)S(1)}, u32[]{:S(2)}, u32[]{:S(2)}) collective-permute-start(bf16[32,2304]{1,0:T(8,128)(2,1)S(1)} %get-tuple-element.42.refs_1_), channel_id=1, source_target_pairs={{0,64},{2,66},{4,68},{6,70},{32,96},{34,98},{36,100},{38,102},{64,... | collective-permute-start | bytes 442376 | tf_op jit(solution)/shard_map/ppermute | solution.py:351
  114.5 67.0 %collective-permute-start.30 = (bf16[144,3456]{1,0:T(8,128)(2,1)}, bf16[144,3456]{1,0:T(8,128)(2,1)S(1)}, u32[]{:S(2)}, u32[]{:S(2)}) collective-permute-start(bf16[144,3456]{1,0:T(8,128)(2,1)} %collective-permute-done.28.refs_17_), channel_id=1, source_target_pairs={{0,8},{8,16},{16,24},{24,0},{1,9},{9,17},{17,25},{25,1},{2,10},{10... | collective-permute-start | bytes 2985992 | tf_op jit(solution)/shard_map/ppermute | solution.py:346
  115.2 66.3 %collective-permute-start.33 = (bf16[144,3456]{1,0:T(8,128)(2,1)}, bf16[144,3456]{1,0:T(8,128)(2,1)S(1)}, u32[]{:S(2)}, u32[]{:S(2)}) collective-permute-start(bf16[144,3456]{1,0:T(8,128)(2,1)} %collective-permute-done.29.refs_18_), channel_id=1, source_target_pairs={{0,24},{8,0},{16,8},{24,16},{1,25},{9,1},{17,9},{25,17},{2,26},{10... | collective-permute-start | bytes 2985992 | tf_op jit(solution)/shard_map/ppermute | solution.py:346
  117.7 64.0 %collective-permute-start.31 = (bf16[144,3456]{1,0:T(8,128)(2,1)}, bf16[144,3456]{1,0:T(8,128)(2,1)S(1)}, u32[]{:S(2)}, u32[]{:S(2)}) collective-permute-start(bf16[144,3456]{1,0:T(8,128)(2,1)} %collective-permute-done.29.refs_18_), channel_id=1, source_target_pairs={{0,8},{8,16},{16,24},{24,0},{1,9},{9,17},{17,25},{25,1},{2,10},{10... | collective-permute-start | bytes 2985992 | tf_op jit(solution)/shard_map/ppermute | solution.py:346
  125.3 57.8 %collective-permute-start.32 = (bf16[144,3456]{1,0:T(8,128)(2,1)}, bf16[144,3456]{1,0:T(8,128)(2,1)}, u32[]{:S(2)}, u32[]{:S(2)}) collective-permute-start(bf16[144,3456]{1,0:T(8,128)(2,1)} %collective-permute-done.28.refs_17_), channel_id=1, source_target_pairs={{0,24},{8,0},{16,8},{24,16},{1,25},{9,1},{17,9},{25,17},{2,26},{10... | collective-permute-start | bytes 2985992 | tf_op jit(solution)/shard_map/ppermute | solution.py:346
  181.6 23.3 %collective-permute-start.34 = (bf16[144,3456]{1,0:T(8,128)(2,1)S(1)}, bf16[144,3456]{1,0:T(8,128)(2,1)}, u32[]{:S(2)}, u32[]{:S(2)}) collective-permute-start(bf16[144,3456]{1,0:T(8,128)(2,1)S(1)} %collective-permute-done.30.refs_19_), channel_id=1, source_target_pairs={{0,8},{8,16},{16,24},{24,0},{1,9},{9,17},{17,25},{25,1},{2,10},{10... | collective-permute-start | bytes 2985992 | tf_op jit(solution)/shard_map/ppermute | solution.py:346
  181.6 24.5 %collective-permute-start.35 = (bf16[144,3456]{1,0:T(8,128)(2,1)S(1)}, bf16[144,3456]{1,0:T(8,128)(2,1)}, u32[]{:S(2)}, u32[]{:S(2)}) collective-permute-start(bf16[144,3456]{1,0:T(8,128)(2,1)S(1)} %collective-permute-done.33.refs_22_), channel_id=1, source_target_pairs={{0,24},{8,0},{16,8},{24,16},{1,25},{9,1},{17,9},{25,17},{2,26},{10... | collective-permute-start | bytes 2985992 | tf_op jit(solution)/shard_map/ppermute | solution.py:346
  183.1 23.4 %collective-permute-start.38 = (bf16[144,3456]{1,0:T(8,128)(2,1)S(1)}, bf16[144,3456]{1,0:T(8,128)(2,1)S(1)}, u32[]{:S(2)}, u32[]{:S(2)}) collective-permute-start(bf16[144,3456]{1,0:T(8,128)(2,1)S(1)} %collective-permute-done.30.refs_19_), channel_id=1, source_target_pairs={{0,1},{1,0},{2,3},{3,2},{4,5},{5,4},{6,7},{7,6},{8,9},{9,8},{10,11... | collective-permute-start | bytes 2985992 | tf_op jit(solution)/shard_map/ppermute | solution.py:346
  185.0 23.7 %collective-permute-start.41 = (bf16[144,3456]{1,0:T(8,128)(2,1)S(1)}, bf16[144,3456]{1,0:T(8,128)(2,1)}, u32[]{:S(2)}, u32[]{:S(2)}) collective-permute-start(bf16[144,3456]{1,0:T(8,128)(2,1)S(1)} %collective-permute-done.33.refs_22_), channel_id=1, source_target_pairs={{0,1},{1,0},{2,3},{3,2},{4,5},{5,4},{6,7},{7,6},{8,9},{9,8},{10,11... | collective-permute-start | bytes 2985992 | tf_op jit(solution)/shard_map/ppermute | solution.py:346
  186.4 21.4 %collective-permute-start.39 = (bf16[144,3456]{1,0:T(8,128)(2,1)S(1)}, bf16[144,3456]{1,0:T(8,128)(2,1)}, u32[]{:S(2)}, u32[]{:S(2)}) collective-permute-start(bf16[144,3456]{1,0:T(8,128)(2,1)S(1)} %collective-permute-done.31.refs_20_), channel_id=1, source_target_pairs={{0,1},{1,0},{2,3},{3,2},{4,5},{5,4},{6,7},{7,6},{8,9},{9,8},{10,11... | collective-permute-start | bytes 2985992 | tf_op jit(solution)/shard_map/ppermute | solution.py:346
  264.6 18.7 %collective-permute-start.51 = (bf16[32,2304]{1,0:T(8,128)(2,1)}, bf16[32,2304]{1,0:T(8,128)(2,1)S(1)}, u32[]{:S(2)}, u32[]{:S(2)}) collective-permute-start(bf16[32,2304]{1,0:T(8,128)(2,1)} %get-tuple-element.51), channel_id=1, source_target_pairs={{0,64},{2,66},{4,68},{6,70},{32,96},{34,98},{36,100},{38,102},{64,... | collective-permute-start | bytes 442376 | tf_op jit(solution)/shard_map/ppermute | solution.py:351
  265.4 17.8 %collective-permute-start.52 = (bf16[32,2304]{1,0:T(8,128)(2,1)}, bf16[32,2304]{1,0:T(8,128)(2,1)S(1)}, u32[]{:S(2)}, u32[]{:S(2)}) collective-permute-start(bf16[32,2304]{1,0:T(8,128)(2,1)} %get-tuple-element.52), channel_id=1, source_target_pairs={{0,70},{2,64},{4,66},{6,68},{32,102},{34,96},{36,98},{38,100},{64,... | collective-permute-start | bytes 442376 | tf_op jit(solution)/shard_map/ppermute | solution.py:351
  268.6 15.8 %collective-permute-start.53 = (bf16[32,2304]{1,0:T(8,128)(2,1)}, bf16[32,2304]{1,0:T(8,128)(2,1)S(1)}, u32[]{:S(2)}, u32[]{:S(2)}) collective-permute-start(bf16[32,2304]{1,0:T(8,128)(2,1)} %get-tuple-element.53), channel_id=1, source_target_pairs={{0,68},{2,70},{4,64},{6,66},{32,100},{34,102},{36,96},{38,98},{64,... | collective-permute-start | bytes 442376 | tf_op jit(solution)/shard_map/ppermute | solution.py:351
  270.3 14.9 %collective-permute-start.54 = (bf16[32,2304]{1,0:T(8,128)(2,1)}, bf16[32,2304]{1,0:T(8,128)(2,1)S(1)}, u32[]{:S(2)}, u32[]{:S(2)}) collective-permute-start(bf16[32,2304]{1,0:T(8,128)(2,1)} %copy-done.55), channel_id=1, source_target_pairs={{0,66},{2,68},{4,70},{6,64},{32,98},{34,100},{36,102},{38,96},{64,... | collective-permute-start | bytes 442376 | tf_op jit(solution)/shard_map/ppermute | solution.py:351
  (109 other events, 693.5 us)

commit v2 on v1

v2 whole, which is shorter than its diff:
```python
import functools
import math

import jax
import jax.numpy as jnp
from jax import lax
from jax.experimental import pallas as pl
from jax.experimental.pallas import tpu as pltpu
from jax.sharding import Mesh, PartitionSpec as P

D = 2304
CAP = 256
SEQ_DEV = 1024
HD = 128
FF_DEV = 1152
ROWS = 144
STEP = 512
OWN = 32
EPS = 1e-06
NEG = -1e30
LOG2E = 1.4426950408889634
MB = 1024 * 1024
F32 = jnp.float32
BF16 = jnp.bfloat16


def vmem_spec():
    return pl.BlockSpec(memory_space=pltpu.VMEM)


def smem_spec():
    return pl.BlockSpec(memory_space=pltpu.SMEM)


def hbm_spec():
    return pl.BlockSpec(memory_space=pltpu.HBM)


def params(mib):
    return pltpu.CompilerParams(vmem_limit_bytes=mib * MB)


def begin_body(info, block_hbm, chosen, gain, frequency, wq_hbm, wk_hbm, wv_hbm,
               q_out, kv_out, own_out, block, picked, normed, wq, wk, wv, sems):
    tiles = D // 256
    loads = [pltpu.make_async_copy(block_hbm.at[:, i * 256:(i + 1) * 256],
                                   block.at[:, i * 256:(i + 1) * 256], sems.at[i])
             for i in range(tiles)]
    weights = [pltpu.make_async_copy(src, dst, sems.at[9 + i])
               for i, (src, dst) in enumerate(((wk_hbm, wk), (wv_hbm, wv), (wq_hbm, wq)))]
    for copy in loads + weights:
        copy.start()
    wide = jnp.broadcast_to(chosen[...].astype(F32), (128, CAP))
    column = jnp.transpose(wide)[:, 0:1].astype(jnp.int32)
    lanes = lax.broadcasted_iota(jnp.int32, (CAP, SEQ_DEV), 1)
    one_hot = jnp.where(lanes == column, 1.0, 0.0).astype(BF16)
    total = jnp.zeros((CAP, 256), F32)
    for i in range(tiles):
        cols = slice(i * 256, (i + 1) * 256)
        loads[i].wait()
        part = jnp.dot(one_hot, block[:, cols], preferred_element_type=F32)
        picked[:, cols] = part.astype(BF16)
        total = total + part * part
    angles = (column + info[6]).astype(F32) * frequency[...]
    cosine, sine = jnp.cos(angles), jnp.sin(angles)
    sine = jnp.where(lax.broadcasted_iota(jnp.int32, (CAP, HD), 1) < HD // 2, -sine, sine)
    inv = lax.rsqrt(jnp.sum(total, axis=1, keepdims=True) / D + EPS)
    for i in range(tiles):
        cols = slice(i * 256, (i + 1) * 256)
        normed[:, cols] = (picked[:, cols].astype(F32) * inv * gain[:, cols]).astype(BF16)
    own_out[...] = picked[pl.ds(pl.multiple_of(info[0], OWN), OWN), :]

    def turn(values):
        return values * cosine + pltpu.roll(values, HD // 2, 1) * sine

    weights[0].wait()
    keys = jnp.dot(normed[...], wk[...], preferred_element_type=F32)
    for h in range(2):
        kv_out[0:CAP, h * HD:(h + 1) * HD] = turn(keys[:, h * HD:(h + 1) * HD]).astype(BF16)
    weights[1].wait()
    kv_out[0:CAP, 256:512] = jnp.dot(normed[...], wv[...], preferred_element_type=F32).astype(BF16)
    kv_out[CAP:CAP + 16, :] = jnp.full((16, 512), info[1].astype(F32), F32).astype(BF16)
    weights[2].wait()
    for j in range(2):
        part = jnp.dot(normed[...], wq[:, j * 256:(j + 1) * 256], preferred_element_type=F32)
        for h in range(2):
            at = j * 256 + h * HD
            q_out[:, at:at + HD] = turn(part[:, h * HD:(h + 1) * HD]).astype(BF16)


def begin(info, block, chosen, gain, frequency, wq, wk, wv):
    return pl.pallas_call(
        begin_body,
        out_shape=(jax.ShapeDtypeStruct((CAP, 512), BF16), jax.ShapeDtypeStruct((CAP + 16, 512), BF16),
                   jax.ShapeDtypeStruct((OWN, D), BF16)),
        in_specs=[smem_spec(), hbm_spec()] + [vmem_spec()] * 3 + [hbm_spec()] * 3,
        out_specs=(vmem_spec(),) * 3,
        scratch_shapes=[pltpu.VMEM((SEQ_DEV, D), BF16), pltpu.VMEM((CAP, D), BF16), pltpu.VMEM((CAP, D), BF16),
                        pltpu.VMEM((D, 512), BF16), pltpu.VMEM((D, 256), BF16), pltpu.VMEM((D, 256), BF16),
                        pltpu.SemaphoreType.DMA((12,))],
        compiler_params=params(60),
        name="begin",
    )(info, block, chosen, gain, frequency, wq, wk, wv)


def pack_body(info, gate, up, down, out0, out1, packed, sems):
    loads, stores = [], []
    for s, out in enumerate((out0, out1)):
        cols = pl.ds(pl.multiple_of(lax.rem(info[4] + s, 2) * FF_DEV, FF_DEV), FF_DEV)
        for k, weight in enumerate((gate, up, down)):
            rows = slice(k * ROWS, (k + 1) * ROWS)
            at = 3 * s + k
            loads.append(pltpu.make_async_copy(weight.at[:, cols], packed.at[s, rows, :], sems.at[at]))
            stores.append(pltpu.make_async_copy(packed.at[s, rows, :], out.at[rows, :], sems.at[6 + at]))
    for load in loads:
        load.start()
    for load, store in zip(loads, stores):
        load.wait()
        store.start()
    for store in stores:
        store.wait()


def pack(info, gate, up, down):
    return pl.pallas_call(
        pack_body,
        out_shape=(jax.ShapeDtypeStruct((3 * ROWS, FF_DEV), BF16),) * 2,
        in_specs=[smem_spec()] + [hbm_spec()] * 3,
        out_specs=(hbm_spec(),) * 2,
        scratch_shapes=[pltpu.VMEM((2, 3 * ROWS, FF_DEV), BF16), pltpu.SemaphoreType.DMA((12,))],
        compiler_params=params(60),
        name="pack",
    )(info, gate, up, down)


def attend_body(diagonal, at, scale, q, kv0, kv1, kv2, kv3, out, stats, turned):
    lane = lax.broadcasted_iota(jnp.int32, (1, CAP), 1).astype(F32)
    bias = []
    kvs = (kv0, kv1, kv2, kv3)
    for j, kv in enumerate(kvs):
        count = kv[CAP:CAP + 16, 0:CAP].astype(F32)[0:1, :]
        live = (lane < count) & (at[j] >= 0)
        bias.append(jnp.where(live, 0.0, NEG))
        for g in range(2):
            turned[g * HD:(g + 1) * HD, j * CAP:(j + 1) * CAP] = jnp.transpose(kv[0:CAP, g * HD:(g + 1) * HD])
    past = lax.broadcasted_iota(jnp.int32, (CAP, CAP), 1) - lax.broadcasted_iota(jnp.int32, (CAP, CAP), 0)
    for head in range(4):
        g = head // 2
        cols = slice(head * HD, (head + 1) * HD)
        query = q[:, cols]
        scores = []
        for j in range(4):
            part = jnp.dot(query, turned[g * HD:(g + 1) * HD, j * CAP:(j + 1) * CAP],
                           preferred_element_type=F32)
            part = part * scale[head] + bias[j]
            if diagonal:
                part = jnp.where(past <= at[j], part, NEG)
            scores.append(part)
        top = jnp.max(functools.reduce(jnp.maximum, scores), axis=1, keepdims=True)
        weights = [jnp.exp2(part - top) for part in scores]
        total = jnp.sum(functools.reduce(jnp.add, weights), axis=1, keepdims=True)
        mixed = jnp.zeros((CAP, HD), F32)
        for j, kv in enumerate(kvs):
            mixed = mixed + jnp.dot(weights[j].astype(BF16), kv[0:CAP, 256 + g * HD:256 + (g + 1) * HD],
                                    preferred_element_type=F32)
        out[0:CAP, cols] = (mixed * (1.0 / total)).astype(BF16)
        log_sum = top + jnp.log2(total)
        first = log_sum.astype(BF16).astype(F32)
        second = (log_sum - first).astype(BF16).astype(F32)
        stats[:, head:head + 1] = first
        stats[:, 4 + head:5 + head] = second
        stats[:, 8 + head:9 + head] = log_sum - first - second
    lanes = lax.broadcasted_iota(jnp.int32, (CAP, 128), 1)
    clean = jnp.where(lanes < 12, stats[...], 0.0)
    out[CAP:CAP + 16, 0:CAP] = jnp.transpose(clean)[0:16, :].astype(BF16)
    out[CAP:CAP + 16, CAP:512] = jnp.zeros((16, 512 - CAP), BF16)


def attend(diagonal, at, scale, q, kvs):
    return pl.pallas_call(
        functools.partial(attend_body, diagonal),
        out_shape=jax.ShapeDtypeStruct((CAP + 16, 512), BF16),
        in_specs=[smem_spec()] * 2 + [vmem_spec()] * 5,
        out_specs=vmem_spec(),
        scratch_shapes=[pltpu.VMEM((CAP, 128), F32), pltpu.VMEM((256, 1024), BF16)],
        compiler_params=params(12),
        name="attend",
    )(at, scale, q, *kvs)


def mix_body(info, p0, p1, p2, p3, wo, keep, send, mixed):
    parts = (p0, p1, p2, p3)
    logs = []
    for part in parts:
        rows = part[CAP:CAP + 16, 0:CAP].astype(F32)
        rows = jnp.concatenate([rows, jnp.zeros((112, CAP), F32)], axis=0)
        logs.append(jnp.transpose(rows))
    for head in range(4):
        cols = slice(head * HD, (head + 1) * HD)
        each = [log[:, head:head + 1] + log[:, 4 + head:5 + head] + log[:, 8 + head:9 + head] for log in logs]
        top = functools.reduce(jnp.maximum, each)
        weights = [jnp.exp2(one - top) for one in each]
        total = functools.reduce(jnp.add, weights)
        value = functools.reduce(jnp.add, [w * part[0:CAP, cols].astype(F32) for w, part in zip(weights, parts)])
        mixed[:, cols] = (value / total).astype(BF16)
    core = info[2]
    mine = mixed[pl.ds(pl.multiple_of(core * 128, 128), 128), :]
    other = mixed[pl.ds(pl.multiple_of((1 - core) * 128, 128), 128), :]

    @pl.loop(0, D // 256)
    def _(i):
        cols = pl.ds(pl.multiple_of(i * 256, 256), 256)
        send[:, cols] = jnp.dot(other, wo[:, cols], preferred_element_type=F32).astype(BF16)
        keep[:, cols] = jnp.dot(mine, wo[:, cols], preferred_element_type=F32)


def mix(info, parts, wo):
    return pl.pallas_call(
        mix_body,
        out_shape=(jax.ShapeDtypeStruct((128, D), F32), jax.ShapeDtypeStruct((128, D), BF16)),
        in_specs=[smem_spec()] + [vmem_spec()] * 5,
        out_specs=(vmem_spec(),) * 2,
        scratch_shapes=[pltpu.VMEM((CAP, 512), BF16)],
        compiler_params=params(12),
        name="mix",
    )(info, *parts, wo)


def split_body(info, keep, got, own, s1, s2, s3):
    x = info[3]
    for d, ref in enumerate((own, s1, s2, s3)):
        rows = pl.ds(pl.multiple_of(lax.rem(x + d, 4) * OWN, OWN), OWN)
        ref[...] = (keep[rows, :] + got[rows, :].astype(F32)).astype(ref.dtype)


def split(info, keep, got):
    piece = jax.ShapeDtypeStruct((OWN, D), BF16)
    return pl.pallas_call(
        split_body,
        out_shape=(jax.ShapeDtypeStruct((OWN, D), F32), piece, piece, piece),
        in_specs=[smem_spec()] + [vmem_spec()] * 2,
        out_specs=(vmem_spec(),) * 4,
        compiler_params=params(12),
        name="split",
    )(info, keep, got)


def middle_body(picked, own, r1, r2, r3, gain, attention, normed):
    total = own[...] + r1[...].astype(F32) + r2[...].astype(F32) + r3[...].astype(F32)
    attention[...] = total
    mid = (picked[...].astype(F32) + total).astype(BF16).astype(F32)
    inv = lax.rsqrt(jnp.mean(mid * mid, axis=1, keepdims=True) + EPS)
    normed[...] = (mid * inv * gain[...]).astype(BF16)


def middle(picked, own, got, gain):
    return pl.pallas_call(
        middle_body,
        out_shape=(jax.ShapeDtypeStruct((OWN, D), F32), jax.ShapeDtypeStruct((OWN, D), BF16)),
        in_specs=[vmem_spec()] * 6,
        out_specs=(vmem_spec(),) * 2,
        compiler_params=params(12),
        name="middle",
    )(picked, own, *got, gain)


def feed_body(*refs):
    place = refs[0]
    xs = refs[1:5]
    pieces = refs[5:13]
    outs = refs[13:17]
    tokens, gate, up, down, hidden, sems = refs[17:]
    copies = [[], [], []]
    for e, x in enumerate(xs):
        copies[0].append(pltpu.make_async_copy(x, tokens.at[e * 128:(e + 1) * 128, :], sems.at[e]))
    for k, weight in enumerate((gate, up, down)):
        for i in range(16):
            rows = pl.ds(pl.multiple_of(place[i] * ROWS, 16), ROWS)
            at = (3 * (i % 2) + k) * ROWS
            copies[k].append(pltpu.make_async_copy(pieces[i // 2].at[at:at + ROWS, :], weight.at[rows, :],
                                                   sems.at[4 + 16 * k + i]))
    for copy in copies[0] + copies[1] + copies[2]:
        copy.start()
    for copy in copies[0]:
        copy.wait()
    chunks = [slice(j * 256, min((j + 1) * 256, FF_DEV)) for j in range(5)]
    for j, cols in enumerate(chunks):
        one = jnp.dot(tokens[...], gate[:, cols], preferred_element_type=F32)
        if j == 0:
            for copy in copies[1]:
                copy.wait()
        two = jnp.dot(tokens[...], up[:, cols], preferred_element_type=F32)
        hidden[:, cols] = (one / (1.0 + jnp.exp(-one)) * two).astype(BF16)
    for copy in copies[2]:
        copy.wait()
    for n in range(D // 256):
        rows = slice(n * 256, (n + 1) * 256)
        part = lax.dot_general(hidden[...], down[rows, :], (((1,), (1,)), ((), ())),
                               preferred_element_type=F32).astype(BF16)
        for e, out in enumerate(outs):
            out[:, rows] = part[e * 128:(e + 1) * 128, :]


def feed(place, xs, pieces):
    return pl.pallas_call(
        feed_body,
        out_shape=(jax.ShapeDtypeStruct((4 * OWN, D), BF16),) * 4,
        in_specs=[smem_spec()] + [hbm_spec()] * 12,
        out_specs=(vmem_spec(),) * 4,
        scratch_shapes=[pltpu.VMEM((512, D), BF16), pltpu.VMEM((D, FF_DEV), BF16), pltpu.VMEM((D, FF_DEV), BF16),
                        pltpu.VMEM((D, FF_DEV), BF16), pltpu.VMEM((512, FF_DEV), BF16),
                        pltpu.SemaphoreType.DMA((52,))],
        compiler_params=params(60),
        name="feed",
    )(place, *xs, *pieces)


def fold_body(p0, p1, p2, p3, own, s1, s2, s3):
    for d, out in enumerate((own, s1, s2, s3)):
        rows = slice(d * OWN, (d + 1) * OWN)
        total = p0[rows, :].astype(F32) + p1[rows, :].astype(F32)
        out[...] = (total + p2[rows, :].astype(F32) + p3[rows, :].astype(F32)).astype(out.dtype)


def fold(parts):
    piece = jax.ShapeDtypeStruct((OWN, D), BF16)
    return pl.pallas_call(
        fold_body,
        out_shape=(jax.ShapeDtypeStruct((OWN, D), F32), piece, piece, piece),
        in_specs=[vmem_spec()] * 4,
        out_specs=(vmem_spec(),) * 4,
        compiler_params=params(12),
        name="fold",
    )(*parts)


def finish_body(picked, attention, gate, own, r1, r2, r3, out):
    total = attention[...] + own[...]
    total = total + r1[...].astype(F32) + r2[...].astype(F32) + r3[...].astype(F32)
    out[...] = (picked[...].astype(F32) + gate[...] * total).astype(BF16)


def finish(picked, attention, gate, parts):
    return pl.pallas_call(
        finish_body,
        out_shape=jax.ShapeDtypeStruct((OWN, D), BF16),
        in_specs=[vmem_spec()] * 7,
        out_specs=vmem_spec(),
        compiler_params=params(12),
        name="finish",
    )(picked, attention, gate, *parts)


def merge_body(first, second, out, sems):
    copies = [pltpu.make_async_copy(ref, out.at[s * 3 * ROWS:(s + 1) * 3 * ROWS, :], sems.at[s])
              for s, ref in enumerate((first, second))]
    for copy in copies:
        copy.start()
    for copy in copies:
        copy.wait()


def merge(first, second):
    return pl.pallas_call(
        merge_body,
        out_shape=jax.ShapeDtypeStruct((6 * ROWS, FF_DEV), BF16),
        in_specs=[hbm_spec()] * 2,
        out_specs=vmem_spec(),
        scratch_shapes=[pltpu.SemaphoreType.DMA((2,))],
        compiler_params=params(60),
        name="merge",
    )(first, second)


def join_body(*refs):
    for i, ref in enumerate(refs[:4]):
        refs[4][i * OWN:(i + 1) * OWN, :] = ref[...]


def join(pieces):
    return pl.pallas_call(
        join_body,
        out_shape=jax.ShapeDtypeStruct((4 * OWN, D), BF16),
        in_specs=[vmem_spec()] * 4,
        out_specs=vmem_spec(),
        compiler_params=params(12),
        name="join",
    )(*pieces)


def place_body(info, chosen, block, *refs):
    pieces = refs[:2]
    out = refs[2]
    rows = refs[3]

    @pl.when(pl.program_id(0) == 0)
    def _():
        for core, piece in enumerate(pieces):
            for dx in range(4):
                at = lax.rem(info[2] + core, 2) * 128 + lax.rem(info[3] + 4 - dx, 4) * OWN
                rows[pl.ds(pl.multiple_of(at, OWN), OWN), :] = piece[dx * OWN:(dx + 1) * OWN, :]

    position = lax.broadcasted_iota(jnp.int32, (STEP, CAP), 0) + pl.program_id(0) * STEP
    slot = lax.broadcasted_iota(jnp.int32, (STEP, CAP), 1)
    hit = jnp.where((position == chosen[...]) & (slot < info[1]), 1.0, 0.0)
    taken = jnp.sum(hit, axis=1, keepdims=True) > 0.5
    hit = hit.astype(BF16)
    for n in range(D // 256):
        cols = slice(n * 256, (n + 1) * 256)
        new = jnp.dot(hit, rows[:, cols], preferred_element_type=F32).astype(BF16)
        out[:, cols] = jnp.where(taken, new, block[:, cols])


def put_back(info, chosen, block, pieces):
    return pl.pallas_call(
        place_body,
        grid=(SEQ_DEV // STEP,),
        out_shape=jax.ShapeDtypeStruct((SEQ_DEV, D), BF16),
        in_specs=[smem_spec(), pl.BlockSpec((1, CAP), lambda i: (0, 0)),
                  pl.BlockSpec((STEP, D), lambda i: (i, 0))]
        + [pl.BlockSpec((128, D), lambda i: (0, 0))] * 2,
        out_specs=pl.BlockSpec((STEP, D), lambda i: (i, 0)),
        scratch_shapes=[pltpu.VMEM((CAP, D), BF16)],
        compiler_params=params(60),
        name="put_back",
    )(info, chosen, block, *pieces)


def shift(value, axis, step, size=4):
    return lax.ppermute(value, axis, [(i, (i + step) % size) for i in range(size)])


def cross(value, step, first):
    pairs = []
    for y in range(4):
        for x in range(4):
            for c in range(2):
                along_x = (c == 0) == first
                to_y, to_x = (y, (x + step) % 4) if along_x else ((y + step) % 4, x)
                pairs.append((8 * y + 2 * x + c, 8 * to_y + 2 * to_x + c))
    return lax.ppermute(value, ("y", "x", "c"), pairs)


def around(value, step):
    pairs = [(2 * z + c, 2 * ((z + (step if c == 0 else 4 - step)) % 4) + c) for z in range(4) for c in range(2)]
    return lax.ppermute(value, ("z", "c"), pairs)


def swap(value):
    return shift(value, "c", 1, 2)


def weight_pairs(s):
    return [(2 * sy + sc, 2 * (2 * sc + (sy + s) % 2) + sy // 2) for sy in range(4) for sc in range(2)]


def tie(*values):
    return lax.optimization_barrier(values)


def local(block, preference, chosen, occupied, gain1, wq, wk, wv, wo, sharpness, gain2, gate_w, up_w, down_w):
    y, z, x, c = (lax.axis_index(n) for n in ("y", "z", "x", "c"))
    own_at = c * 128 + x * OWN
    info = jnp.stack([own_at, occupied[0], c, x, y, z, (4 * y + z) * SEQ_DEV]).astype(jnp.int32)
    near = 3 - 2 * c
    place = []
    for core, step in ((c, near), (1 - c, 4 - near)):
        for source in (z, z + step, z + 4 - step, z + 2):
            for s in range(2):
                place.append(4 * (2 * core + (y + s) % 2) + source % 4)
    place = jnp.stack(place).astype(jnp.int32)

    half = HD // 2
    frequency = 10000.0 ** (-jnp.arange(half, dtype=F32) / half)
    frequency = jnp.concatenate([frequency, frequency])[None, :]
    packs = pack(info, gate_w, up_w, down_w)
    *packs, info = tie(*packs, info)
    got = [lax.ppermute(p, ("y", "c"), weight_pairs(s)) for s, p in enumerate(packs)]
    q, kv, picked = begin(info, block, chosen[None, :], gain1[None, :], frequency, wq, wk, wv)

    kvs = [kv] + [shift(kv, "z", d) for d in (1, 2, 3)]
    q, *got = tie(q, *got)
    asked = [shift(q, "y", d) for d in (1, 2, 3)]
    merged = merge(*got)
    *kvs, merged = tie(*kvs, merged)
    near, side = around(merged, 1), around(merged, 3)

    scale = sharpness * (LOG2E / math.sqrt(HD))
    parts = []
    for d in (1, 2, 3):
        at = jnp.broadcast_to(jnp.where((y - d) % 4 > y, CAP, -CAP), (4,)).astype(jnp.int32)
        parts.append(shift(attend(False, at, scale, asked[d - 1], kvs), "y", 4 - d))
    at = jnp.stack([z * 0] + [jnp.where(z >= d, CAP, -CAP) for d in (1, 2, 3)]).astype(jnp.int32)
    parts.append(attend(True, at, scale, q, kvs))

    keep, send = mix(info, parts, wo)
    met, near = tie(swap(send), near)
    far = around(near, 1)
    own, s1, s2, s3 = split(info, keep, met)
    moved = [shift(s, "x", d) for d, s in ((1, s1), (2, s2), (3, s3))]
    *moved, side = tie(*moved, side)
    attention, normed = middle(picked, own, moved, gain2[None, :])

    moved = [cross(normed, d, True) for d in (1, 2, 3)]
    others = [swap(merged), swap(near), swap(side)]
    *moved, others[0], others[1], others[2] = tie(*moved, *others)
    row = join([normed] + moved)
    xs = [row] + [cross(row, e, False) for e in (1, 2, 3)]
    *xs, far = tie(*xs, far)
    outs = feed(place, xs, [merged, near, side, far] + others + [swap(far)])
    own, s1, s2, s3 = fold([outs[0]] + [cross(outs[e], 4 - e, False) for e in (1, 2, 3)])
    outs = [own] + [cross(s, 4 - d, True) for d, s in ((1, s1), (2, s2), (3, s3))]

    mine = lax.dynamic_slice_in_dim(chosen, own_at, OWN, 0)
    hit = mine[:, None] == jnp.arange(SEQ_DEV, dtype=jnp.int32)[None, :]
    router = jax.nn.sigmoid(jnp.sum(jnp.where(hit, preference[None, :], 0.0), axis=1, keepdims=True))
    result = finish(picked, attention, router, outs)
    rows = join([result] + [shift(result, "x", d) for d in (1, 2, 3)])
    return put_back(info, chosen[None, :], block, [rows, swap(rows)])


def solution(mesh):
    grid = Mesh(mesh.devices.reshape(4, 4, 4, 2), ("y", "z", "x", "c"))
    ctx, mp = ("y", "z"), ("x", "c")
    return jax.shard_map(
        local,
        mesh=grid,
        in_specs=(P(ctx, None), P(ctx), P(ctx), P(ctx), P(), P(None, mp), P(None, mp), P(None, mp),
                  P(mp, None), P(mp), P(), P(ctx, mp), P(ctx, mp), P(ctx, mp)),
        out_specs=P(ctx, None),
        check_vma=False,
    )
```

time: 340 us -> 212 us (0.62)
  the two profiles are of different devices: /device:TPU:39 before, /device:TPU:1 now
where the time goes in v2:
time: 212 us; the launch traced here: 209 us
  waiting for transfers between devices  77.6 us (37%)
  starting transfers between devices  66.4 us (31%)
  Pallas kernels  57.5 us (27%)
  local copies, waits for them, and re-layouts  5.06 us (2%)
    ppermute x12, waiting for transfers between devices, cross(): return lax.ppermute(value, ('y', 'x', 'c'), pairs)  41.2 us
    ppermute x21, starting transfers between devices, shift(): lax.ppermute(value, axis, [(i, (i + step) % size) for i in range(size)])  28.9 us
    ppermute x21, waiting for transfers between devices, shift(): lax.ppermute(value, axis, [(i, (i + step) % size) for i in range(size)])  27.9 us
    ppermute x12, starting transfers between devices, cross(): return lax.ppermute(value, ('y', 'x', 'c'), pairs)  23.9 us
    pallas_call x1, Pallas kernels, feed(): pl.pallas_call(feed_body, out_shape=(jax.ShapeDtypeStruct((4 * OWN, D), B...  17.1 us
    pallas_call x4, Pallas kernels, attend(): pl.pallas_call(functools.partial(attend_body, diagonal), out_shape=jax.Sh...  14.3 us
    pallas_call x1, Pallas kernels, begin(): pl.pallas_call(begin_body, out_shape=(jax.ShapeDtypeStruct((CAP, 512), BF...  9.45 us
    ppermute x2, waiting for transfers between devices, local(): lax.ppermute(p, ('y', 'c'), weight_pairs(s))  7.55 us
  transfers between devices with their start and end apart: 38, of which 22 were waited for; matrix products, arithmetic and copies ran while one was open for 1% of the time, Pallas kernels for 15%

profile of v2, /device:TPU:1, one launch (start us, length us, event | category | flops | bytes accessed | tf_op | source)
XLA Modules:
  0.0 208.7 jit_solution(15391826369877327676)
XLA Ops:
  4.3 6.2 %collective-permute-start = (bf16[432,1152]{1,0:T(8,128)(2,1)}, bf16[432,1152]{1,0:T(8,128)(2,1)S(1)}, u32[]{:S(2)}, u32[]{:S(2)}) collective-permute-start(bf16[432,1152]{1,0:T(8,128)(2,1)} %get-tuple-element.59), channel_id=1, source_target_pairs={{0,0},{1,64},{32,32},{33,96},{64,1},{65,65},{96,33},{97,97},{2,2},... | collective-permute-start | bytes 2985992 | tf_op jit(solution)/shard_map/ppermute | solution.py:478
  12.3 9.4 %begin.1 = (bf16[256,512]{1,0:T(8,128)(2,1)}, bf16[272,512]{1,0:T(8,128)(2,1)}, bf16[32,2304]{1,0:T(8,128)(2,1)}) custom-call(s32[7]{0:T(128)} %stack.90.info, bf16[1024,2304]{1,0:T(8,128)(2,1)} %block.1, s32[1,256]{1,0:T(1,128)} %bitcast.30, f32[1,2304]{1,0:T(1,128)} %broadcast_in_dim.39.gain, f32[1,128]{1,0:T(1,128)} %maximum_bitcast_fusion.frequency, ...), custom_call_target="tpu_custom_call" | custom-call | tf_op jit(solution)/shard_map/begin/pallas_call | solution.py:92
  23.5 3.3 %collective-permute-start.4 = (bf16[272,512]{1,0:T(8,128)(2,1)}, bf16[272,512]{1,0:T(8,128)(2,1)S(1)}, u32[]{:S(2)}, u32[]{:S(2)}) collective-permute-start(bf16[272,512]{1,0:T(8,128)(2,1)} %get-tuple-element.65.kv0), channel_id=1, source_target_pairs={{0,16},{8,24},{16,0},{24,8},{1,17},{9,25},{17,1},{25,9},{2,18},{10... | collective-permute-start | bytes 835592 | tf_op jit(solution)/shard_map/ppermute | solution.py:430
  27.5 6.0 %collective-permute-done.first = bf16[432,1152]{1,0:T(8,128)(2,1)S(1)} collective-permute-done((bf16[432,1152]{1,0:T(8,128)(2,1)}, bf16[432,1152]{1,0:T(8,128)(2,1)S(1)}, u32[]{:S(2)}, u32[]{:S(2)}) %collective-permute-start) | collective-permute-done | bytes 995360 | tf_op jit(solution)/shard_map/ppermute | solution.py:478
  38.9 3.8 %collective-permute-start.12 = (bf16[864,1152]{1,0:T(8,128)(2,1)}, bf16[864,1152]{1,0:T(8,128)(2,1)}, u32[]{:S(2)}, u32[]{:S(2)}) collective-permute-start(bf16[864,1152]{1,0:T(8,128)(2,1)} %merge.1.refs_5_), channel_id=1, source_target_pairs={{0,8},{1,25},{8,16},{9,1},{16,24},{17,9},{24,0},{25,17},{2,10},{3,... | collective-permute-start | bytes 5971976 | tf_op jit(solution)/shard_map/ppermute | solution.py:446
  44.7 6.7 %collective-permute-done.9.q = bf16[256,512]{1,0:T(8,128)(2,1)S(1)} collective-permute-done((bf16[256,512]{1,0:T(8,128)(2,1)}, bf16[256,512]{1,0:T(8,128)(2,1)S(1)}, u32[]{:S(2)}, u32[]{:S(2)}) %collective-permute-start.9) | collective-permute-done | bytes 262176 | tf_op jit(solution)/shard_map/ppermute | solution.py:430
  51.4 3.5 %attend.6 = bf16[272,512]{1,0:T(8,128)(2,1)} custom-call(s32[4]{0:T(128)S(1)} %broadcast_in_dim.43.at, f32[4]{0:T(128)S(1)} %broadcast_multiply_fusion.scale, bf16[256,512]{1,0:T(8,128)(2,1)S(1)} %collective-permute-done.9.q, bf16[272,512]{1,0:T(8,128)(2,1)S(1)} %copy-done, bf16[272,512]{1,0:T(8,128)(2,1)S(1)} %collective-permute-done.3.kv1, ...), custom_call_target="tpu_custom_call" | custom-call | tf_op jit(solution)/shard_map/attend/pallas_call | solution.py:180
  54.9 5.5 %collective-permute-start.10 = (bf16[272,512]{1,0:T(8,128)(2,1)}, bf16[272,512]{1,0:T(8,128)(2,1)}, u32[]{:S(2)}, u32[]{:S(2)}) collective-permute-start(bf16[272,512]{1,0:T(8,128)(2,1)} %attend.6), channel_id=1, source_target_pairs={{0,32},{32,64},{64,96},{96,0},{1,33},{33,65},{65,97},{97,1},{2,34}... | collective-permute-start | bytes 835592 | tf_op jit(solution)/shard_map/ppermute | solution.py:430
  60.5 3.5 %attend.5 = bf16[272,512]{1,0:T(8,128)(2,1)} custom-call(s32[4]{0:T(128)S(1)} %broadcast_in_dim.42.at, f32[4]{0:T(128)S(1)} %broadcast_multiply_fusion.scale, bf16[256,512]{1,0:T(8,128)(2,1)S(1)} %collective-permute-done.7.q, bf16[272,512]{1,0:T(8,128)(2,1)S(1)} %copy-done, bf16[272,512]{1,0:T(8,128)(2,1)S(1)} %collective-permute-done.3.kv1, ...), custom_call_target="tpu_custom_call" | custom-call | tf_op jit(solution)/shard_map/attend/pallas_call | solution.py:180
  64.0 4.1 %attend.4 = bf16[272,512]{1,0:T(8,128)(2,1)} custom-call(s32[4]{0:T(128)S(1)} %broadcast_in_dim.41.at, f32[4]{0:T(128)S(1)} %broadcast_multiply_fusion.scale, bf16[256,512]{1,0:T(8,128)(2,1)} %collective-permute-done.2.q, bf16[272,512]{1,0:T(8,128)(2,1)S(1)} %copy-done, bf16[272,512]{1,0:T(8,128)(2,1)S(1)} %collective-permute-done.3.kv1, ...), custom_call_target="tpu_custom_call" | custom-call | tf_op jit(solution)/shard_map/attend/pallas_call | solution.py:180
  73.9 3.4 %collective-permute-done.6.p0 = bf16[272,512]{1,0:T(8,128)(2,1)} collective-permute-done((bf16[272,512]{1,0:T(8,128)(2,1)}, bf16[272,512]{1,0:T(8,128)(2,1)}, u32[]{:S(2)}, u32[]{:S(2)}) %collective-permute-start.6) | collective-permute-done | bytes 278560 | tf_op jit(solution)/shard_map/ppermute | solution.py:430
  77.3 4.4 %mix.1 = (f32[128,2304]{1,0:T(8,128)S(1)}, bf16[128,2304]{1,0:T(8,128)(2,1)S(1)}) custom-call(s32[7]{0:T(128)S(1)} %copy-done.7, bf16[272,512]{1,0:T(8,128)(2,1)} %collective-permute-done.6.p0, bf16[272,512]{1,0:T(8,128)(2,1)} %collective-permute-done.8.p1, bf16[272,512]{1,0:T(8,128)(2,1)} %collective-permute-done.10.p2, bf16[272,512]{1,0:T(8,128)(2,1)S(1)} %attend.7.p3, ...), custom_call_target="tpu_custom_call" | custom-call | tf_op jit(solution)/shard_map/mix/pallas_call | solution.py:218
  92.6 4.2 %collective-permute-done.14.r2 = bf16[32,2304]{1,0:T(8,128)(2,1)S(1)} collective-permute-done((bf16[32,2304]{1,0:T(8,128)(2,1)S(1)}, bf16[32,2304]{1,0:T(8,128)(2,1)S(1)}, u32[]{:S(2)}, u32[]{:S(2)}) %collective-permute-start.14) | collective-permute-done | bytes 147488 | tf_op jit(solution)/shard_map/ppermute | solution.py:430
  106.1 10.0 %collective-permute-start.19 = (bf16[32,2304]{1,0:T(8,128)(2,1)S(1)}, bf16[32,2304]{1,0:T(8,128)(2,1)S(1)}, u32[]{:S(2)}, u32[]{:S(2)}) collective-permute-start(bf16[32,2304]{1,0:T(8,128)(2,1)S(1)} %get-tuple-element.81.refs_0_), channel_id=1, source_target_pairs={{0,6},{1,97},{2,0},{3,99},{4,2},{5,101},{6,4},{7,103},{32,38},{33,... | collective-permute-start | bytes 442376 | tf_op jit(solution)/shard_map/ppermute | solution.py:441
  116.1 4.0 %collective-permute-done.19.refs_3_ = bf16[32,2304]{1,0:T(8,128)(2,1)S(1)} collective-permute-done((bf16[32,2304]{1,0:T(8,128)(2,1)S(1)}, bf16[32,2304]{1,0:T(8,128)(2,1)S(1)}, u32[]{:S(2)}, u32[]{:S(2)}) %collective-permute-start.19) | collective-permute-done | bytes 147488 | tf_op jit(solution)/shard_map/ppermute | solution.py:441
  124.9 5.6 %collective-permute-done.23.refs_2_ = bf16[128,2304]{1,0:T(8,128)(2,1)S(1)} collective-permute-done((bf16[128,2304]{1,0:T(8,128)(2,1)S(1)}, bf16[128,2304]{1,0:T(8,128)(2,1)S(1)}, u32[]{:S(2)}, u32[]{:S(2)}) %collective-permute-start.23) | collective-permute-done | bytes 589856 | tf_op jit(solution)/shard_map/ppermute | solution.py:441
  130.5 6.7 %collective-permute-done.24.refs_3_ = bf16[128,2304]{1,0:T(8,128)(2,1)S(1)} collective-permute-done((bf16[128,2304]{1,0:T(8,128)(2,1)S(1)}, bf16[128,2304]{1,0:T(8,128)(2,1)S(1)}, u32[]{:S(2)}, u32[]{:S(2)}) %collective-permute-start.24) | collective-permute-done | bytes 589856 | tf_op jit(solution)/shard_map/ppermute | solution.py:441
  138.2 3.5 %collective-permute-done.27.refs_12_ = bf16[864,1152]{1,0:T(8,128)(2,1)} collective-permute-done((bf16[864,1152]{1,0:T(8,128)(2,1)}, bf16[864,1152]{1,0:T(8,128)(2,1)}, u32[]{:S(2)}, u32[]{:S(2)}) %collective-permute-start.27) | collective-permute-done | bytes 1990688 | tf_op jit(solution)/shard_map/ppermute | solution.py:430
  141.7 17.1 %feed.1 = (bf16[128,2304]{1,0:T(8,128)(2,1)}, bf16[128,2304]{1,0:T(8,128)(2,1)}, bf16[128,2304]{1,0:T(8,128)(2,1)}, bf16[128,2304]{1,0:T(8,128)(2,1)}) custom-call(s32[16]{0:T(128)} %stack.111.refs_0_, bf16[128,2304]{1,0:T(8,128)(2,1)} %copy-done.3, bf16[128,2304]{1,0:T(8,128)(2,1)} %copy-done.15, bf16[128,2304]{1,0:T(8,128)(2,1)} %copy-done.16, ...), custom_call_target="tpu_custom_call" | custom-call | tf_op jit(solution)/shard_map/feed/pallas_call | solution.py:305
  162.5 12.1 %collective-permute-done.28.p1 = bf16[128,2304]{1,0:T(8,128)(2,1)S(1)} collective-permute-done((bf16[128,2304]{1,0:T(8,128)(2,1)}, bf16[128,2304]{1,0:T(8,128)(2,1)S(1)}, u32[]{:S(2)}, u32[]{:S(2)}) %collective-permute-start.28) | collective-permute-done | bytes 589856 | tf_op jit(solution)/shard_map/ppermute | solution.py:441
  174.6 3.6 %collective-permute-done.30.p3 = bf16[128,2304]{1,0:T(8,128)(2,1)S(1)} collective-permute-done((bf16[128,2304]{1,0:T(8,128)(2,1)}, bf16[128,2304]{1,0:T(8,128)(2,1)S(1)}, u32[]{:S(2)}, u32[]{:S(2)}) %collective-permute-start.30) | collective-permute-done | bytes 589856 | tf_op jit(solution)/shard_map/ppermute | solution.py:441
  191.8 4.1 %collective-permute-done.34.refs_1_ = bf16[32,2304]{1,0:T(8,128)(2,1)S(1)} collective-permute-done((bf16[32,2304]{1,0:T(8,128)(2,1)S(1)}, bf16[32,2304]{1,0:T(8,128)(2,1)S(1)}, u32[]{:S(2)}, u32[]{:S(2)}) %collective-permute-start.34) | collective-permute-done | bytes 147488 | tf_op jit(solution)/shard_map/ppermute | solution.py:430
  196.8 4.2 %collective-permute-start.37 = (bf16[128,2304]{1,0:T(8,128)(2,1)S(1)}, bf16[128,2304]{1,0:T(8,128)(2,1)S(1)}, u32[]{:S(2)}, u32[]{:S(2)}) collective-permute-start(bf16[128,2304]{1,0:T(8,128)(2,1)S(1)} %join.3.refs_0_), channel_id=1, source_target_pairs={{0,1},{1,0},{2,3},{3,2},{4,5},{5,4},{6,7},{7,6},{8,9},{9,8},{10,11... | collective-permute-start | bytes 1769480 | tf_op jit(solution)/shard_map/ppermute | solution.py:430
  203.4 5.1 %put_back.1 = bf16[1024,2304]{1,0:T(8,128)(2,1)} custom-call(s32[7]{0:T(128)} %stack.90.info, s32[1,256]{1,0:T(1,128)} %bitcast.31, bf16[1024,2304]{1,0:T(8,128)(2,1)} %block.1, bf16[128,2304]{1,0:T(8,128)(2,1)} %copy-done.1, bf16[128,2304]{1,0:T(8,128)(2,1)} %copy-done.14), custom_call_target="tpu_custom_call" | custom-call | tf_op jit(solution)/shard_map/put_back/pallas_call | solution.py:415
  (129 shorter events, 67.6 us)
Async XLA Ops:
  4.3 29.2 %collective-permute-start = (bf16[432,1152]{1,0:T(8,128)(2,1)}, bf16[432,1152]{1,0:T(8,128)(2,1)S(1)}, u32[]{:S(2)}, u32[]{:S(2)}) collective-permute-start(bf16[432,1152]{1,0:T(8,128)(2,1)} %get-tuple-element.59), channel_id=1, source_target_pairs={{0,0},{1,64},{32,32},{33,96},{64,1},{65,65},{96,33},{97,97},{2,2},... | collective-permute-start | bytes 2985992 | tf_op jit(solution)/shard_map/ppermute | solution.py:478
  10.5 24.5 %collective-permute-start.1 = (bf16[432,1152]{1,0:T(8,128)(2,1)}, bf16[432,1152]{1,0:T(8,128)(2,1)S(1)}, u32[]{:S(2)}, u32[]{:S(2)}) collective-permute-start(bf16[432,1152]{1,0:T(8,128)(2,1)} %get-tuple-element.60), channel_id=1, source_target_pairs={{0,32},{1,96},{32,0},{33,64},{64,33},{65,97},{96,1},{97,65},{2,34}... | collective-permute-start | bytes 2985992 | tf_op jit(solution)/shard_map/ppermute | solution.py:478
  21.7 17.2 %collective-permute-start.3 = (bf16[272,512]{1,0:T(8,128)(2,1)}, bf16[272,512]{1,0:T(8,128)(2,1)S(1)}, u32[]{:S(2)}, u32[]{:S(2)}) collective-permute-start(bf16[272,512]{1,0:T(8,128)(2,1)} %get-tuple-element.65.kv0), channel_id=1, source_target_pairs={{0,8},{8,16},{16,24},{24,0},{1,9},{9,17},{17,25},{25,1},{2,10},{10... | collective-permute-start | bytes 835592 | tf_op jit(solution)/shard_map/ppermute | solution.py:430
  23.5 15.5 %collective-permute-start.4 = (bf16[272,512]{1,0:T(8,128)(2,1)}, bf16[272,512]{1,0:T(8,128)(2,1)S(1)}, u32[]{:S(2)}, u32[]{:S(2)}) collective-permute-start(bf16[272,512]{1,0:T(8,128)(2,1)} %get-tuple-element.65.kv0), channel_id=1, source_target_pairs={{0,16},{8,24},{16,0},{24,8},{1,17},{9,25},{17,1},{25,9},{2,18},{10... | collective-permute-start | bytes 835592 | tf_op jit(solution)/shard_map/ppermute | solution.py:430
  26.8 12.2 %collective-permute-start.5 = (bf16[272,512]{1,0:T(8,128)(2,1)}, bf16[272,512]{1,0:T(8,128)(2,1)S(1)}, u32[]{:S(2)}, u32[]{:S(2)}) collective-permute-start(bf16[272,512]{1,0:T(8,128)(2,1)} %get-tuple-element.65.kv0), channel_id=1, source_target_pairs={{0,24},{8,0},{16,8},{24,16},{1,25},{9,1},{17,9},{25,17},{2,26},{10... | collective-permute-start | bytes 835592 | tf_op jit(solution)/shard_map/ppermute | solution.py:430
  38.9 46.0 %collective-permute-start.12 = (bf16[864,1152]{1,0:T(8,128)(2,1)}, bf16[864,1152]{1,0:T(8,128)(2,1)}, u32[]{:S(2)}, u32[]{:S(2)}) collective-permute-start(bf16[864,1152]{1,0:T(8,128)(2,1)} %merge.1.refs_5_), channel_id=1, source_target_pairs={{0,8},{1,25},{8,16},{9,1},{16,24},{17,9},{24,0},{25,17},{2,10},{3,... | collective-permute-start | bytes 5971976 | tf_op jit(solution)/shard_map/ppermute | solution.py:446
  42.8 47.7 %collective-permute-start.16 = (bf16[864,1152]{1,0:T(8,128)(2,1)}, bf16[864,1152]{1,0:T(8,128)(2,1)}, u32[]{:S(2)}, u32[]{:S(2)}) collective-permute-start(bf16[864,1152]{1,0:T(8,128)(2,1)} %merge.1.refs_5_), channel_id=1, source_target_pairs={{0,24},{1,9},{8,0},{9,17},{16,8},{17,25},{24,16},{25,1},{2,26},{3,... | collective-permute-start | bytes 5971976 | tf_op jit(solution)/shard_map/ppermute | solution.py:446
  42.8 17.7 %collective-permute-start.7 = (bf16[256,512]{1,0:T(8,128)(2,1)}, bf16[256,512]{1,0:T(8,128)(2,1)S(1)}, u32[]{:S(2)}, u32[]{:S(2)}) collective-permute-start(bf16[256,512]{1,0:T(8,128)(2,1)} %get-tuple-element.61.q), channel_id=1, source_target_pairs={{0,64},{32,96},{64,0},{96,32},{1,65},{33,97},{65,1},{97,33},{2,66}... | collective-permute-start | bytes 786440 | tf_op jit(solution)/shard_map/ppermute | solution.py:430
  44.7 19.2 %collective-permute-start.2 = (bf16[256,512]{1,0:T(8,128)(2,1)}, bf16[256,512]{1,0:T(8,128)(2,1)}, u32[]{:S(2)}, u32[]{:S(2)}) collective-permute-start(bf16[256,512]{1,0:T(8,128)(2,1)} %get-tuple-element.61.q), channel_id=1, source_target_pairs={{0,32},{32,64},{64,96},{96,0},{1,33},{33,65},{65,97},{97,1},{2,34}... | collective-permute-start | bytes 786440 | tf_op jit(solution)/shard_map/ppermute | solution.py:430
  54.9 18.7 %collective-permute-start.10 = (bf16[272,512]{1,0:T(8,128)(2,1)}, bf16[272,512]{1,0:T(8,128)(2,1)}, u32[]{:S(2)}, u32[]{:S(2)}) collective-permute-start(bf16[272,512]{1,0:T(8,128)(2,1)} %attend.6), channel_id=1, source_target_pairs={{0,32},{32,64},{64,96},{96,0},{1,33},{33,65},{65,97},{97,1},{2,34}... | collective-permute-start | bytes 835592 | tf_op jit(solution)/shard_map/ppermute | solution.py:430
  64.0 9.9 %collective-permute-start.8 = (bf16[272,512]{1,0:T(8,128)(2,1)}, bf16[272,512]{1,0:T(8,128)(2,1)}, u32[]{:S(2)}, u32[]{:S(2)}) collective-permute-start(bf16[272,512]{1,0:T(8,128)(2,1)} %attend.5), channel_id=1, source_target_pairs={{0,64},{32,96},{64,0},{96,32},{1,65},{33,97},{65,1},{97,33},{2,66}... | collective-permute-start | bytes 835592 | tf_op jit(solution)/shard_map/ppermute | solution.py:430
  82.4 18.9 %collective-permute-start.20 = (bf16[864,1152]{1,0:T(8,128)(2,1)S(1)}, bf16[864,1152]{1,0:T(8,128)(2,1)S(1)}, u32[]{:S(2)}, u32[]{:S(2)}) collective-permute-start(bf16[864,1152]{1,0:T(8,128)(2,1)S(1)} %copy-done.8), channel_id=1, source_target_pairs={{0,1},{1,0},{2,3},{3,2},{4,5},{5,4},{6,7},{7,6},{8,9},{9,8},{10,11... | collective-permute-start | bytes 5971976 | tf_op jit(solution)/shard_map/ppermute | solution.py:430
  86.8 9.9 %collective-permute-start.14 = (bf16[32,2304]{1,0:T(8,128)(2,1)S(1)}, bf16[32,2304]{1,0:T(8,128)(2,1)S(1)}, u32[]{:S(2)}, u32[]{:S(2)}) collective-permute-start(bf16[32,2304]{1,0:T(8,128)(2,1)S(1)} %get-tuple-element.75), channel_id=1, source_target_pairs={{0,4},{2,6},{4,0},{6,2},{1,5},{3,7},{5,1},{7,3},{8,12},{10,14},{12... | collective-permute-start | bytes 442376 | tf_op jit(solution)/shard_map/ppermute | solution.py:430
  90.4 29.6 %collective-permute-start.21 = (bf16[864,1152]{1,0:T(8,128)(2,1)}, bf16[864,1152]{1,0:T(8,128)(2,1)S(1)}, u32[]{:S(2)}, u32[]{:S(2)}) collective-permute-start(bf16[864,1152]{1,0:T(8,128)(2,1)} %collective-permute-done.12.refs_6_), channel_id=1, source_target_pairs={{0,1},{1,0},{2,3},{3,2},{4,5},{5,4},{6,7},{7,6},{8,9},{9,8},{10,11... | collective-permute-start | bytes 5971976 | tf_op jit(solution)/shard_map/ppermute | solution.py:430
  96.7 23.3 %collective-permute-start.22 = (bf16[864,1152]{1,0:T(8,128)(2,1)}, bf16[864,1152]{1,0:T(8,128)(2,1)S(1)}, u32[]{:S(2)}, u32[]{:S(2)}) collective-permute-start(bf16[864,1152]{1,0:T(8,128)(2,1)} %collective-permute-done.16.refs_7_), channel_id=1, source_target_pairs={{0,1},{1,0},{2,3},{3,2},{4,5},{5,4},{6,7},{7,6},{8,9},{9,8},{10,11... | collective-permute-start | bytes 5971976 | tf_op jit(solution)/shard_map/ppermute | solution.py:430
  97.1 27.7 %collective-permute-start.26 = (bf16[864,1152]{1,0:T(8,128)(2,1)}, bf16[864,1152]{1,0:T(8,128)(2,1)}, u32[]{:S(2)}, u32[]{:S(2)}) collective-permute-start(bf16[864,1152]{1,0:T(8,128)(2,1)} %collective-permute-done.12.refs_6_), channel_id=1, source_target_pairs={{0,8},{1,25},{8,16},{9,1},{16,24},{17,9},{24,0},{25,17},{2,10},{3,... | collective-permute-start | bytes 5971976 | tf_op jit(solution)/shard_map/ppermute | solution.py:446
  101.3 14.8 %collective-permute-start.18 = (bf16[32,2304]{1,0:T(8,128)(2,1)S(1)}, bf16[32,2304]{1,0:T(8,128)(2,1)S(1)}, u32[]{:S(2)}, u32[]{:S(2)}) collective-permute-start(bf16[32,2304]{1,0:T(8,128)(2,1)S(1)} %get-tuple-element.81.refs_0_), channel_id=1, source_target_pairs={{0,4},{1,65},{2,6},{3,67},{4,0},{5,69},{6,2},{7,71},{32,36},{33,97... | collective-permute-start | bytes 442376 | tf_op jit(solution)/shard_map/ppermute | solution.py:441
  106.1 14.0 %collective-permute-start.19 = (bf16[32,2304]{1,0:T(8,128)(2,1)S(1)}, bf16[32,2304]{1,0:T(8,128)(2,1)S(1)}, u32[]{:S(2)}, u32[]{:S(2)}) collective-permute-start(bf16[32,2304]{1,0:T(8,128)(2,1)S(1)} %get-tuple-element.81.refs_0_), channel_id=1, source_target_pairs={{0,6},{1,97},{2,0},{3,99},{4,2},{5,101},{6,4},{7,103},{32,38},{33,... | collective-permute-start | bytes 442376 | tf_op jit(solution)/shard_map/ppermute | solution.py:441
  120.1 10.3 %collective-permute-start.23 = (bf16[128,2304]{1,0:T(8,128)(2,1)S(1)}, bf16[128,2304]{1,0:T(8,128)(2,1)S(1)}, u32[]{:S(2)}, u32[]{:S(2)}) collective-permute-start(bf16[128,2304]{1,0:T(8,128)(2,1)S(1)} %join.2.refs_1_), channel_id=1, source_target_pairs={{0,32},{1,3},{2,34},{3,5},{4,36},{5,7},{6,38},{7,1},{32,64},{33,35... | collective-permute-start | bytes 1769480 | tf_op jit(solution)/shard_map/ppermute | solution.py:441
  121.5 15.7 %collective-permute-start.24 = (bf16[128,2304]{1,0:T(8,128)(2,1)S(1)}, bf16[128,2304]{1,0:T(8,128)(2,1)S(1)}, u32[]{:S(2)}, u32[]{:S(2)}) collective-permute-start(bf16[128,2304]{1,0:T(8,128)(2,1)S(1)} %join.2.refs_1_), channel_id=1, source_target_pairs={{0,64},{1,5},{2,66},{3,7},{4,68},{5,1},{6,70},{7,3},{32,96},{33,37... | collective-permute-start | bytes 1769480 | tf_op jit(solution)/shard_map/ppermute | solution.py:441
  123.6 13.6 %collective-permute-start.25 = (bf16[128,2304]{1,0:T(8,128)(2,1)S(1)}, bf16[128,2304]{1,0:T(8,128)(2,1)S(1)}, u32[]{:S(2)}, u32[]{:S(2)}) collective-permute-start(bf16[128,2304]{1,0:T(8,128)(2,1)S(1)} %join.2.refs_1_), channel_id=1, source_target_pairs={{0,96},{1,7},{2,98},{3,1},{4,100},{5,3},{6,102},{7,5},{32,0},{33,3... | collective-permute-start | bytes 1769480 | tf_op jit(solution)/shard_map/ppermute | solution.py:441
  158.8 15.8 %collective-permute-start.28 = (bf16[128,2304]{1,0:T(8,128)(2,1)}, bf16[128,2304]{1,0:T(8,128)(2,1)S(1)}, u32[]{:S(2)}, u32[]{:S(2)}) collective-permute-start(bf16[128,2304]{1,0:T(8,128)(2,1)} %get-tuple-element.96), channel_id=1, source_target_pairs={{0,96},{1,7},{2,98},{3,1},{4,100},{5,3},{6,102},{7,5},{32,0},{33,3... | collective-permute-start | bytes 1769480 | tf_op jit(solution)/shard_map/ppermute | solution.py:441
  161.1 13.5 %collective-permute-start.29 = (bf16[128,2304]{1,0:T(8,128)(2,1)}, bf16[128,2304]{1,0:T(8,128)(2,1)S(1)}, u32[]{:S(2)}, u32[]{:S(2)}) collective-permute-start(bf16[128,2304]{1,0:T(8,128)(2,1)} %get-tuple-element.97), channel_id=1, source_target_pairs={{0,64},{1,5},{2,66},{3,7},{4,68},{5,1},{6,70},{7,3},{32,96},{33,37... | collective-permute-start | bytes 1769480 | tf_op jit(solution)/shard_map/ppermute | solution.py:441
  162.0 16.2 %collective-permute-start.30 = (bf16[128,2304]{1,0:T(8,128)(2,1)}, bf16[128,2304]{1,0:T(8,128)(2,1)S(1)}, u32[]{:S(2)}, u32[]{:S(2)}) collective-permute-start(bf16[128,2304]{1,0:T(8,128)(2,1)} %get-tuple-element.98), channel_id=1, source_target_pairs={{0,32},{1,3},{2,34},{3,5},{4,36},{5,7},{6,38},{7,1},{32,64},{33,35... | collective-permute-start | bytes 1769480 | tf_op jit(solution)/shard_map/ppermute | solution.py:441
  (37 other events, 428.8 us)

commit v3 on v2

--- a/solution.py
+++ b/solution.py
@@ -7,6 +7,7 @@
 from jax.experimental import pallas as pl
 from jax.experimental.pallas import tpu as pltpu
 from jax.sharding import Mesh, PartitionSpec as P
+import numpy as np
 
 D = 2304
 CAP = 256
@@ -40,7 +41,7 @@
     return pltpu.CompilerParams(vmem_limit_bytes=mib * MB)
 
 
-def begin_body(info, block_hbm, chosen, gain, frequency, wq_hbm, wk_hbm, wv_hbm,
+def begin_body(occupied, block_hbm, chosen, gain, frequency, wq_hbm, wk_hbm, wv_hbm,
                q_out, kv_out, own_out, block, picked, normed, wq, wk, wv, sems):
     tiles = D // 256
     loads = [pltpu.make_async_copy(block_hbm.at[:, i * 256:(i + 1) * 256],
@@ -52,6 +53,10 @@
         copy.start()
     wide = jnp.broadcast_to(chosen[...].astype(F32), (128, CAP))
     column = jnp.transpose(wide)[:, 0:1].astype(jnp.int32)
+    shard = 4 * lax.axis_index("y") + lax.axis_index("z")
+    angles = (column + shard * SEQ_DEV).astype(F32) * frequency[...]
+    cosine, sine = jnp.cos(angles), jnp.sin(angles)
+    sine = jnp.where(lax.broadcasted_iota(jnp.int32, (CAP, HD), 1) < HD // 2, -sine, sine)
     lanes = lax.broadcasted_iota(jnp.int32, (CAP, SEQ_DEV), 1)
     one_hot = jnp.where(lanes == column, 1.0, 0.0).astype(BF16)
     total = jnp.zeros((CAP, 256), F32)
@@ -61,14 +66,12 @@
         part = jnp.dot(one_hot, block[:, cols], preferred_element_type=F32)
         picked[:, cols] = part.astype(BF16)
         total = total + part * part
-    angles = (column + info[6]).astype(F32) * frequency[...]
-    cosine, sine = jnp.cos(angles), jnp.sin(angles)
-    sine = jnp.where(lax.broadcasted_iota(jnp.int32, (CAP, HD), 1) < HD // 2, -sine, sine)
     inv = lax.rsqrt(jnp.sum(total, axis=1, keepdims=True) / D + EPS)
     for i in range(tiles):
         cols = slice(i * 256, (i + 1) * 256)
         normed[:, cols] = (picked[:, cols].astype(F32) * inv * gain[:, cols]).astype(BF16)
-    own_out[...] = picked[pl.ds(pl.multiple_of(info[0], OWN), OWN), :]
+    first = lax.axis_index("c") * 128 + lax.axis_index("x") * OWN
+    own_out[...] = picked[pl.ds(pl.multiple_of(first, OWN), OWN), :]
 
     def turn(values):
         return values * cosine + pltpu.roll(values, HD // 2, 1) * sine
@@ -76,10 +79,10 @@
     weights[0].wait()
     keys = jnp.dot(normed[...], wk[...], preferred_element_type=F32)
     for h in range(2):
-        kv_out[0:CAP, h * HD:(h + 1) * HD] = turn(keys[:, h * HD:(h + 1) * HD]).astype(BF16)
+        kv_out[h * HD:(h + 1) * HD, 0:CAP] = jnp.transpose(turn(keys[:, h * HD:(h + 1) * HD])).astype(BF16)
     weights[1].wait()
     kv_out[0:CAP, 256:512] = jnp.dot(normed[...], wv[...], preferred_element_type=F32).astype(BF16)
-    kv_out[CAP:CAP + 16, :] = jnp.full((16, 512), info[1].astype(F32), F32).astype(BF16)
+    kv_out[CAP:CAP + 16, :] = jnp.full((16, 512), occupied[0].astype(F32), F32).astype(BF16)
     weights[2].wait()
     for j in range(2):
         part = jnp.dot(normed[...], wq[:, j * 256:(j + 1) * 256], preferred_element_type=F32)
@@ -88,7 +91,7 @@
             q_out[:, at:at + HD] = turn(part[:, h * HD:(h + 1) * HD]).astype(BF16)
 
 
-def begin(info, block, chosen, gain, frequency, wq, wk, wv):
+def begin(occupied, block, chosen, gain, frequency, wq, wk, wv):
     return pl.pallas_call(
         begin_body,
         out_shape=(jax.ShapeDtypeStruct((CAP, 512), BF16), jax.ShapeDtypeStruct((CAP + 16, 512), BF16),
@@ -100,13 +103,13 @@
                         pltpu.SemaphoreType.DMA((12,))],
         compiler_params=params(60),
         name="begin",
-    )(info, block, chosen, gain, frequency, wq, wk, wv)
-
-
-def pack_body(info, gate, up, down, out0, out1, packed, sems):
+    )(occupied, block, chosen, gain, frequency, wq, wk, wv)
+
+
+def pack_body(gate, up, down, out0, out1, packed, sems):
     loads, stores = [], []
     for s, out in enumerate((out0, out1)):
-        cols = pl.ds(pl.multiple_of(lax.rem(info[4] + s, 2) * FF_DEV, FF_DEV), FF_DEV)
+        cols = pl.ds(pl.multiple_of(lax.rem(lax.axis_index("y") + s, 2) * FF_DEV, FF_DEV), FF_DEV)
         for k, weight in enumerate((gate, up, down)):
             rows = slice(k * ROWS, (k + 1) * ROWS)
             at = 3 * s + k
@@ -121,19 +124,19 @@
         store.wait()
 
 
-def pack(info, gate, up, down):
+def pack(gate, up, down):
     return pl.pallas_call(
         pack_body,
         out_shape=(jax.ShapeDtypeStruct((3 * ROWS, FF_DEV), BF16),) * 2,
-        in_specs=[smem_spec()] + [hbm_spec()] * 3,
+        in_specs=[hbm_spec()] * 3,
         out_specs=(hbm_spec(),) * 2,
         scratch_shapes=[pltpu.VMEM((2, 3 * ROWS, FF_DEV), BF16), pltpu.SemaphoreType.DMA((12,))],
         compiler_params=params(60),
         name="pack",
-    )(info, gate, up, down)
-
-
-def attend_body(diagonal, at, scale, q, kv0, kv1, kv2, kv3, out, stats, turned):
+    )(gate, up, down)
+
+
+def attend_body(diagonal, at, scale, q, kv0, kv1, kv2, kv3, out, stats):
     lane = lax.broadcasted_iota(jnp.int32, (1, CAP), 1).astype(F32)
     bias = []
     kvs = (kv0, kv1, kv2, kv3)
@@ -141,8 +144,6 @@
         count = kv[CAP:CAP + 16, 0:CAP].astype(F32)[0:1, :]
         live = (lane < count) & (at[j] >= 0)
         bias.append(jnp.where(live, 0.0, NEG))
-        for g in range(2):
-            turned[g * HD:(g + 1) * HD, j * CAP:(j + 1) * CAP] = jnp.transpose(kv[0:CAP, g * HD:(g + 1) * HD])
     past = lax.broadcasted_iota(jnp.int32, (CAP, CAP), 1) - lax.broadcasted_iota(jnp.int32, (CAP, CAP), 0)
     for head in range(4):
         g = head // 2
@@ -150,8 +151,7 @@
         query = q[:, cols]
         scores = []
         for j in range(4):
-            part = jnp.dot(query, turned[g * HD:(g + 1) * HD, j * CAP:(j + 1) * CAP],
-                           preferred_element_type=F32)
+            part = jnp.dot(query, kvs[j][g * HD:(g + 1) * HD, 0:CAP], preferred_element_type=F32)
             part = part * scale[head] + bias[j]
             if diagonal:
                 part = jnp.where(past <= at[j], part, NEG)
@@ -182,13 +182,15 @@
         out_shape=jax.ShapeDtypeStruct((CAP + 16, 512), BF16),
         in_specs=[smem_spec()] * 2 + [vmem_spec()] * 5,
         out_specs=vmem_spec(),
-        scratch_shapes=[pltpu.VMEM((CAP, 128), F32), pltpu.VMEM((256, 1024), BF16)],
+        scratch_shapes=[pltpu.VMEM((CAP, 128), F32)],
         compiler_params=params(12),
         name="attend",
     )(at, scale, q, *kvs)
 
 
-def mix_body(info, p0, p1, p2, p3, wo, keep, send, mixed):
+def mix_body(p0, p1, p2, p3, wo_hbm, keep, send, mixed, wo, sem):
+    load = pltpu.make_async_copy(wo_hbm, wo, sem)
+    load.start()
     parts = (p0, p1, p2, p3)
     logs = []
     for part in parts:
@@ -203,46 +205,46 @@
         total = functools.reduce(jnp.add, weights)
         value = functools.reduce(jnp.add, [w * part[0:CAP, cols].astype(F32) for w, part in zip(weights, parts)])
         mixed[:, cols] = (value / total).astype(BF16)
-    core = info[2]
+    core = lax.axis_index("c")
     mine = mixed[pl.ds(pl.multiple_of(core * 128, 128), 128), :]
     other = mixed[pl.ds(pl.multiple_of((1 - core) * 128, 128), 128), :]
 
-    @pl.loop(0, D // 256)
-    def _(i):
-        cols = pl.ds(pl.multiple_of(i * 256, 256), 256)
+    load.wait()
+    for i in range(D // 256):
+        cols = slice(i * 256, (i + 1) * 256)
         send[:, cols] = jnp.dot(other, wo[:, cols], preferred_element_type=F32).astype(BF16)
         keep[:, cols] = jnp.dot(mine, wo[:, cols], preferred_element_type=F32)
 
 
-def mix(info, parts, wo):
+def mix(parts, wo):
     return pl.pallas_call(
         mix_body,
         out_shape=(jax.ShapeDtypeStruct((128, D), F32), jax.ShapeDtypeStruct((128, D), BF16)),
-        in_specs=[smem_spec()] + [vmem_spec()] * 5,
+        in_specs=[vmem_spec()] * 4 + [hbm_spec()],
         out_specs=(vmem_spec(),) * 2,
-        scratch_shapes=[pltpu.VMEM((CAP, 512), BF16)],
-        compiler_params=params(12),
+        scratch_shapes=[pltpu.VMEM((CAP, 512), BF16), pltpu.VMEM((512, D), BF16), pltpu.SemaphoreType.DMA],
+        compiler_params=params(16),
         name="mix",
-    )(info, *parts, wo)
-
-
-def split_body(info, keep, got, own, s1, s2, s3):
-    x = info[3]
+    )(*parts, wo)
+
+
+def split_body(keep, got, own, s1, s2, s3):
+    x = lax.axis_index("x")
     for d, ref in enumerate((own, s1, s2, s3)):
         rows = pl.ds(pl.multiple_of(lax.rem(x + d, 4) * OWN, OWN), OWN)
         ref[...] = (keep[rows, :] + got[rows, :].astype(F32)).astype(ref.dtype)
 
 
-def split(info, keep, got):
+def split(keep, got):
     piece = jax.ShapeDtypeStruct((OWN, D), BF16)
     return pl.pallas_call(
         split_body,
         out_shape=(jax.ShapeDtypeStruct((OWN, D), F32), piece, piece, piece),
-        in_specs=[smem_spec()] + [vmem_spec()] * 2,
+        in_specs=[vmem_spec()] * 2,
         out_specs=(vmem_spec(),) * 4,
         compiler_params=params(12),
         name="split",
-    )(info, keep, got)
+    )(keep, got)
 
 
 def middle_body(picked, own, r1, r2, r3, gain, attention, normed):
@@ -388,7 +390,25 @@
     )(*pieces)
 
 
-def place_body(info, chosen, block, *refs):
+def hold_body(block, out, sem):
+    copy = pltpu.make_async_copy(block, out, sem)
+    copy.start()
+    copy.wait()
+
+
+def hold(block):
+    return pl.pallas_call(
+        hold_body,
+        out_shape=jax.ShapeDtypeStruct((SEQ_DEV, D), BF16),
+        in_specs=[hbm_spec()],
+        out_specs=vmem_spec(),
+        scratch_shapes=[pltpu.SemaphoreType.DMA],
+        compiler_params=params(20),
+        name="hold",
+    )(block)
+
+
+def place_body(occupied, chosen, block, *refs):
     pieces = refs[:2]
     out = refs[2]
     rows = refs[3]
@@ -397,12 +417,12 @@
     def _():
         for core, piece in enumerate(pieces):
             for dx in range(4):
-                at = lax.rem(info[2] + core, 2) * 128 + lax.rem(info[3] + 4 - dx, 4) * OWN
+                at = lax.rem(lax.axis_index("c") + core, 2) * 128 + lax.rem(lax.axis_index("x") + 4 - dx, 4) * OWN
                 rows[pl.ds(pl.multiple_of(at, OWN), OWN), :] = piece[dx * OWN:(dx + 1) * OWN, :]
 
     position = lax.broadcasted_iota(jnp.int32, (STEP, CAP), 0) + pl.program_id(0) * STEP
     slot = lax.broadcasted_iota(jnp.int32, (STEP, CAP), 1)
-    hit = jnp.where((position == chosen[...]) & (slot < info[1]), 1.0, 0.0)
+    hit = jnp.where((position == chosen[...]) & (slot < occupied[0]), 1.0, 0.0)
     taken = jnp.sum(hit, axis=1, keepdims=True) > 0.5
     hit = hit.astype(BF16)
     for n in range(D // 256):
@@ -411,7 +431,7 @@
         out[:, cols] = jnp.where(taken, new, block[:, cols])
 
 
-def put_back(info, chosen, block, pieces):
+def put_back(occupied, chosen, block, pieces):
     return pl.pallas_call(
         place_body,
         grid=(SEQ_DEV // STEP,),
@@ -421,9 +441,9 @@
         + [pl.BlockSpec((128, D), lambda i: (0, 0))] * 2,
         out_specs=pl.BlockSpec((STEP, D), lambda i: (i, 0)),
         scratch_shapes=[pltpu.VMEM((CAP, D), BF16)],
-        compiler_params=params(60),
+        compiler_params=params(20),
         name="put_back",
-    )(info, chosen, block, *pieces)
+    )(occupied, chosen, block, *pieces)
 
 
 def shift(value, axis, step, size=4):
@@ -461,7 +481,6 @@
 def local(block, preference, chosen, occupied, gain1, wq, wk, wv, wo, sharpness, gain2, gate_w, up_w, down_w):
     y, z, x, c = (lax.axis_index(n) for n in ("y", "z", "x", "c"))
     own_at = c * 128 + x * OWN
-    info = jnp.stack([own_at, occupied[0], c, x, y, z, (4 * y + z) * SEQ_DEV]).astype(jnp.int32)
     near = 3 - 2 * c
     place = []
     for core, step in ((c, near), (1 - c, 4 - near)):
@@ -470,44 +489,44 @@
                 place.append(4 * (2 * core + (y + s) % 2) + source % 4)
     place = jnp.stack(place).astype(jnp.int32)
 
-    half = HD // 2
-    frequency = 10000.0 ** (-jnp.arange(half, dtype=F32) / half)
-    frequency = jnp.concatenate([frequency, frequency])[None, :]
-    packs = pack(info, gate_w, up_w, down_w)
-    *packs, info = tie(*packs, info)
+    frequency = 10000.0 ** (-(np.arange(HD) % (HD // 2)) / (HD // 2))
+    frequency = jnp.asarray(frequency.astype(np.float32)[None, :])
+    packs = pack(gate_w, up_w, down_w)
+    *packs, occupied = tie(*packs, occupied)
     got = [lax.ppermute(p, ("y", "c"), weight_pairs(s)) for s, p in enumerate(packs)]
-    q, kv, picked = begin(info, block, chosen[None, :], gain1[None, :], frequency, wq, wk, wv)
+    q, kv, picked = begin(occupied, block, chosen[None, :], gain1[None, :], frequency, wq, wk, wv)
 
     kvs = [kv] + [shift(kv, "z", d) for d in (1, 2, 3)]
     q, *got = tie(q, *got)
     asked = [shift(q, "y", d) for d in (1, 2, 3)]
     merged = merge(*got)
-    *kvs, merged = tie(*kvs, merged)
+
+    scale = sharpness * (LOG2E / math.sqrt(HD))
+    at = jnp.stack([z * 0] + [jnp.where(z >= d, CAP, -CAP) for d in (1, 2, 3)]).astype(jnp.int32)
+    mine = attend(True, at, scale, q, kvs)
+    mine, merged = tie(mine, merged)
     near, side = around(merged, 1), around(merged, 3)
-
-    scale = sharpness * (LOG2E / math.sqrt(HD))
-    parts = []
+    asked[0], mine = tie(asked[0], mine)
+    parts = [mine]
     for d in (1, 2, 3):
         at = jnp.broadcast_to(jnp.where((y - d) % 4 > y, CAP, -CAP), (4,)).astype(jnp.int32)
         parts.append(shift(attend(False, at, scale, asked[d - 1], kvs), "y", 4 - d))
-    at = jnp.stack([z * 0] + [jnp.where(z >= d, CAP, -CAP) for d in (1, 2, 3)]).astype(jnp.int32)
-    parts.append(attend(True, at, scale, q, kvs))
-
-    keep, send = mix(info, parts, wo)
-    met, near = tie(swap(send), near)
+
+    keep, send = mix(parts, wo)
+    own, s1, s2, s3 = split(keep, swap(send))
+    moved = [shift(s, "x", d) for d, s in ((1, s1), (2, s2), (3, s3))]
+    *moved, near, side = tie(*moved, near, side)
     far = around(near, 1)
-    own, s1, s2, s3 = split(info, keep, met)
-    moved = [shift(s, "x", d) for d, s in ((1, s1), (2, s2), (3, s3))]
-    *moved, side = tie(*moved, side)
     attention, normed = middle(picked, own, moved, gain2[None, :])
 
     moved = [cross(normed, d, True) for d in (1, 2, 3)]
-    others = [swap(merged), swap(near), swap(side)]
-    *moved, others[0], others[1], others[2] = tie(*moved, *others)
+    others = [swap(piece) for piece in (merged, near, side)]
+    *moved, others[0], others[1] = tie(*moved, *others[:2])
     row = join([normed] + moved)
     xs = [row] + [cross(row, e, False) for e in (1, 2, 3)]
-    *xs, far = tie(*xs, far)
-    outs = feed(place, xs, [merged, near, side, far] + others + [swap(far)])
+    *xs, others[2], far = tie(*xs, others[2], far)
+    others.append(swap(far))
+    outs = feed(place, xs, [merged, near, side, far] + others)
     own, s1, s2, s3 = fold([outs[0]] + [cross(outs[e], 4 - e, False) for e in (1, 2, 3)])
     outs = [own] + [cross(s, 4 - d, True) for d, s in ((1, s1), (2, s2), (3, s3))]
 
@@ -515,8 +534,9 @@
     hit = mine[:, None] == jnp.arange(SEQ_DEV, dtype=jnp.int32)[None, :]
     router = jax.nn.sigmoid(jnp.sum(jnp.where(hit, preference[None, :], 0.0), axis=1, keepdims=True))
     result = finish(picked, attention, router, outs)
-    rows = join([result] + [shift(result, "x", d) for d in (1, 2, 3)])
-    return put_back(info, chosen[None, :], block, [rows, swap(rows)])
+    *rows, block = tie(*[shift(result, "x", d) for d in (1, 2, 3)], hold(block))
+    rows = join([result] + rows)
+    return put_back(occupied, chosen[None, :], block, [rows, swap(rows)])
 
 
 def solution(mesh):

time: 212 us -> 204 us (0.962)
  Pallas kernels: 57.5 us -> 48.6 us
  waiting for transfers between devices: 77.6 us -> 71.7 us
  starting transfers between devices: 66.4 us -> 70.7 us
  local copies, waits for them, and re-layouts: 5.06 us -> 7.55 us
    ppermute x21, starting transfers between devices: 28.9 us -> 33.3 us  [shift(): lax.ppermute(value, axis, [(i, (i + step) % size) for i in range(size)])]
    ppermute x12, waiting for transfers between devices: 41.2 us -> 37.1 us  [cross(): return lax.ppermute(value, ('y', 'x', 'c'), pairs)]
    pallas_call x4, Pallas kernels: 14.3 us -> 10.8 us  [attend(): pl.pallas_call(functools.partial(attend_body, diagonal), out_shape=jax.Sh...]
    unnamed x46 -> x42, local copies, waits for them, and re-layouts: 2.96 us -> 6.15 us
    pallas_call x1, Pallas kernels: 4.4 us -> 2.1 us  [mix(): pl.pallas_call(mix_body, out_shape=(jax.ShapeDtypeStruct((128, D), F32),...]
  transfers between devices with their start and end apart: 38 -> 38, of which waited for: 22 -> 24; matrix products, arithmetic and copies ran while one was open for 1% -> 1% of each run, Pallas kernels for 15% -> 11%
where the time goes in v3:
time: 204 us; the launch traced here: 200 us
  waiting for transfers between devices  71.7 us (35%)
  starting transfers between devices  70.7 us (35%)
  Pallas kernels  48.6 us (24%)
  local copies, waits for them, and re-layouts  7.55 us (4%)
    ppermute x12, waiting for transfers between devices, cross(): return lax.ppermute(value, ('y', 'x', 'c'), pairs)  37.1 us
    ppermute x21, starting transfers between devices, shift(): lax.ppermute(value, axis, [(i, (i + step) % size) for i in range(size)])  33.3 us
    ppermute x21, waiting for transfers between devices, shift(): lax.ppermute(value, axis, [(i, (i + step) % size) for i in range(size)])  26.7 us
    ppermute x12, starting transfers between devices, cross(): return lax.ppermute(value, ('y', 'x', 'c'), pairs)  25.7 us
    pallas_call x1, Pallas kernels, feed(): pl.pallas_call(feed_body, out_shape=(jax.ShapeDtypeStruct((4 * OWN, D), B...  16.9 us
    pallas_call x4, Pallas kernels, attend(): pl.pallas_call(functools.partial(attend_body, diagonal), out_shape=jax.Sh...  10.8 us
    pallas_call x1, Pallas kernels, begin(): pl.pallas_call(begin_body, out_shape=(jax.ShapeDtypeStruct((CAP, 512), BF...  9.23 us
    ppermute x2, waiting for transfers between devices, local(): lax.ppermute(p, ('y', 'c'), weight_pairs(s))  7.63 us
  transfers between devices with their start and end apart: 38, of which 24 were waited for; matrix products, arithmetic and copies ran while one was open for 1% of the time, Pallas kernels for 11%

profile of v3, /device:TPU:1, one launch (start us, length us, event | category | flops | bytes accessed | tf_op | source)
XLA Modules:
  0.0 200.0 jit_solution(13785640713108936299)
XLA Ops:
  2.4 6.2 %collective-permute-start = (bf16[432,1152]{1,0:T(8,128)(2,1)}, bf16[432,1152]{1,0:T(8,128)(2,1)S(1)}, u32[]{:S(2)}, u32[]{:S(2)}) collective-permute-start(bf16[432,1152]{1,0:T(8,128)(2,1)} %get-tuple-element.61), channel_id=1, source_target_pairs={{0,0},{1,64},{32,32},{33,96},{64,1},{65,65},{96,33},{97,97},{2,2},... | collective-permute-start | bytes 2985992 | tf_op jit(solution)/shard_map/ppermute | solution.py:496
  10.4 9.2 %begin.1 = (bf16[256,512]{1,0:T(8,128)(2,1)}, bf16[272,512]{1,0:T(8,128)(2,1)}, bf16[32,2304]{1,0:T(8,128)(2,1)}) custom-call(s32[1]{0:T(128)S(6)} %copy.18.occupied, bf16[1024,2304]{1,0:T(8,128)(2,1)} %block.1, s32[1,256]{1,0:T(1,128)} %bitcast.22, f32[1,2304]{1,0:T(1,128)} %broadcast_in_dim.36.gain, f32[1,128]{1,0:T(1,128)} %constant.149.clone.frequency, ...), custom_call_target="tpu_custom_call" | custom-call | tf_op jit(solution)/shard_map/begin/pallas_call | solution.py:95
  21.4 3.3 %collective-permute-start.4 = (bf16[272,512]{1,0:T(8,128)(2,1)}, bf16[272,512]{1,0:T(8,128)(2,1)S(1)}, u32[]{:S(2)}, u32[]{:S(2)}) collective-permute-start(bf16[272,512]{1,0:T(8,128)(2,1)} %get-tuple-element.64.kv0), channel_id=1, source_target_pairs={{0,16},{8,24},{16,0},{24,8},{1,17},{9,25},{17,1},{25,9},{2,18},{10... | collective-permute-start | bytes 835592 | tf_op jit(solution)/shard_map/ppermute | solution.py:450
  25.5 6.1 %collective-permute-done.first = bf16[432,1152]{1,0:T(8,128)(2,1)S(1)} collective-permute-done((bf16[432,1152]{1,0:T(8,128)(2,1)}, bf16[432,1152]{1,0:T(8,128)(2,1)S(1)}, u32[]{:S(2)}, u32[]{:S(2)}) %collective-permute-start) | collective-permute-done | bytes 995360 | tf_op jit(solution)/shard_map/ppermute | solution.py:496
  33.1 2.9 %merge.1.refs_5_ = bf16[864,1152]{1,0:T(8,128)(2,1)} custom-call(bf16[432,1152]{1,0:T(8,128)(2,1)} %copy-done.13, bf16[432,1152]{1,0:T(8,128)(2,1)} %collective-permute-done.1.second), custom_call_target="tpu_custom_call" | custom-call | tf_op jit(solution)/shard_map/merge/pallas_call | solution.py:366
  36.4 2.8 %attend.4.p0 = bf16[272,512]{1,0:T(8,128)(2,1)S(1)} custom-call(s32[4]{0:T(128)S(1)} %pad_add_fusion.at, f32[4]{0:T(128)S(1)} %broadcast_multiply_fusion.scale, bf16[256,512]{1,0:T(8,128)(2,1)S(1)} %copy-done.6, bf16[272,512]{1,0:T(8,128)(2,1)S(1)} %copy-done.1, bf16[272,512]{1,0:T(8,128)(2,1)S(1)} %collective-permute-done.3.kv1, ...), custom_call_target="tpu_custom_call" | custom-call | tf_op jit(solution)/shard_map/attend/pallas_call | solution.py:180
  39.2 3.5 %collective-permute-start.15 = (bf16[864,1152]{1,0:T(8,128)(2,1)}, bf16[864,1152]{1,0:T(8,128)(2,1)}, u32[]{:S(2)}, u32[]{:S(2)}) collective-permute-start(bf16[864,1152]{1,0:T(8,128)(2,1)} %merge.1.refs_5_), channel_id=1, source_target_pairs={{0,8},{1,25},{8,16},{9,1},{16,24},{17,9},{24,0},{25,17},{2,10},{3,... | collective-permute-start | bytes 5971976 | tf_op jit(solution)/shard_map/ppermute | solution.py:466
  44.9 6.1 %collective-permute-done.9.q = bf16[256,512]{1,0:T(8,128)(2,1)S(1)} collective-permute-done((bf16[256,512]{1,0:T(8,128)(2,1)S(1)}, bf16[256,512]{1,0:T(8,128)(2,1)S(1)}, u32[]{:S(2)}, u32[]{:S(2)}) %collective-permute-start.9) | collective-permute-done | bytes 262176 | tf_op jit(solution)/shard_map/ppermute | solution.py:450
  53.7 5.7 %collective-permute-start.10 = (bf16[272,512]{1,0:T(8,128)(2,1)S(1)}, bf16[272,512]{1,0:T(8,128)(2,1)S(1)}, u32[]{:S(2)}, u32[]{:S(2)}) collective-permute-start(bf16[272,512]{1,0:T(8,128)(2,1)S(1)} %attend.7), channel_id=1, source_target_pairs={{0,32},{32,64},{64,96},{96,0},{1,33},{33,65},{65,97},{97,1},{2,34}... | collective-permute-start | bytes 835592 | tf_op jit(solution)/shard_map/ppermute | solution.py:450
  59.5 2.7 %attend.6 = bf16[272,512]{1,0:T(8,128)(2,1)S(1)} custom-call(s32[4]{0:T(128)S(1)} %broadcast_in_dim.38.at, f32[4]{0:T(128)S(1)} %broadcast_multiply_fusion.scale, bf16[256,512]{1,0:T(8,128)(2,1)S(1)} %collective-permute-done.7.q, bf16[272,512]{1,0:T(8,128)(2,1)S(1)} %copy-done.1, bf16[272,512]{1,0:T(8,128)(2,1)S(1)} %collective-permute-done.3.kv1, ...), custom_call_target="tpu_custom_call" | custom-call | tf_op jit(solution)/shard_map/attend/pallas_call | solution.py:180
  62.2 2.7 %attend.5 = bf16[272,512]{1,0:T(8,128)(2,1)S(1)} custom-call(s32[4]{0:T(128)S(1)} %broadcast_in_dim.37.at, f32[4]{0:T(128)S(1)} %broadcast_multiply_fusion.scale, bf16[256,512]{1,0:T(8,128)(2,1)S(1)} %collective-permute-done.2.q, bf16[272,512]{1,0:T(8,128)(2,1)S(1)} %copy-done.1, bf16[272,512]{1,0:T(8,128)(2,1)S(1)} %collective-permute-done.3.kv1, ...), custom_call_target="tpu_custom_call" | custom-call | tf_op jit(solution)/shard_map/attend/pallas_call | solution.py:180
  67.4 3.8 %collective-permute-done.8.p2 = bf16[272,512]{1,0:T(8,128)(2,1)S(1)} collective-permute-done((bf16[272,512]{1,0:T(8,128)(2,1)S(1)}, bf16[272,512]{1,0:T(8,128)(2,1)S(1)}, u32[]{:S(2)}, u32[]{:S(2)}) %collective-permute-start.8) | collective-permute-done | bytes 278560 | tf_op jit(solution)/shard_map/ppermute | solution.py:450
  71.2 3.8 %collective-permute-done.6.p1 = bf16[272,512]{1,0:T(8,128)(2,1)S(1)} collective-permute-done((bf16[272,512]{1,0:T(8,128)(2,1)S(1)}, bf16[272,512]{1,0:T(8,128)(2,1)S(1)}, u32[]{:S(2)}, u32[]{:S(2)}) %collective-permute-start.6) | collective-permute-done | bytes 278560 | tf_op jit(solution)/shard_map/ppermute | solution.py:450
  87.3 2.9 %collective-permute-done.13.r2 = bf16[32,2304]{1,0:T(8,128)(2,1)S(1)} collective-permute-done((bf16[32,2304]{1,0:T(8,128)(2,1)S(1)}, bf16[32,2304]{1,0:T(8,128)(2,1)S(1)}, u32[]{:S(2)}, u32[]{:S(2)}) %collective-permute-start.13) | collective-permute-done | bytes 147488 | tf_op jit(solution)/shard_map/ppermute | solution.py:450
  94.9 11.9 %collective-permute-start.18 = (bf16[32,2304]{1,0:T(8,128)(2,1)S(1)}, bf16[32,2304]{1,0:T(8,128)(2,1)S(1)}, u32[]{:S(2)}, u32[]{:S(2)}) collective-permute-start(bf16[32,2304]{1,0:T(8,128)(2,1)S(1)} %get-tuple-element.81.refs_0_), channel_id=1, source_target_pairs={{0,4},{1,65},{2,6},{3,67},{4,0},{5,69},{6,2},{7,71},{32,36},{33,97... | collective-permute-start | bytes 442376 | tf_op jit(solution)/shard_map/ppermute | solution.py:461
  107.6 2.7 %collective-permute-done.18.refs_2_ = bf16[32,2304]{1,0:T(8,128)(2,1)S(1)} collective-permute-done((bf16[32,2304]{1,0:T(8,128)(2,1)S(1)}, bf16[32,2304]{1,0:T(8,128)(2,1)S(1)}, u32[]{:S(2)}, u32[]{:S(2)}) %collective-permute-start.18) | collective-permute-done | bytes 147488 | tf_op jit(solution)/shard_map/ppermute | solution.py:461
  116.0 5.6 %collective-permute-done.22.refs_2_ = bf16[128,2304]{1,0:T(8,128)(2,1)S(1)} collective-permute-done((bf16[128,2304]{1,0:T(8,128)(2,1)S(1)}, bf16[128,2304]{1,0:T(8,128)(2,1)S(1)}, u32[]{:S(2)}, u32[]{:S(2)}) %collective-permute-start.22) | collective-permute-done | bytes 589856 | tf_op jit(solution)/shard_map/ppermute | solution.py:461
  121.6 6.7 %collective-permute-done.23.refs_3_ = bf16[128,2304]{1,0:T(8,128)(2,1)S(1)} collective-permute-done((bf16[128,2304]{1,0:T(8,128)(2,1)S(1)}, bf16[128,2304]{1,0:T(8,128)(2,1)S(1)}, u32[]{:S(2)}, u32[]{:S(2)}) %collective-permute-start.23) | collective-permute-done | bytes 589856 | tf_op jit(solution)/shard_map/ppermute | solution.py:461
  131.9 3.2 %collective-permute-done.27.refs_12_ = bf16[864,1152]{1,0:T(8,128)(2,1)S(1)} collective-permute-done((bf16[864,1152]{1,0:T(8,128)(2,1)}, bf16[864,1152]{1,0:T(8,128)(2,1)S(1)}, u32[]{:S(2)}, u32[]{:S(2)}) %collective-permute-start.27) | collective-permute-done | bytes 1990688 | tf_op jit(solution)/shard_map/ppermute | solution.py:450
  136.4 16.9 %feed.1 = (bf16[128,2304]{1,0:T(8,128)(2,1)}, bf16[128,2304]{1,0:T(8,128)(2,1)}, bf16[128,2304]{1,0:T(8,128)(2,1)}, bf16[128,2304]{1,0:T(8,128)(2,1)}) custom-call(s32[16]{0:T(128)} %stack.83.refs_0_, bf16[128,2304]{1,0:T(8,128)(2,1)} %copy-done.3, bf16[128,2304]{1,0:T(8,128)(2,1)} %copy-done.14, bf16[128,2304]{1,0:T(8,128)(2,1)} %copy-done.15, ...), custom_call_target="tpu_custom_call" | custom-call | tf_op jit(solution)/shard_map/feed/pallas_call | solution.py:307
  157.2 12.2 %collective-permute-done.28.p1 = bf16[128,2304]{1,0:T(8,128)(2,1)S(1)} collective-permute-done((bf16[128,2304]{1,0:T(8,128)(2,1)}, bf16[128,2304]{1,0:T(8,128)(2,1)S(1)}, u32[]{:S(2)}, u32[]{:S(2)}) %collective-permute-start.28) | collective-permute-done | bytes 589856 | tf_op jit(solution)/shard_map/ppermute | solution.py:461
  169.4 3.6 %collective-permute-done.30.p3 = bf16[128,2304]{1,0:T(8,128)(2,1)S(1)} collective-permute-done((bf16[128,2304]{1,0:T(8,128)(2,1)}, bf16[128,2304]{1,0:T(8,128)(2,1)S(1)}, u32[]{:S(2)}, u32[]{:S(2)}) %collective-permute-start.30) | collective-permute-done | bytes 589856 | tf_op jit(solution)/shard_map/ppermute | solution.py:461
  190.9 4.2 %collective-permute-start.37 = (bf16[128,2304]{1,0:T(8,128)(2,1)S(1)}, bf16[128,2304]{1,0:T(8,128)(2,1)S(1)}, u32[]{:S(2)}, u32[]{:S(2)}) collective-permute-start(bf16[128,2304]{1,0:T(8,128)(2,1)S(1)} %join.3.refs_0_), channel_id=1, source_target_pairs={{0,1},{1,0},{2,3},{3,2},{4,5},{5,4},{6,7},{7,6},{8,9},{9,8},{10,11... | collective-permute-start | bytes 1769480 | tf_op jit(solution)/shard_map/ppermute | solution.py:450
  196.7 3.1 %put_back.1 = bf16[1024,2304]{1,0:T(8,128)(2,1)} custom-call(s32[1]{0:T(128)S(6)} %copy.18.occupied, s32[1,256]{1,0:T(1,128)S(1)} %bitcast.23, bf16[1024,2304]{1,0:T(8,128)(2,1)S(1)} %hold.1.block, bf16[128,2304]{1,0:T(8,128)(2,1)S(1)} %join.3.refs_0_, bf16[128,2304]{1,0:T(8,128)(2,1)S(1)} %collective-permute-done.37.refs_1_), custom_call_target="tpu_custom_call" | custom-call | tf_op jit(solution)/shard_map/put_back/pallas_call | solution.py:435
  (123 shorter events, 67.1 us)
Async XLA Ops:
  2.4 29.2 %collective-permute-start = (bf16[432,1152]{1,0:T(8,128)(2,1)}, bf16[432,1152]{1,0:T(8,128)(2,1)S(1)}, u32[]{:S(2)}, u32[]{:S(2)}) collective-permute-start(bf16[432,1152]{1,0:T(8,128)(2,1)} %get-tuple-element.61), channel_id=1, source_target_pairs={{0,0},{1,64},{32,32},{33,96},{64,1},{65,65},{96,33},{97,97},{2,2},... | collective-permute-start | bytes 2985992 | tf_op jit(solution)/shard_map/ppermute | solution.py:496
  8.6 24.5 %collective-permute-start.1 = (bf16[432,1152]{1,0:T(8,128)(2,1)}, bf16[432,1152]{1,0:T(8,128)(2,1)}, u32[]{:S(2)}, u32[]{:S(2)}) collective-permute-start(bf16[432,1152]{1,0:T(8,128)(2,1)} %get-tuple-element.62), channel_id=1, source_target_pairs={{0,32},{1,96},{32,0},{33,64},{64,33},{65,97},{96,1},{97,65},{2,34}... | collective-permute-start | bytes 2985992 | tf_op jit(solution)/shard_map/ppermute | solution.py:496
  19.7 16.3 %collective-permute-start.3 = (bf16[272,512]{1,0:T(8,128)(2,1)}, bf16[272,512]{1,0:T(8,128)(2,1)S(1)}, u32[]{:S(2)}, u32[]{:S(2)}) collective-permute-start(bf16[272,512]{1,0:T(8,128)(2,1)} %get-tuple-element.64.kv0), channel_id=1, source_target_pairs={{0,8},{8,16},{16,24},{24,0},{1,9},{9,17},{17,25},{25,1},{2,10},{10... | collective-permute-start | bytes 835592 | tf_op jit(solution)/shard_map/ppermute | solution.py:450
  21.4 15.0 %collective-permute-start.4 = (bf16[272,512]{1,0:T(8,128)(2,1)}, bf16[272,512]{1,0:T(8,128)(2,1)S(1)}, u32[]{:S(2)}, u32[]{:S(2)}) collective-permute-start(bf16[272,512]{1,0:T(8,128)(2,1)} %get-tuple-element.64.kv0), channel_id=1, source_target_pairs={{0,16},{8,24},{16,0},{24,8},{1,17},{9,25},{17,1},{25,9},{2,18},{10... | collective-permute-start | bytes 835592 | tf_op jit(solution)/shard_map/ppermute | solution.py:450
  24.7 11.7 %collective-permute-start.5 = (bf16[272,512]{1,0:T(8,128)(2,1)}, bf16[272,512]{1,0:T(8,128)(2,1)S(1)}, u32[]{:S(2)}, u32[]{:S(2)}) collective-permute-start(bf16[272,512]{1,0:T(8,128)(2,1)} %get-tuple-element.64.kv0), channel_id=1, source_target_pairs={{0,24},{8,0},{16,8},{24,16},{1,25},{9,1},{17,9},{25,17},{2,26},{10... | collective-permute-start | bytes 835592 | tf_op jit(solution)/shard_map/ppermute | solution.py:450
  39.2 51.1 %collective-permute-start.15 = (bf16[864,1152]{1,0:T(8,128)(2,1)}, bf16[864,1152]{1,0:T(8,128)(2,1)}, u32[]{:S(2)}, u32[]{:S(2)}) collective-permute-start(bf16[864,1152]{1,0:T(8,128)(2,1)} %merge.1.refs_5_), channel_id=1, source_target_pairs={{0,8},{1,25},{8,16},{9,1},{16,24},{17,9},{24,0},{25,17},{2,10},{3,... | collective-permute-start | bytes 5971976 | tf_op jit(solution)/shard_map/ppermute | solution.py:466
  42.6 47.7 %collective-permute-start.16 = (bf16[864,1152]{1,0:T(8,128)(2,1)}, bf16[864,1152]{1,0:T(8,128)(2,1)}, u32[]{:S(2)}, u32[]{:S(2)}) collective-permute-start(bf16[864,1152]{1,0:T(8,128)(2,1)} %merge.1.refs_5_), channel_id=1, source_target_pairs={{0,24},{1,9},{8,0},{9,17},{16,8},{17,25},{24,16},{25,1},{2,26},{3,... | collective-permute-start | bytes 5971976 | tf_op jit(solution)/shard_map/ppermute | solution.py:466
  42.6 16.8 %collective-permute-start.7 = (bf16[256,512]{1,0:T(8,128)(2,1)S(1)}, bf16[256,512]{1,0:T(8,128)(2,1)S(1)}, u32[]{:S(2)}, u32[]{:S(2)}) collective-permute-start(bf16[256,512]{1,0:T(8,128)(2,1)S(1)} %copy-done.6), channel_id=1, source_target_pairs={{0,64},{32,96},{64,0},{96,32},{1,65},{33,97},{65,1},{97,33},{2,66}... | collective-permute-start | bytes 786440 | tf_op jit(solution)/shard_map/ppermute | solution.py:450
  44.6 17.6 %collective-permute-start.2 = (bf16[256,512]{1,0:T(8,128)(2,1)S(1)}, bf16[256,512]{1,0:T(8,128)(2,1)S(1)}, u32[]{:S(2)}, u32[]{:S(2)}) collective-permute-start(bf16[256,512]{1,0:T(8,128)(2,1)S(1)} %copy-done.6), channel_id=1, source_target_pairs={{0,32},{32,64},{64,96},{96,0},{1,33},{33,65},{65,97},{97,1},{2,34}... | collective-permute-start | bytes 786440 | tf_op jit(solution)/shard_map/ppermute | solution.py:450
  53.7 13.7 %collective-permute-start.10 = (bf16[272,512]{1,0:T(8,128)(2,1)S(1)}, bf16[272,512]{1,0:T(8,128)(2,1)S(1)}, u32[]{:S(2)}, u32[]{:S(2)}) collective-permute-start(bf16[272,512]{1,0:T(8,128)(2,1)S(1)} %attend.7), channel_id=1, source_target_pairs={{0,32},{32,64},{64,96},{96,0},{1,33},{33,65},{65,97},{97,1},{2,34}... | collective-permute-start | bytes 835592 | tf_op jit(solution)/shard_map/ppermute | solution.py:450
  62.2 9.0 %collective-permute-start.8 = (bf16[272,512]{1,0:T(8,128)(2,1)S(1)}, bf16[272,512]{1,0:T(8,128)(2,1)S(1)}, u32[]{:S(2)}, u32[]{:S(2)}) collective-permute-start(bf16[272,512]{1,0:T(8,128)(2,1)S(1)} %attend.6), channel_id=1, source_target_pairs={{0,64},{32,96},{64,0},{96,32},{1,65},{33,97},{65,1},{97,33},{2,66}... | collective-permute-start | bytes 835592 | tf_op jit(solution)/shard_map/ppermute | solution.py:450
  65.0 10.0 %collective-permute-start.6 = (bf16[272,512]{1,0:T(8,128)(2,1)S(1)}, bf16[272,512]{1,0:T(8,128)(2,1)S(1)}, u32[]{:S(2)}, u32[]{:S(2)}) collective-permute-start(bf16[272,512]{1,0:T(8,128)(2,1)S(1)} %attend.5), channel_id=1, source_target_pairs={{0,96},{32,0},{64,32},{96,64},{1,97},{33,1},{65,33},{97,65},{2,98}... | collective-permute-start | bytes 835592 | tf_op jit(solution)/shard_map/ppermute | solution.py:450
  81.1 9.2 %collective-permute-start.13 = (bf16[32,2304]{1,0:T(8,128)(2,1)S(1)}, bf16[32,2304]{1,0:T(8,128)(2,1)S(1)}, u32[]{:S(2)}, u32[]{:S(2)}) collective-permute-start(bf16[32,2304]{1,0:T(8,128)(2,1)S(1)} %get-tuple-element.74), channel_id=1, source_target_pairs={{0,4},{2,6},{4,0},{6,2},{1,5},{3,7},{5,1},{7,3},{8,12},{10,14},{12... | collective-permute-start | bytes 442376 | tf_op jit(solution)/shard_map/ppermute | solution.py:450
  90.3 21.0 %collective-permute-start.21 = (bf16[864,1152]{1,0:T(8,128)(2,1)}, bf16[864,1152]{1,0:T(8,128)(2,1)S(1)}, u32[]{:S(2)}, u32[]{:S(2)}) collective-permute-start(bf16[864,1152]{1,0:T(8,128)(2,1)} %collective-permute-done.15.refs_6_), channel_id=1, source_target_pairs={{0,1},{1,0},{2,3},{3,2},{4,5},{5,4},{6,7},{7,6},{8,9},{9,8},{10,11... | collective-permute-start | bytes 5971976 | tf_op jit(solution)/shard_map/ppermute | solution.py:450
  91.6 24.2 %collective-permute-start.25 = (bf16[864,1152]{1,0:T(8,128)(2,1)}, bf16[864,1152]{1,0:T(8,128)(2,1)S(1)}, u32[]{:S(2)}, u32[]{:S(2)}) collective-permute-start(bf16[864,1152]{1,0:T(8,128)(2,1)} %collective-permute-done.16.refs_7_), channel_id=1, source_target_pairs={{0,1},{1,0},{2,3},{3,2},{4,5},{5,4},{6,7},{7,6},{8,9},{9,8},{10,11... | collective-permute-start | bytes 5971976 | tf_op jit(solution)/shard_map/ppermute | solution.py:450
  91.7 24.4 %collective-permute-start.26 = (bf16[864,1152]{1,0:T(8,128)(2,1)}, bf16[864,1152]{1,0:T(8,128)(2,1)}, u32[]{:S(2)}, u32[]{:S(2)}) collective-permute-start(bf16[864,1152]{1,0:T(8,128)(2,1)} %collective-permute-done.15.refs_6_), channel_id=1, source_target_pairs={{0,8},{1,25},{8,16},{9,1},{16,24},{17,9},{24,0},{25,17},{2,10},{3,... | collective-permute-start | bytes 5971976 | tf_op jit(solution)/shard_map/ppermute | solution.py:466
  93.3 13.6 %collective-permute-start.17 = (bf16[32,2304]{1,0:T(8,128)(2,1)S(1)}, bf16[32,2304]{1,0:T(8,128)(2,1)S(1)}, u32[]{:S(2)}, u32[]{:S(2)}) collective-permute-start(bf16[32,2304]{1,0:T(8,128)(2,1)S(1)} %get-tuple-element.81.refs_0_), channel_id=1, source_target_pairs={{0,2},{1,33},{2,4},{3,35},{4,6},{5,37},{6,0},{7,39},{32,34},{33,65... | collective-permute-start | bytes 442376 | tf_op jit(solution)/shard_map/ppermute | solution.py:461
  94.9 15.4 %collective-permute-start.18 = (bf16[32,2304]{1,0:T(8,128)(2,1)S(1)}, bf16[32,2304]{1,0:T(8,128)(2,1)S(1)}, u32[]{:S(2)}, u32[]{:S(2)}) collective-permute-start(bf16[32,2304]{1,0:T(8,128)(2,1)S(1)} %get-tuple-element.81.refs_0_), channel_id=1, source_target_pairs={{0,4},{1,65},{2,6},{3,67},{4,0},{5,69},{6,2},{7,71},{32,36},{33,97... | collective-permute-start | bytes 442376 | tf_op jit(solution)/shard_map/ppermute | solution.py:461
  111.3 10.3 %collective-permute-start.22 = (bf16[128,2304]{1,0:T(8,128)(2,1)S(1)}, bf16[128,2304]{1,0:T(8,128)(2,1)S(1)}, u32[]{:S(2)}, u32[]{:S(2)}) collective-permute-start(bf16[128,2304]{1,0:T(8,128)(2,1)S(1)} %join.2.refs_1_), channel_id=1, source_target_pairs={{0,32},{1,3},{2,34},{3,5},{4,36},{5,7},{6,38},{7,1},{32,64},{33,35... | collective-permute-start | bytes 1769480 | tf_op jit(solution)/shard_map/ppermute | solution.py:461
  112.3 16.0 %collective-permute-start.23 = (bf16[128,2304]{1,0:T(8,128)(2,1)S(1)}, bf16[128,2304]{1,0:T(8,128)(2,1)S(1)}, u32[]{:S(2)}, u32[]{:S(2)}) collective-permute-start(bf16[128,2304]{1,0:T(8,128)(2,1)S(1)} %join.2.refs_1_), channel_id=1, source_target_pairs={{0,64},{1,5},{2,66},{3,7},{4,68},{5,1},{6,70},{7,3},{32,96},{33,37... | collective-permute-start | bytes 1769480 | tf_op jit(solution)/shard_map/ppermute | solution.py:461
  114.5 14.1 %collective-permute-start.24 = (bf16[128,2304]{1,0:T(8,128)(2,1)S(1)}, bf16[128,2304]{1,0:T(8,128)(2,1)S(1)}, u32[]{:S(2)}, u32[]{:S(2)}) collective-permute-start(bf16[128,2304]{1,0:T(8,128)(2,1)S(1)} %join.2.refs_1_), channel_id=1, source_target_pairs={{0,96},{1,7},{2,98},{3,1},{4,100},{5,3},{6,102},{7,5},{32,0},{33,3... | collective-permute-start | bytes 1769480 | tf_op jit(solution)/shard_map/ppermute | solution.py:461
  153.3 16.1 %collective-permute-start.28 = (bf16[128,2304]{1,0:T(8,128)(2,1)}, bf16[128,2304]{1,0:T(8,128)(2,1)S(1)}, u32[]{:S(2)}, u32[]{:S(2)}) collective-permute-start(bf16[128,2304]{1,0:T(8,128)(2,1)} %get-tuple-element.96), channel_id=1, source_target_pairs={{0,96},{1,7},{2,98},{3,1},{4,100},{5,3},{6,102},{7,5},{32,0},{33,3... | collective-permute-start | bytes 1769480 | tf_op jit(solution)/shard_map/ppermute | solution.py:461
  155.9 13.5 %collective-permute-start.29 = (bf16[128,2304]{1,0:T(8,128)(2,1)}, bf16[128,2304]{1,0:T(8,128)(2,1)S(1)}, u32[]{:S(2)}, u32[]{:S(2)}) collective-permute-start(bf16[128,2304]{1,0:T(8,128)(2,1)} %get-tuple-element.97), channel_id=1, source_target_pairs={{0,64},{1,5},{2,66},{3,7},{4,68},{5,1},{6,70},{7,3},{32,96},{33,37... | collective-permute-start | bytes 1769480 | tf_op jit(solution)/shard_map/ppermute | solution.py:461
  156.9 16.1 %collective-permute-start.30 = (bf16[128,2304]{1,0:T(8,128)(2,1)}, bf16[128,2304]{1,0:T(8,128)(2,1)S(1)}, u32[]{:S(2)}, u32[]{:S(2)}) collective-permute-start(bf16[128,2304]{1,0:T(8,128)(2,1)} %get-tuple-element.98), channel_id=1, source_target_pairs={{0,32},{1,3},{2,34},{3,5},{4,36},{5,7},{6,38},{7,1},{32,64},{33,35... | collective-permute-start | bytes 1769480 | tf_op jit(solution)/shard_map/ppermute | solution.py:461
  (35 other events, 365.8 us)

commit v4 on v3

--- a/solution.py
+++ b/solution.py
@@ -42,14 +42,14 @@
 
 
 def begin_body(occupied, block_hbm, chosen, gain, frequency, wq_hbm, wk_hbm, wv_hbm,
-               q_out, kv_out, own_out, block, picked, normed, wq, wk, wv, sems):
+               q_out, kv_hbm, own_out, block, picked, normed, wq, wk, wv, kv_out, sems):
     tiles = D // 256
     loads = [pltpu.make_async_copy(block_hbm.at[:, i * 256:(i + 1) * 256],
                                    block.at[:, i * 256:(i + 1) * 256], sems.at[i])
              for i in range(tiles)]
     weights = [pltpu.make_async_copy(src, dst, sems.at[9 + i])
                for i, (src, dst) in enumerate(((wk_hbm, wk), (wv_hbm, wv), (wq_hbm, wq)))]
-    for copy in loads + weights:
+    for copy in loads:
         copy.start()
     wide = jnp.broadcast_to(chosen[...].astype(F32), (128, CAP))
     column = jnp.transpose(wide)[:, 0:1].astype(jnp.int32)
@@ -63,6 +63,9 @@
     for i in range(tiles):
         cols = slice(i * 256, (i + 1) * 256)
         loads[i].wait()
+        if i == 4:
+            for copy in weights:
+                copy.start()
         part = jnp.dot(one_hot, block[:, cols], preferred_element_type=F32)
         picked[:, cols] = part.astype(BF16)
         total = total + part * part
@@ -83,23 +86,29 @@
     weights[1].wait()
     kv_out[0:CAP, 256:512] = jnp.dot(normed[...], wv[...], preferred_element_type=F32).astype(BF16)
     kv_out[CAP:CAP + 16, :] = jnp.full((16, 512), occupied[0].astype(F32), F32).astype(BF16)
+    stores = [pltpu.make_async_copy(kv_out, kv_hbm.at[n], sems.at[n]) for n in range(4)]
+    for copy in stores:
+        copy.start()
     weights[2].wait()
     for j in range(2):
         part = jnp.dot(normed[...], wq[:, j * 256:(j + 1) * 256], preferred_element_type=F32)
         for h in range(2):
             at = j * 256 + h * HD
             q_out[:, at:at + HD] = turn(part[:, h * HD:(h + 1) * HD]).astype(BF16)
+    for copy in stores:
+        copy.wait()
 
 
 def begin(occupied, block, chosen, gain, frequency, wq, wk, wv):
     return pl.pallas_call(
         begin_body,
-        out_shape=(jax.ShapeDtypeStruct((CAP, 512), BF16), jax.ShapeDtypeStruct((CAP + 16, 512), BF16),
+        out_shape=(jax.ShapeDtypeStruct((CAP, 512), BF16), jax.ShapeDtypeStruct((4, CAP + 16, 512), BF16),
                    jax.ShapeDtypeStruct((OWN, D), BF16)),
         in_specs=[smem_spec(), hbm_spec()] + [vmem_spec()] * 3 + [hbm_spec()] * 3,
-        out_specs=(vmem_spec(),) * 3,
+        out_specs=(vmem_spec(), hbm_spec(), vmem_spec()),
         scratch_shapes=[pltpu.VMEM((SEQ_DEV, D), BF16), pltpu.VMEM((CAP, D), BF16), pltpu.VMEM((CAP, D), BF16),
                         pltpu.VMEM((D, 512), BF16), pltpu.VMEM((D, 256), BF16), pltpu.VMEM((D, 256), BF16),
+                        pltpu.VMEM((CAP + 16, 512), BF16),
                         pltpu.SemaphoreType.DMA((12,))],
         compiler_params=params(60),
         name="begin",
@@ -136,12 +145,11 @@
     )(gate, up, down)
 
 
-def attend_body(diagonal, at, scale, q, kv0, kv1, kv2, kv3, out, stats):
+def attend_body(diagonal, at, scale, q, kv, out, stats):
     lane = lax.broadcasted_iota(jnp.int32, (1, CAP), 1).astype(F32)
     bias = []
-    kvs = (kv0, kv1, kv2, kv3)
-    for j, kv in enumerate(kvs):
-        count = kv[CAP:CAP + 16, 0:CAP].astype(F32)[0:1, :]
+    for j in range(4):
+        count = kv[j, CAP:CAP + 16, 0:CAP].astype(F32)[0:1, :]
         live = (lane < count) & (at[j] >= 0)
         bias.append(jnp.where(live, 0.0, NEG))
     past = lax.broadcasted_iota(jnp.int32, (CAP, CAP), 1) - lax.broadcasted_iota(jnp.int32, (CAP, CAP), 0)
@@ -151,7 +159,7 @@
         query = q[:, cols]
         scores = []
         for j in range(4):
-            part = jnp.dot(query, kvs[j][g * HD:(g + 1) * HD, 0:CAP], preferred_element_type=F32)
+            part = jnp.dot(query, kv[j, g * HD:(g + 1) * HD, 0:CAP], preferred_element_type=F32)
             part = part * scale[head] + bias[j]
             if diagonal:
                 part = jnp.where(past <= at[j], part, NEG)
@@ -160,8 +168,8 @@
         weights = [jnp.exp2(part - top) for part in scores]
         total = jnp.sum(functools.reduce(jnp.add, weights), axis=1, keepdims=True)
         mixed = jnp.zeros((CAP, HD), F32)
-        for j, kv in enumerate(kvs):
-            mixed = mixed + jnp.dot(weights[j].astype(BF16), kv[0:CAP, 256 + g * HD:256 + (g + 1) * HD],
+        for j in range(4):
+            mixed = mixed + jnp.dot(weights[j].astype(BF16), kv[j, 0:CAP, 256 + g * HD:256 + (g + 1) * HD],
                                     preferred_element_type=F32)
         out[0:CAP, cols] = (mixed * (1.0 / total)).astype(BF16)
         log_sum = top + jnp.log2(total)
@@ -176,16 +184,16 @@
     out[CAP:CAP + 16, CAP:512] = jnp.zeros((16, 512 - CAP), BF16)
 
 
-def attend(diagonal, at, scale, q, kvs):
+def attend(diagonal, at, scale, q, kv):
     return pl.pallas_call(
         functools.partial(attend_body, diagonal),
         out_shape=jax.ShapeDtypeStruct((CAP + 16, 512), BF16),
-        in_specs=[smem_spec()] * 2 + [vmem_spec()] * 5,
+        in_specs=[smem_spec()] * 2 + [vmem_spec()] * 2,
         out_specs=vmem_spec(),
         scratch_shapes=[pltpu.VMEM((CAP, 128), F32)],
         compiler_params=params(12),
         name="attend",
-    )(at, scale, q, *kvs)
+    )(at, scale, q, kv)
 
 
 def mix_body(p0, p1, p2, p3, wo_hbm, keep, send, mixed, wo, sem):
@@ -271,7 +279,7 @@
     xs = refs[1:5]
     pieces = refs[5:13]
     outs = refs[13:17]
-    tokens, gate, up, down, hidden, sems = refs[17:]
+    tokens, gate, up, down, hidden, acted, sems = refs[17:]
     copies = [[], [], []]
     for e, x in enumerate(xs):
         copies[0].append(pltpu.make_async_copy(x, tokens.at[e * 128:(e + 1) * 128, :], sems.at[e]))
@@ -281,18 +289,23 @@
             at = (3 * (i % 2) + k) * ROWS
             copies[k].append(pltpu.make_async_copy(pieces[i // 2].at[at:at + ROWS, :], weight.at[rows, :],
                                                    sems.at[4 + 16 * k + i]))
-    for copy in copies[0] + copies[1] + copies[2]:
+    for copy in copies[0]:
         copy.start()
+    chunks = [slice(j * 256, min((j + 1) * 256, FF_DEV)) for j in range(5)]
     for copy in copies[0]:
         copy.wait()
-    chunks = [slice(j * 256, min((j + 1) * 256, FF_DEV)) for j in range(5)]
-    for j, cols in enumerate(chunks):
+    for copy in copies[1]:
+        copy.start()
+    for cols in chunks:
         one = jnp.dot(tokens[...], gate[:, cols], preferred_element_type=F32)
-        if j == 0:
-            for copy in copies[1]:
-                copy.wait()
+        acted[:, cols] = one / (1.0 + jnp.exp(-one))
+    for copy in copies[1]:
+        copy.wait()
+    for copy in copies[2]:
+        copy.start()
+    for cols in chunks:
         two = jnp.dot(tokens[...], up[:, cols], preferred_element_type=F32)
-        hidden[:, cols] = (one / (1.0 + jnp.exp(-one)) * two).astype(BF16)
+        hidden[:, cols] = (acted[:, cols] * two).astype(BF16)
     for copy in copies[2]:
         copy.wait()
     for n in range(D // 256):
@@ -310,7 +323,7 @@
         in_specs=[smem_spec()] + [hbm_spec()] * 12,
         out_specs=(vmem_spec(),) * 4,
         scratch_shapes=[pltpu.VMEM((512, D), BF16), pltpu.VMEM((D, FF_DEV), BF16), pltpu.VMEM((D, FF_DEV), BF16),
-                        pltpu.VMEM((D, FF_DEV), BF16), pltpu.VMEM((512, FF_DEV), BF16),
+                        pltpu.VMEM((D, FF_DEV), BF16), pltpu.VMEM((512, FF_DEV), BF16), pltpu.VMEM((512, FF_DEV), F32),
                         pltpu.SemaphoreType.DMA((52,))],
         compiler_params=params(60),
         name="feed",
@@ -496,32 +509,34 @@
     got = [lax.ppermute(p, ("y", "c"), weight_pairs(s)) for s, p in enumerate(packs)]
     q, kv, picked = begin(occupied, block, chosen[None, :], gain1[None, :], frequency, wq, wk, wv)
 
-    kvs = [kv] + [shift(kv, "z", d) for d in (1, 2, 3)]
-    q, *got = tie(q, *got)
+    kv = lax.all_to_all(kv, "z", 0, 0)
     asked = [shift(q, "y", d) for d in (1, 2, 3)]
     merged = merge(*got)
+    kv, *asked, merged = tie(kv, *asked, merged)
+    near = around(merged, 1)
 
     scale = sharpness * (LOG2E / math.sqrt(HD))
-    at = jnp.stack([z * 0] + [jnp.where(z >= d, CAP, -CAP) for d in (1, 2, 3)]).astype(jnp.int32)
-    mine = attend(True, at, scale, q, kvs)
-    mine, merged = tie(mine, merged)
-    near, side = around(merged, 1), around(merged, 3)
-    asked[0], mine = tie(asked[0], mine)
-    parts = [mine]
+    parts = []
     for d in (1, 2, 3):
         at = jnp.broadcast_to(jnp.where((y - d) % 4 > y, CAP, -CAP), (4,)).astype(jnp.int32)
-        parts.append(shift(attend(False, at, scale, asked[d - 1], kvs), "y", 4 - d))
-
+        parts.append(shift(attend(False, at, scale, asked[d - 1], kv), "y", 4 - d))
+    at = jnp.stack([jnp.where(j < z, CAP, jnp.where(j == z, 0, -CAP)) for j in range(4)]).astype(jnp.int32)
+    parts.append(attend(True, at, scale, q, kv))
+
+    *parts, near, merged = tie(*parts, near, merged)
+    side = around(merged, 3)
     keep, send = mix(parts, wo)
-    own, s1, s2, s3 = split(keep, swap(send))
+    others = [swap(piece) for piece in (merged, near, side)]
+    met, others[0] = tie(swap(send), others[0])
+    own, s1, s2, s3 = split(keep, met)
     moved = [shift(s, "x", d) for d, s in ((1, s1), (2, s2), (3, s3))]
-    *moved, near, side = tie(*moved, near, side)
+    *moved, others[1], near = tie(*moved, others[1], near)
     far = around(near, 1)
     attention, normed = middle(picked, own, moved, gain2[None, :])
 
     moved = [cross(normed, d, True) for d in (1, 2, 3)]
-    others = [swap(piece) for piece in (merged, near, side)]
-    *moved, others[0], others[1] = tie(*moved, *others[:2])
+    *moved, side = tie(*moved, side)
+    others[2] = swap(side)
     row = join([normed] + moved)
     xs = [row] + [cross(row, e, False) for e in (1, 2, 3)]
     *xs, others[2], far = tie(*xs, others[2], far)

time: 204 us -> 189 us (0.926); the launches traced: 200 us -> 189 us
  starting transfers between devices: 70.7 us -> 60.5 us
  waiting for transfers between devices: 71.7 us -> 67.7 us
  Pallas kernels: 48.6 us -> 51.7 us
    ppermute x12, starting transfers between devices: 25.7 us -> 10.8 us  [cross(): return lax.ppermute(value, ('y', 'x', 'c'), pairs)]
    ppermute x21 -> x18, waiting for transfers between devices: 26.7 us -> 19.2 us  [shift(): lax.ppermute(value, axis, [(i, (i + step) % size) for i in range(size)])]
    all_to_all x0 -> x1, starting transfers between devices: none -> 5.17 us  [local(): kv = lax.all_to_all(kv, 'z', 0, 0)]
    ppermute x3, waiting for transfers between devices: 0.25 us -> 3.64 us  [around(): return lax.ppermute(value, ('z', 'c'), pairs)]
    ppermute x2, waiting for transfers between devices: 7.63 us -> 10.5 us  [local(): lax.ppermute(p, ('y', 'c'), weight_pairs(s))]
    ppermute x12, waiting for transfers between devices: 37.1 us -> 34.3 us  [cross(): return lax.ppermute(value, ('y', 'x', 'c'), pairs)]
    pallas_call x4, Pallas kernels: 10.8 us -> 13 us  [attend(): pl.pallas_call(functools.partial(attend_body, diagonal), out_shape=jax.Sh...]
    ppermute x21 -> x18, starting transfers between devices: 33.3 us -> 32.4 us  [shift(): lax.ppermute(value, axis, [(i, (i + step) % size) for i in range(size)])]
  transfers between devices with their start and end apart: 38 -> 36, of which waited for: 24 -> 23; matrix products, arithmetic and copies ran while one was open for 1% -> 1% of each run, Pallas kernels for 11% -> 15%
where the time goes in v4:
time: 189 us
  waiting for transfers between devices  67.7 us (36%)
  starting transfers between devices  60.5 us (32%)
  Pallas kernels  51.7 us (27%)
  local copies, waits for them, and re-layouts  7.82 us (4%)
    ppermute x12, waiting for transfers between devices, cross(): return lax.ppermute(value, ('y', 'x', 'c'), pairs)  34.3 us
    ppermute x18, starting transfers between devices, shift(): lax.ppermute(value, axis, [(i, (i + step) % size) for i in range(size)])  32.4 us
    ppermute x18, waiting for transfers between devices, shift(): lax.ppermute(value, axis, [(i, (i + step) % size) for i in range(size)])  19.2 us
    pallas_call x1, Pallas kernels, feed(): pl.pallas_call(feed_body, out_shape=(jax.ShapeDtypeStruct((4 * OWN, D), B...  16.7 us
    pallas_call x4, Pallas kernels, attend(): pl.pallas_call(functools.partial(attend_body, diagonal), out_shape=jax.Sh...  13 us
    ppermute x12, starting transfers between devices, cross(): return lax.ppermute(value, ('y', 'x', 'c'), pairs)  10.8 us
    ppermute x2, waiting for transfers between devices, local(): lax.ppermute(p, ('y', 'c'), weight_pairs(s))  10.5 us
    pallas_call x1, Pallas kernels, begin(): pl.pallas_call(begin_body, out_shape=(jax.ShapeDtypeStruct((CAP, 512), BF...  9.39 us
  transfers between devices with their start and end apart: 36, of which 23 were waited for; matrix products, arithmetic and copies ran while one was open for 1% of the time, Pallas kernels for 15%

profile of v4, /device:TPU:1, one launch (start us, length us, event | category | flops | bytes accessed | tf_op | source)
XLA Modules:
  0.0 188.9 jit_solution(5223419787091404960)
XLA Ops:
  2.4 6.2 %collective-permute-start.3 = (bf16[432,1152]{1,0:T(8,128)(2,1)}, bf16[432,1152]{1,0:T(8,128)(2,1)S(1)}, u32[]{:S(2)}, u32[]{:S(2)}) collective-permute-start(bf16[432,1152]{1,0:T(8,128)(2,1)} %get-tuple-element.67), channel_id=1, source_target_pairs={{0,0},{1,64},{32,32},{33,96},{64,1},{65,65},{96,33},{97,97},{2,2},... | collective-permute-start | bytes 2985992 | tf_op jit(solution)/shard_map/ppermute | solution.py:509
  10.5 9.4 %begin.1 = (bf16[256,512]{1,0:T(8,128)(2,1)}, bf16[4,272,512]{2,1,0:T(8,128)(2,1)}, bf16[32,2304]{1,0:T(8,128)(2,1)}) custom-call(s32[1]{0:T(128)S(6)} %copy.18.occupied, bf16[1024,2304]{1,0:T(8,128)(2,1)} %block.1, s32[1,256]{1,0:T(1,128)} %bitcast.23, f32[1,2304]{1,0:T(1,128)} %broadcast_in_dim.36.gain, f32[1,128]{1,0:T(1,128)} %constant.147.clone.frequency, ...), custom_call_target="tpu_custom_call" | custom-call | tf_op jit(solution)/shard_map/begin/pallas_call | solution.py:103
  19.9 5.2 %all-to-all-start = ((bf16[4,272,512]{2,1,0:T(8,128)(2,1)}), bf16[4,272,512]{2,1,0:T(8,128)(2,1)S(1)}, u32[]{:S(2)}, u32[]{:S(2)}) async-start(bf16[4,272,512]{2,1,0:T(8,128)(2,1)} %get-tuple-element.65), calls=%async_computation | async-start | bytes 2228224 | tf_op jit(solution)/shard_map/all_to_all | solution.py:512
  27.7 3.6 %collective-permute-done.3.first = bf16[432,1152]{1,0:T(8,128)(2,1)S(1)} collective-permute-done((bf16[432,1152]{1,0:T(8,128)(2,1)}, bf16[432,1152]{1,0:T(8,128)(2,1)S(1)}, u32[]{:S(2)}, u32[]{:S(2)}) %collective-permute-start.3) | collective-permute-done | bytes 995360 | tf_op jit(solution)/shard_map/ppermute | solution.py:509
  31.3 6.9 %collective-permute-done.4.second = bf16[432,1152]{1,0:T(8,128)(2,1)} collective-permute-done((bf16[432,1152]{1,0:T(8,128)(2,1)}, bf16[432,1152]{1,0:T(8,128)(2,1)}, u32[]{:S(2)}, u32[]{:S(2)}) %collective-permute-start.4) | collective-permute-done | bytes 995360 | tf_op jit(solution)/shard_map/ppermute | solution.py:509
  38.2 2.8 %merge.1.refs_5_ = bf16[864,1152]{1,0:T(8,128)(2,1)} custom-call(bf16[432,1152]{1,0:T(8,128)(2,1)} %copy-done.15, bf16[432,1152]{1,0:T(8,128)(2,1)} %collective-permute-done.4.second), custom_call_target="tpu_custom_call" | custom-call | tf_op jit(solution)/shard_map/merge/pallas_call | solution.py:379
  42.9 3.8 %collective-permute-start.8 = (bf16[864,1152]{1,0:T(8,128)(2,1)}, bf16[864,1152]{1,0:T(8,128)(2,1)}, u32[]{:S(2)}, u32[]{:S(2)}) collective-permute-start(bf16[864,1152]{1,0:T(8,128)(2,1)} %merge.1.refs_5_), channel_id=1, source_target_pairs={{0,8},{1,25},{8,16},{9,1},{16,24},{17,9},{24,0},{25,17},{2,10},{3,... | collective-permute-start | bytes 5971976 | tf_op jit(solution)/shard_map/ppermute | solution.py:479
  46.6 3.4 %attend.6 = bf16[272,512]{1,0:T(8,128)(2,1)} custom-call(s32[4]{0:T(128)S(1)} %broadcast_in_dim.39.at, f32[4]{0:T(128)S(1)} %broadcast_multiply_fusion.scale, bf16[256,512]{1,0:T(8,128)(2,1)S(1)} %collective-permute-done.2.q, bf16[4,272,512]{2,1,0:T(8,128)(2,1)S(1)} %all-to-all-done.kv), custom_call_target="tpu_custom_call" | custom-call | tf_op jit(solution)/shard_map/attend/pallas_call | solution.py:188
  51.5 3.4 %attend.5 = bf16[272,512]{1,0:T(8,128)(2,1)} custom-call(s32[4]{0:T(128)S(1)} %broadcast_in_dim.38.at, f32[4]{0:T(128)S(1)} %broadcast_multiply_fusion.scale, bf16[256,512]{1,0:T(8,128)(2,1)S(1)} %collective-permute-done.1.q, bf16[4,272,512]{2,1,0:T(8,128)(2,1)S(1)} %all-to-all-done.kv), custom_call_target="tpu_custom_call" | custom-call | tf_op jit(solution)/shard_map/attend/pallas_call | solution.py:188
  57.2 3.4 %attend.4 = bf16[272,512]{1,0:T(8,128)(2,1)} custom-call(s32[4]{0:T(128)S(1)} %broadcast_in_dim.37.at, f32[4]{0:T(128)S(1)} %broadcast_multiply_fusion.scale, bf16[256,512]{1,0:T(8,128)(2,1)S(1)} %copy-done.9, bf16[4,272,512]{2,1,0:T(8,128)(2,1)S(1)} %all-to-all-done.kv), custom_call_target="tpu_custom_call" | custom-call | tf_op jit(solution)/shard_map/attend/pallas_call | solution.py:188
  65.9 3.8 %collective-permute-done.5.p0 = bf16[272,512]{1,0:T(8,128)(2,1)} collective-permute-done((bf16[272,512]{1,0:T(8,128)(2,1)}, bf16[272,512]{1,0:T(8,128)(2,1)}, u32[]{:S(2)}, u32[]{:S(2)}) %collective-permute-start.5) | collective-permute-done | bytes 278560 | tf_op jit(solution)/shard_map/ppermute | solution.py:463
  69.6 3.2 %collective-permute-start.10 = (bf16[864,1152]{1,0:T(8,128)(2,1)}, bf16[864,1152]{1,0:T(8,128)(2,1)S(1)}, u32[]{:S(2)}, u32[]{:S(2)}) collective-permute-start(bf16[864,1152]{1,0:T(8,128)(2,1)} %merge.1.refs_5_), channel_id=1, source_target_pairs={{0,1},{1,0},{2,3},{3,2},{4,5},{5,4},{6,7},{7,6},{8,9},{9,8},{10,11... | collective-permute-start | bytes 5971976 | tf_op jit(solution)/shard_map/ppermute | solution.py:463
  72.8 3.2 %mix.1 = (f32[128,2304]{1,0:T(8,128)S(1)}, bf16[128,2304]{1,0:T(8,128)(2,1)S(1)}) custom-call(bf16[272,512]{1,0:T(8,128)(2,1)} %collective-permute-done.5.p0, bf16[272,512]{1,0:T(8,128)(2,1)} %collective-permute-done.6.p1, bf16[272,512]{1,0:T(8,128)(2,1)} %collective-permute-done.7.p2, bf16[272,512]{1,0:T(8,128)(2,1)S(1)} %attend.7.p3, ...), custom_call_target="tpu_custom_call" | custom-call | tf_op jit(solution)/shard_map/mix/pallas_call | solution.py:228
  86.7 4.1 %collective-permute-done.12.r2 = bf16[32,2304]{1,0:T(8,128)(2,1)S(1)} collective-permute-done((bf16[32,2304]{1,0:T(8,128)(2,1)S(1)}, bf16[32,2304]{1,0:T(8,128)(2,1)S(1)}, u32[]{:S(2)}, u32[]{:S(2)}) %collective-permute-start.12) | collective-permute-done | bytes 147488 | tf_op jit(solution)/shard_map/ppermute | solution.py:463
  95.4 2.8 %collective-permute-done.18.refs_7_ = bf16[864,1152]{1,0:T(8,128)(2,1)S(1)} collective-permute-done((bf16[864,1152]{1,0:T(8,128)(2,1)}, bf16[864,1152]{1,0:T(8,128)(2,1)S(1)}, u32[]{:S(2)}, u32[]{:S(2)}) %collective-permute-start.18) | collective-permute-done | bytes 1990688 | tf_op jit(solution)/shard_map/ppermute | solution.py:479
  105.8 5.9 %collective-permute-done.19.refs_2_ = bf16[128,2304]{1,0:T(8,128)(2,1)S(1)} collective-permute-done((bf16[128,2304]{1,0:T(8,128)(2,1)S(1)}, bf16[128,2304]{1,0:T(8,128)(2,1)S(1)}, u32[]{:S(2)}, u32[]{:S(2)}) %collective-permute-start.19) | collective-permute-done | bytes 589856 | tf_op jit(solution)/shard_map/ppermute | solution.py:474
  111.7 6.9 %collective-permute-done.20.refs_3_ = bf16[128,2304]{1,0:T(8,128)(2,1)S(1)} collective-permute-done((bf16[128,2304]{1,0:T(8,128)(2,1)S(1)}, bf16[128,2304]{1,0:T(8,128)(2,1)S(1)}, u32[]{:S(2)}, u32[]{:S(2)}) %collective-permute-start.20) | collective-permute-done | bytes 589856 | tf_op jit(solution)/shard_map/ppermute | solution.py:474
  120.8 4.6 %collective-permute-start.24 = (bf16[864,1152]{1,0:T(8,128)(2,1)}, bf16[864,1152]{1,0:T(8,128)(2,1)}, u32[]{:S(2)}, u32[]{:S(2)}) collective-permute-start(bf16[864,1152]{1,0:T(8,128)(2,1)} %collective-permute-done.23.refs_8_), channel_id=1, source_target_pairs={{0,1},{1,0},{2,3},{3,2},{4,5},{5,4},{6,7},{7,6},{8,9},{9,8},{10,11... | collective-permute-start | bytes 5971976 | tf_op jit(solution)/shard_map/ppermute | solution.py:463
  126.0 3.4 %collective-permute-done.24.refs_12_ = bf16[864,1152]{1,0:T(8,128)(2,1)} collective-permute-done((bf16[864,1152]{1,0:T(8,128)(2,1)}, bf16[864,1152]{1,0:T(8,128)(2,1)}, u32[]{:S(2)}, u32[]{:S(2)}) %collective-permute-start.24) | collective-permute-done | bytes 1990688 | tf_op jit(solution)/shard_map/ppermute | solution.py:463
  129.4 16.7 %feed.1 = (bf16[128,2304]{1,0:T(8,128)(2,1)}, bf16[128,2304]{1,0:T(8,128)(2,1)}, bf16[128,2304]{1,0:T(8,128)(2,1)}, bf16[128,2304]{1,0:T(8,128)(2,1)}) custom-call(s32[16]{0:T(128)} %stack.87.refs_0_, bf16[128,2304]{1,0:T(8,128)(2,1)} %copy-done.2, bf16[128,2304]{1,0:T(8,128)(2,1)} %copy-done.16, bf16[128,2304]{1,0:T(8,128)(2,1)} %copy-done.17, ...), custom_call_target="tpu_custom_call" | custom-call | tf_op jit(solution)/shard_map/feed/pallas_call | solution.py:320
  148.4 7.0 %collective-permute-done.25.p1 = bf16[128,2304]{1,0:T(8,128)(2,1)S(1)} collective-permute-done((bf16[128,2304]{1,0:T(8,128)(2,1)}, bf16[128,2304]{1,0:T(8,128)(2,1)S(1)}, u32[]{:S(2)}, u32[]{:S(2)}) %collective-permute-start.25) | collective-permute-done | bytes 589856 | tf_op jit(solution)/shard_map/ppermute | solution.py:474
  157.0 6.3 %collective-permute-done.27.p3 = bf16[128,2304]{1,0:T(8,128)(2,1)S(1)} collective-permute-done((bf16[128,2304]{1,0:T(8,128)(2,1)}, bf16[128,2304]{1,0:T(8,128)(2,1)S(1)}, u32[]{:S(2)}, u32[]{:S(2)}) %collective-permute-start.27) | collective-permute-done | bytes 589856 | tf_op jit(solution)/shard_map/ppermute | solution.py:474
  180.1 4.0 %collective-permute-start.34 = (bf16[128,2304]{1,0:T(8,128)(2,1)S(1)}, bf16[128,2304]{1,0:T(8,128)(2,1)S(1)}, u32[]{:S(2)}, u32[]{:S(2)}) collective-permute-start(bf16[128,2304]{1,0:T(8,128)(2,1)S(1)} %join.3.refs_0_), channel_id=1, source_target_pairs={{0,1},{1,0},{2,3},{3,2},{4,5},{5,4},{6,7},{7,6},{8,9},{9,8},{10,11... | collective-permute-start | bytes 1769480 | tf_op jit(solution)/shard_map/ppermute | solution.py:463
  185.8 3.1 %put_back.1 = bf16[1024,2304]{1,0:T(8,128)(2,1)} custom-call(s32[1]{0:T(128)S(6)} %copy.18.occupied, s32[1,256]{1,0:T(1,128)S(1)} %bitcast.24, bf16[1024,2304]{1,0:T(8,128)(2,1)S(1)} %hold.1.block, bf16[128,2304]{1,0:T(8,128)(2,1)S(1)} %join.3.refs_0_, bf16[128,2304]{1,0:T(8,128)(2,1)S(1)} %collective-permute-done.34.refs_1_), custom_call_target="tpu_custom_call" | custom-call | tf_op jit(solution)/shard_map/put_back/pallas_call | solution.py:448
  (123 shorter events, 64.9 us)
Async XLA Ops:
  2.4 28.9 %collective-permute-start.3 = (bf16[432,1152]{1,0:T(8,128)(2,1)}, bf16[432,1152]{1,0:T(8,128)(2,1)S(1)}, u32[]{:S(2)}, u32[]{:S(2)}) collective-permute-start(bf16[432,1152]{1,0:T(8,128)(2,1)} %get-tuple-element.67), channel_id=1, source_target_pairs={{0,0},{1,64},{32,32},{33,96},{64,1},{65,65},{96,33},{97,97},{2,2},... | collective-permute-start | bytes 2985992 | tf_op jit(solution)/shard_map/ppermute | solution.py:509
  8.6 29.6 %collective-permute-start.4 = (bf16[432,1152]{1,0:T(8,128)(2,1)}, bf16[432,1152]{1,0:T(8,128)(2,1)}, u32[]{:S(2)}, u32[]{:S(2)}) collective-permute-start(bf16[432,1152]{1,0:T(8,128)(2,1)} %get-tuple-element.68), channel_id=1, source_target_pairs={{0,32},{1,96},{32,0},{33,64},{64,33},{65,97},{96,1},{97,65},{2,34}... | collective-permute-start | bytes 2985992 | tf_op jit(solution)/shard_map/ppermute | solution.py:509
  19.9 23.0 %all-to-all-start = ((bf16[4,272,512]{2,1,0:T(8,128)(2,1)}), bf16[4,272,512]{2,1,0:T(8,128)(2,1)S(1)}, u32[]{:S(2)}, u32[]{:S(2)}) async-start(bf16[4,272,512]{2,1,0:T(8,128)(2,1)} %get-tuple-element.65), calls=%async_computation | async-start | bytes 2228224 | tf_op jit(solution)/shard_map/all_to_all | solution.py:512
  25.0 16.0 %collective-permute-start = (bf16[256,512]{1,0:T(8,128)(2,1)S(1)}, bf16[256,512]{1,0:T(8,128)(2,1)S(1)}, u32[]{:S(2)}, u32[]{:S(2)}) collective-permute-start(bf16[256,512]{1,0:T(8,128)(2,1)S(1)} %copy-done.6), channel_id=1, source_target_pairs={{0,32},{32,64},{64,96},{96,0},{1,33},{33,65},{65,97},{97,1},{2,34}... | collective-permute-start | bytes 786440 | tf_op jit(solution)/shard_map/ppermute | solution.py:463
  25.0 17.8 %collective-permute-start.1 = (bf16[256,512]{1,0:T(8,128)(2,1)S(1)}, bf16[256,512]{1,0:T(8,128)(2,1)S(1)}, u32[]{:S(2)}, u32[]{:S(2)}) collective-permute-start(bf16[256,512]{1,0:T(8,128)(2,1)S(1)} %copy-done.6), channel_id=1, source_target_pairs={{0,64},{32,96},{64,0},{96,32},{1,65},{33,97},{65,1},{97,33},{2,66}... | collective-permute-start | bytes 786440 | tf_op jit(solution)/shard_map/ppermute | solution.py:463
  25.3 17.5 %collective-permute-start.2 = (bf16[256,512]{1,0:T(8,128)(2,1)S(1)}, bf16[256,512]{1,0:T(8,128)(2,1)S(1)}, u32[]{:S(2)}, u32[]{:S(2)}) collective-permute-start(bf16[256,512]{1,0:T(8,128)(2,1)S(1)} %copy-done.6), channel_id=1, source_target_pairs={{0,96},{32,0},{64,32},{96,64},{1,97},{33,1},{65,33},{97,65},{2,98}... | collective-permute-start | bytes 786440 | tf_op jit(solution)/shard_map/ppermute | solution.py:463
  42.9 26.8 %collective-permute-start.8 = (bf16[864,1152]{1,0:T(8,128)(2,1)}, bf16[864,1152]{1,0:T(8,128)(2,1)}, u32[]{:S(2)}, u32[]{:S(2)}) collective-permute-start(bf16[864,1152]{1,0:T(8,128)(2,1)} %merge.1.refs_5_), channel_id=1, source_target_pairs={{0,8},{1,25},{8,16},{9,1},{16,24},{17,9},{24,0},{25,17},{2,10},{3,... | collective-permute-start | bytes 5971976 | tf_op jit(solution)/shard_map/ppermute | solution.py:479
  50.0 15.2 %collective-permute-start.7 = (bf16[272,512]{1,0:T(8,128)(2,1)}, bf16[272,512]{1,0:T(8,128)(2,1)}, u32[]{:S(2)}, u32[]{:S(2)}) collective-permute-start(bf16[272,512]{1,0:T(8,128)(2,1)} %attend.6), channel_id=1, source_target_pairs={{0,32},{32,64},{64,96},{96,0},{1,33},{33,65},{65,97},{97,1},{2,34}... | collective-permute-start | bytes 835592 | tf_op jit(solution)/shard_map/ppermute | solution.py:463
  54.9 11.0 %collective-permute-start.6 = (bf16[272,512]{1,0:T(8,128)(2,1)}, bf16[272,512]{1,0:T(8,128)(2,1)}, u32[]{:S(2)}, u32[]{:S(2)}) collective-permute-start(bf16[272,512]{1,0:T(8,128)(2,1)} %attend.5), channel_id=1, source_target_pairs={{0,64},{32,96},{64,0},{96,32},{1,65},{33,97},{65,1},{97,33},{2,66}... | collective-permute-start | bytes 835592 | tf_op jit(solution)/shard_map/ppermute | solution.py:463
  60.6 9.1 %collective-permute-start.5 = (bf16[272,512]{1,0:T(8,128)(2,1)}, bf16[272,512]{1,0:T(8,128)(2,1)}, u32[]{:S(2)}, u32[]{:S(2)}) collective-permute-start(bf16[272,512]{1,0:T(8,128)(2,1)} %attend.4), channel_id=1, source_target_pairs={{0,96},{32,0},{64,32},{96,64},{1,97},{33,1},{65,33},{97,65},{2,98}... | collective-permute-start | bytes 835592 | tf_op jit(solution)/shard_map/ppermute | solution.py:463
  69.6 10.7 %collective-permute-start.10 = (bf16[864,1152]{1,0:T(8,128)(2,1)}, bf16[864,1152]{1,0:T(8,128)(2,1)S(1)}, u32[]{:S(2)}, u32[]{:S(2)}) collective-permute-start(bf16[864,1152]{1,0:T(8,128)(2,1)} %merge.1.refs_5_), channel_id=1, source_target_pairs={{0,1},{1,0},{2,3},{3,2},{4,5},{5,4},{6,7},{7,6},{8,9},{9,8},{10,11... | collective-permute-start | bytes 5971976 | tf_op jit(solution)/shard_map/ppermute | solution.py:463
  72.8 12.5 %collective-permute-start.14 = (bf16[864,1152]{1,0:T(8,128)(2,1)}, bf16[864,1152]{1,0:T(8,128)(2,1)S(1)}, u32[]{:S(2)}, u32[]{:S(2)}) collective-permute-start(bf16[864,1152]{1,0:T(8,128)(2,1)} %collective-permute-done.8.refs_6_), channel_id=1, source_target_pairs={{0,1},{1,0},{2,3},{3,2},{4,5},{5,4},{6,7},{7,6},{8,9},{9,8},{10,11... | collective-permute-start | bytes 5971976 | tf_op jit(solution)/shard_map/ppermute | solution.py:463
  72.8 25.5 %collective-permute-start.18 = (bf16[864,1152]{1,0:T(8,128)(2,1)}, bf16[864,1152]{1,0:T(8,128)(2,1)S(1)}, u32[]{:S(2)}, u32[]{:S(2)}) collective-permute-start(bf16[864,1152]{1,0:T(8,128)(2,1)} %merge.1.refs_5_), channel_id=1, source_target_pairs={{0,24},{1,9},{8,0},{9,17},{16,8},{17,25},{24,16},{25,1},{2,26},{3,... | collective-permute-start | bytes 5971976 | tf_op jit(solution)/shard_map/ppermute | solution.py:479
  81.7 9.2 %collective-permute-start.12 = (bf16[32,2304]{1,0:T(8,128)(2,1)S(1)}, bf16[32,2304]{1,0:T(8,128)(2,1)S(1)}, u32[]{:S(2)}, u32[]{:S(2)}) collective-permute-start(bf16[32,2304]{1,0:T(8,128)(2,1)S(1)} %get-tuple-element.84), channel_id=1, source_target_pairs={{0,4},{2,6},{4,0},{6,2},{1,5},{3,7},{5,1},{7,3},{8,12},{10,14},{12... | collective-permute-start | bytes 442376 | tf_op jit(solution)/shard_map/ppermute | solution.py:463
  91.1 7.2 %collective-permute-start.15 = (bf16[32,2304]{1,0:T(8,128)(2,1)S(1)}, bf16[32,2304]{1,0:T(8,128)(2,1)S(1)}, u32[]{:S(2)}, u32[]{:S(2)}) collective-permute-start(bf16[32,2304]{1,0:T(8,128)(2,1)S(1)} %get-tuple-element.91.refs_0_), channel_id=1, source_target_pairs={{0,2},{1,33},{2,4},{3,35},{4,6},{5,37},{6,0},{7,39},{32,34},{33,65... | collective-permute-start | bytes 442376 | tf_op jit(solution)/shard_map/ppermute | solution.py:474
  93.8 25.6 %collective-permute-start.23 = (bf16[864,1152]{1,0:T(8,128)(2,1)}, bf16[864,1152]{1,0:T(8,128)(2,1)}, u32[]{:S(2)}, u32[]{:S(2)}) collective-permute-start(bf16[864,1152]{1,0:T(8,128)(2,1)} %collective-permute-done.8.refs_6_), channel_id=1, source_target_pairs={{0,8},{1,25},{8,16},{9,1},{16,24},{17,9},{24,0},{25,17},{2,10},{3,... | collective-permute-start | bytes 5971976 | tf_op jit(solution)/shard_map/ppermute | solution.py:479
  98.9 20.6 %collective-permute-start.22 = (bf16[864,1152]{1,0:T(8,128)(2,1)S(1)}, bf16[864,1152]{1,0:T(8,128)(2,1)S(1)}, u32[]{:S(2)}, u32[]{:S(2)}) collective-permute-start(bf16[864,1152]{1,0:T(8,128)(2,1)S(1)} %collective-permute-done.18.refs_7_), channel_id=1, source_target_pairs={{0,1},{1,0},{2,3},{3,2},{4,5},{5,4},{6,7},{7,6},{8,9},{9,8},{10,11... | collective-permute-start | bytes 5971976 | tf_op jit(solution)/shard_map/ppermute | solution.py:463
  101.3 10.4 %collective-permute-start.19 = (bf16[128,2304]{1,0:T(8,128)(2,1)S(1)}, bf16[128,2304]{1,0:T(8,128)(2,1)S(1)}, u32[]{:S(2)}, u32[]{:S(2)}) collective-permute-start(bf16[128,2304]{1,0:T(8,128)(2,1)S(1)} %join.2.refs_1_), channel_id=1, source_target_pairs={{0,32},{1,3},{2,34},{3,5},{4,36},{5,7},{6,38},{7,1},{32,64},{33,35... | collective-permute-start | bytes 1769480 | tf_op jit(solution)/shard_map/ppermute | solution.py:474
  103.0 15.6 %collective-permute-start.20 = (bf16[128,2304]{1,0:T(8,128)(2,1)S(1)}, bf16[128,2304]{1,0:T(8,128)(2,1)S(1)}, u32[]{:S(2)}, u32[]{:S(2)}) collective-permute-start(bf16[128,2304]{1,0:T(8,128)(2,1)S(1)} %join.2.refs_1_), channel_id=1, source_target_pairs={{0,64},{1,5},{2,66},{3,7},{4,68},{5,1},{6,70},{7,3},{32,96},{33,37... | collective-permute-start | bytes 1769480 | tf_op jit(solution)/shard_map/ppermute | solution.py:474
  105.0 13.6 %collective-permute-start.21 = (bf16[128,2304]{1,0:T(8,128)(2,1)S(1)}, bf16[128,2304]{1,0:T(8,128)(2,1)S(1)}, u32[]{:S(2)}, u32[]{:S(2)}) collective-permute-start(bf16[128,2304]{1,0:T(8,128)(2,1)S(1)} %join.2.refs_1_), channel_id=1, source_target_pairs={{0,96},{1,7},{2,98},{3,1},{4,100},{5,3},{6,102},{7,5},{32,0},{33,3... | collective-permute-start | bytes 1769480 | tf_op jit(solution)/shard_map/ppermute | solution.py:474
  120.8 8.6 %collective-permute-start.24 = (bf16[864,1152]{1,0:T(8,128)(2,1)}, bf16[864,1152]{1,0:T(8,128)(2,1)}, u32[]{:S(2)}, u32[]{:S(2)}) collective-permute-start(bf16[864,1152]{1,0:T(8,128)(2,1)} %collective-permute-done.23.refs_8_), channel_id=1, source_target_pairs={{0,1},{1,0},{2,3},{3,2},{4,5},{5,4},{6,7},{7,6},{8,9},{9,8},{10,11... | collective-permute-start | bytes 5971976 | tf_op jit(solution)/shard_map/ppermute | solution.py:463
  146.1 9.3 %collective-permute-start.25 = (bf16[128,2304]{1,0:T(8,128)(2,1)}, bf16[128,2304]{1,0:T(8,128)(2,1)S(1)}, u32[]{:S(2)}, u32[]{:S(2)}) collective-permute-start(bf16[128,2304]{1,0:T(8,128)(2,1)} %get-tuple-element.106), channel_id=1, source_target_pairs={{0,96},{1,7},{2,98},{3,1},{4,100},{5,3},{6,102},{7,5},{32,0},{33,3... | collective-permute-start | bytes 1769480 | tf_op jit(solution)/shard_map/ppermute | solution.py:474
  146.1 10.9 %collective-permute-start.26 = (bf16[128,2304]{1,0:T(8,128)(2,1)}, bf16[128,2304]{1,0:T(8,128)(2,1)S(1)}, u32[]{:S(2)}, u32[]{:S(2)}) collective-permute-start(bf16[128,2304]{1,0:T(8,128)(2,1)} %get-tuple-element.107), channel_id=1, source_target_pairs={{0,64},{1,5},{2,66},{3,7},{4,68},{5,1},{6,70},{7,3},{32,96},{33,37... | collective-permute-start | bytes 1769480 | tf_op jit(solution)/shard_map/ppermute | solution.py:474
  148.1 15.2 %collective-permute-start.27 = (bf16[128,2304]{1,0:T(8,128)(2,1)}, bf16[128,2304]{1,0:T(8,128)(2,1)S(1)}, u32[]{:S(2)}, u32[]{:S(2)}) collective-permute-start(bf16[128,2304]{1,0:T(8,128)(2,1)} %get-tuple-element.108), channel_id=1, source_target_pairs={{0,32},{1,3},{2,34},{3,5},{4,36},{5,7},{6,38},{7,1},{32,64},{33,35... | collective-permute-start | bytes 1769480 | tf_op jit(solution)/shard_map/ppermute | solution.py:474
  (35 other events, 444.6 us)

commit v5 on v4

--- a/solution.py
+++ b/solution.py
@@ -275,11 +275,17 @@
 
 
 def feed_body(*refs):
-    place = refs[0]
-    xs = refs[1:5]
-    pieces = refs[5:13]
-    outs = refs[13:17]
-    tokens, gate, up, down, hidden, acted, sems = refs[17:]
+    xs = refs[0:4]
+    pieces = refs[4:12]
+    outs = refs[12:16]
+    tokens, gate, up, down, hidden, acted, sems = refs[16:]
+    y, z, c = (lax.axis_index(n) for n in ("y", "z", "c"))
+    near = 3 - 2 * c
+    place = []
+    for core, step in ((c, near), (1 - c, 4 - near)):
+        for source in (z, z + step, z + 4 - step, z + 2):
+            for s in range(2):
+                place.append(4 * (2 * core + lax.rem(y + s, 2)) + lax.rem(source, 4))
     copies = [[], [], []]
     for e, x in enumerate(xs):
         copies[0].append(pltpu.make_async_copy(x, tokens.at[e * 128:(e + 1) * 128, :], sems.at[e]))
@@ -316,18 +322,18 @@
             out[:, rows] = part[e * 128:(e + 1) * 128, :]
 
 
-def feed(place, xs, pieces):
+def feed(xs, pieces):
     return pl.pallas_call(
         feed_body,
         out_shape=(jax.ShapeDtypeStruct((4 * OWN, D), BF16),) * 4,
-        in_specs=[smem_spec()] + [hbm_spec()] * 12,
+        in_specs=[hbm_spec()] * 12,
         out_specs=(vmem_spec(),) * 4,
         scratch_shapes=[pltpu.VMEM((512, D), BF16), pltpu.VMEM((D, FF_DEV), BF16), pltpu.VMEM((D, FF_DEV), BF16),
                         pltpu.VMEM((D, FF_DEV), BF16), pltpu.VMEM((512, FF_DEV), BF16), pltpu.VMEM((512, FF_DEV), F32),
                         pltpu.SemaphoreType.DMA((52,))],
         compiler_params=params(60),
         name="feed",
-    )(place, *xs, *pieces)
+    )(*xs, *pieces)
 
 
 def fold_body(p0, p1, p2, p3, own, s1, s2, s3):
@@ -494,14 +500,6 @@
 def local(block, preference, chosen, occupied, gain1, wq, wk, wv, wo, sharpness, gain2, gate_w, up_w, down_w):
     y, z, x, c = (lax.axis_index(n) for n in ("y", "z", "x", "c"))
     own_at = c * 128 + x * OWN
-    near = 3 - 2 * c
-    place = []
-    for core, step in ((c, near), (1 - c, 4 - near)):
-        for source in (z, z + step, z + 4 - step, z + 2):
-            for s in range(2):
-                place.append(4 * (2 * core + (y + s) % 2) + source % 4)
-    place = jnp.stack(place).astype(jnp.int32)
-
     frequency = 10000.0 ** (-(np.arange(HD) % (HD // 2)) / (HD // 2))
     frequency = jnp.asarray(frequency.astype(np.float32)[None, :])
     packs = pack(gate_w, up_w, down_w)
@@ -524,14 +522,13 @@
     parts.append(attend(True, at, scale, q, kv))
 
     *parts, near, merged = tie(*parts, near, merged)
-    side = around(merged, 3)
+    side, far = around(merged, 3), around(near, 1)
     keep, send = mix(parts, wo)
     others = [swap(piece) for piece in (merged, near, side)]
     met, others[0] = tie(swap(send), others[0])
     own, s1, s2, s3 = split(keep, met)
     moved = [shift(s, "x", d) for d, s in ((1, s1), (2, s2), (3, s3))]
-    *moved, others[1], near = tie(*moved, others[1], near)
-    far = around(near, 1)
+    *moved, others[1] = tie(*moved, others[1])
     attention, normed = middle(picked, own, moved, gain2[None, :])
 
     moved = [cross(normed, d, True) for d in (1, 2, 3)]
@@ -541,7 +538,7 @@
     xs = [row] + [cross(row, e, False) for e in (1, 2, 3)]
     *xs, others[2], far = tie(*xs, others[2], far)
     others.append(swap(far))
-    outs = feed(place, xs, [merged, near, side, far] + others)
+    outs = feed(xs, [merged, near, side, far] + others)
     own, s1, s2, s3 = fold([outs[0]] + [cross(outs[e], 4 - e, False) for e in (1, 2, 3)])
     outs = [own] + [cross(s, 4 - d, True) for d, s in ((1, s1), (2, s2), (3, s3))]
 

time: 189 us -> 187 us (0.989)
    ppermute x12, waiting for transfers between devices: 34.3 us -> 21.5 us  [cross(): return lax.ppermute(value, ('y', 'x', 'c'), pairs)]
    ppermute x3, waiting for transfers between devices: 3.64 us -> 16.3 us  [around(): return lax.ppermute(value, ('z', 'c'), pairs)]
    unnamed x46 -> x48, local copies, waits for them, and re-layouts: 6.42 us -> 5.16 us
  transfers between devices with their start and end apart: 36 -> 36, of which waited for: 23 -> 21; matrix products, arithmetic and copies ran while one was open for 1% -> 1% of each run, Pallas kernels for 15% -> 16%
where the time goes in v5:
time: 187 us
  waiting for transfers between devices  67.8 us (36%)
  starting transfers between devices  60.9 us (33%)
  Pallas kernels  51 us (27%)
  local copies, waits for them, and re-layouts  5.94 us (3%)
    ppermute x18, starting transfers between devices, shift(): lax.ppermute(value, axis, [(i, (i + step) % size) for i in range(size)])  32.8 us
    ppermute x12, waiting for transfers between devices, cross(): return lax.ppermute(value, ('y', 'x', 'c'), pairs)  21.5 us
    ppermute x18, waiting for transfers between devices, shift(): lax.ppermute(value, axis, [(i, (i + step) % size) for i in range(size)])  19.6 us
    ppermute x3, waiting for transfers between devices, around(): return lax.ppermute(value, ('z', 'c'), pairs)  16.3 us
    pallas_call x1, Pallas kernels, feed(): pl.pallas_call(feed_body, out_shape=(jax.ShapeDtypeStruct((4 * OWN, D), B...  15.9 us
    pallas_call x4, Pallas kernels, attend(): pl.pallas_call(functools.partial(attend_body, diagonal), out_shape=jax.Sh...  13 us
    ppermute x12, starting transfers between devices, cross(): return lax.ppermute(value, ('y', 'x', 'c'), pairs)  10.8 us
    ppermute x2, waiting for transfers between devices, local(): lax.ppermute(p, ('y', 'c'), weight_pairs(s))  10.5 us
  transfers between devices with their start and end apart: 36, of which 21 were waited for; matrix products, arithmetic and copies ran while one was open for 1% of the time, Pallas kernels for 16%

profile of v5, /device:TPU:1, one launch (start us, length us, event | category | flops | bytes accessed | tf_op | source)
XLA Modules:
  0.0 186.9 jit_solution(16242568219392730215)
XLA Ops:
  2.4 6.2 %collective-permute-start.3 = (bf16[432,1152]{1,0:T(8,128)(2,1)}, bf16[432,1152]{1,0:T(8,128)(2,1)S(1)}, u32[]{:S(2)}, u32[]{:S(2)}) collective-permute-start(bf16[432,1152]{1,0:T(8,128)(2,1)} %get-tuple-element.66), channel_id=1, source_target_pairs={{0,0},{1,64},{32,32},{33,96},{64,1},{65,65},{96,33},{97,97},{2,2},... | collective-permute-start | bytes 2985992 | tf_op jit(solution)/shard_map/ppermute | solution.py:507
  10.4 9.4 %begin.1 = (bf16[256,512]{1,0:T(8,128)(2,1)}, bf16[4,272,512]{2,1,0:T(8,128)(2,1)}, bf16[32,2304]{1,0:T(8,128)(2,1)}) custom-call(s32[1]{0:T(128)S(6)} %copy.18.occupied, bf16[1024,2304]{1,0:T(8,128)(2,1)} %block.1, s32[1,256]{1,0:T(1,128)} %bitcast.7, f32[1,2304]{1,0:T(1,128)} %broadcast_in_dim.36.gain, f32[1,128]{1,0:T(1,128)} %constant.64.clone.frequency, ...), custom_call_target="tpu_custom_call" | custom-call | tf_op jit(solution)/shard_map/begin/pallas_call | solution.py:103
  19.9 5.2 %all-to-all-start = ((bf16[4,272,512]{2,1,0:T(8,128)(2,1)}), bf16[4,272,512]{2,1,0:T(8,128)(2,1)S(1)}, u32[]{:S(2)}, u32[]{:S(2)}) async-start(bf16[4,272,512]{2,1,0:T(8,128)(2,1)} %get-tuple-element.64), calls=%async_computation | async-start | bytes 2228224 | tf_op jit(solution)/shard_map/all_to_all | solution.py:510
  27.7 3.5 %collective-permute-done.3.first = bf16[432,1152]{1,0:T(8,128)(2,1)S(1)} collective-permute-done((bf16[432,1152]{1,0:T(8,128)(2,1)}, bf16[432,1152]{1,0:T(8,128)(2,1)S(1)}, u32[]{:S(2)}, u32[]{:S(2)}) %collective-permute-start.3) | collective-permute-done | bytes 995360 | tf_op jit(solution)/shard_map/ppermute | solution.py:507
  31.3 6.9 %collective-permute-done.4.second = bf16[432,1152]{1,0:T(8,128)(2,1)} collective-permute-done((bf16[432,1152]{1,0:T(8,128)(2,1)}, bf16[432,1152]{1,0:T(8,128)(2,1)}, u32[]{:S(2)}, u32[]{:S(2)}) %collective-permute-start.4) | collective-permute-done | bytes 995360 | tf_op jit(solution)/shard_map/ppermute | solution.py:507
  38.2 2.8 %merge.1.refs_4_ = bf16[864,1152]{1,0:T(8,128)(2,1)} custom-call(bf16[432,1152]{1,0:T(8,128)(2,1)} %copy-done.16, bf16[432,1152]{1,0:T(8,128)(2,1)} %collective-permute-done.4.second), custom_call_target="tpu_custom_call" | custom-call | tf_op jit(solution)/shard_map/merge/pallas_call | solution.py:385
  42.9 3.8 %collective-permute-start.8 = (bf16[864,1152]{1,0:T(8,128)(2,1)}, bf16[864,1152]{1,0:T(8,128)(2,1)}, u32[]{:S(2)}, u32[]{:S(2)}) collective-permute-start(bf16[864,1152]{1,0:T(8,128)(2,1)} %merge.1.refs_4_), channel_id=1, source_target_pairs={{0,8},{1,25},{8,16},{9,1},{16,24},{17,9},{24,0},{25,17},{2,10},{3,... | collective-permute-start | bytes 5971976 | tf_op jit(solution)/shard_map/ppermute | solution.py:485
  46.6 3.4 %attend.6 = bf16[272,512]{1,0:T(8,128)(2,1)} custom-call(s32[4]{0:T(128)S(1)} %broadcast_in_dim.39.at, f32[4]{0:T(128)S(1)} %broadcast_multiply_fusion.scale, bf16[256,512]{1,0:T(8,128)(2,1)S(1)} %collective-permute-done.2.q, bf16[4,272,512]{2,1,0:T(8,128)(2,1)S(1)} %all-to-all-done.kv), custom_call_target="tpu_custom_call" | custom-call | tf_op jit(solution)/shard_map/attend/pallas_call | solution.py:188
  51.5 3.4 %attend.5 = bf16[272,512]{1,0:T(8,128)(2,1)} custom-call(s32[4]{0:T(128)S(1)} %broadcast_in_dim.38.at, f32[4]{0:T(128)S(1)} %broadcast_multiply_fusion.scale, bf16[256,512]{1,0:T(8,128)(2,1)S(1)} %collective-permute-done.1.q, bf16[4,272,512]{2,1,0:T(8,128)(2,1)S(1)} %all-to-all-done.kv), custom_call_target="tpu_custom_call" | custom-call | tf_op jit(solution)/shard_map/attend/pallas_call | solution.py:188
  57.1 3.4 %attend.4 = bf16[272,512]{1,0:T(8,128)(2,1)} custom-call(s32[4]{0:T(128)S(1)} %broadcast_in_dim.37.at, f32[4]{0:T(128)S(1)} %broadcast_multiply_fusion.scale, bf16[256,512]{1,0:T(8,128)(2,1)S(1)} %copy-done.9, bf16[4,272,512]{2,1,0:T(8,128)(2,1)S(1)} %all-to-all-done.kv), custom_call_target="tpu_custom_call" | custom-call | tf_op jit(solution)/shard_map/attend/pallas_call | solution.py:188
  62.5 2.8 %attend.7.p3 = bf16[272,512]{1,0:T(8,128)(2,1)S(1)} custom-call(s32[4]{0:T(128)S(1)} %pad_add_fusion.at, f32[4]{0:T(128)S(1)} %broadcast_multiply_fusion.scale, bf16[256,512]{1,0:T(8,128)(2,1)S(1)} %copy-done.7, bf16[4,272,512]{2,1,0:T(8,128)(2,1)S(1)} %all-to-all-done.kv), custom_call_target="tpu_custom_call" | custom-call | tf_op jit(solution)/shard_map/attend/pallas_call | solution.py:188
  65.9 3.8 %collective-permute-done.5.p0 = bf16[272,512]{1,0:T(8,128)(2,1)} collective-permute-done((bf16[272,512]{1,0:T(8,128)(2,1)}, bf16[272,512]{1,0:T(8,128)(2,1)}, u32[]{:S(2)}, u32[]{:S(2)}) %collective-permute-start.5) | collective-permute-done | bytes 278560 | tf_op jit(solution)/shard_map/ppermute | solution.py:469
  69.6 3.2 %collective-permute-start.10 = (bf16[864,1152]{1,0:T(8,128)(2,1)}, bf16[864,1152]{1,0:T(8,128)(2,1)S(1)}, u32[]{:S(2)}, u32[]{:S(2)}) collective-permute-start(bf16[864,1152]{1,0:T(8,128)(2,1)} %merge.1.refs_4_), channel_id=1, source_target_pairs={{0,1},{1,0},{2,3},{3,2},{4,5},{5,4},{6,7},{7,6},{8,9},{9,8},{10,11... | collective-permute-start | bytes 5971976 | tf_op jit(solution)/shard_map/ppermute | solution.py:469
  72.8 3.2 %mix.1 = (f32[128,2304]{1,0:T(8,128)S(1)}, bf16[128,2304]{1,0:T(8,128)(2,1)S(1)}) custom-call(bf16[272,512]{1,0:T(8,128)(2,1)} %collective-permute-done.5.p0, bf16[272,512]{1,0:T(8,128)(2,1)} %collective-permute-done.6.p1, bf16[272,512]{1,0:T(8,128)(2,1)} %collective-permute-done.7.p2, bf16[272,512]{1,0:T(8,128)(2,1)S(1)} %attend.7.p3, ...), custom_call_target="tpu_custom_call" | custom-call | tf_op jit(solution)/shard_map/mix/pallas_call | solution.py:228
  86.8 4.1 %collective-permute-done.12.r2 = bf16[32,2304]{1,0:T(8,128)(2,1)S(1)} collective-permute-done((bf16[32,2304]{1,0:T(8,128)(2,1)S(1)}, bf16[32,2304]{1,0:T(8,128)(2,1)S(1)}, u32[]{:S(2)}, u32[]{:S(2)}) %collective-permute-start.12) | collective-permute-done | bytes 147488 | tf_op jit(solution)/shard_map/ppermute | solution.py:469
  95.5 2.8 %collective-permute-done.18.refs_6_ = bf16[864,1152]{1,0:T(8,128)(2,1)S(1)} collective-permute-done((bf16[864,1152]{1,0:T(8,128)(2,1)}, bf16[864,1152]{1,0:T(8,128)(2,1)S(1)}, u32[]{:S(2)}, u32[]{:S(2)}) %collective-permute-start.18) | collective-permute-done | bytes 1990688 | tf_op jit(solution)/shard_map/ppermute | solution.py:485
  105.8 13.5 %collective-permute-done.23.refs_7_ = bf16[864,1152]{1,0:T(8,128)(2,1)S(1)} collective-permute-done((bf16[864,1152]{1,0:T(8,128)(2,1)}, bf16[864,1152]{1,0:T(8,128)(2,1)S(1)}, u32[]{:S(2)}, u32[]{:S(2)}) %collective-permute-start.23) | collective-permute-done | bytes 1990688 | tf_op jit(solution)/shard_map/ppermute | solution.py:485
  119.4 4.9 %collective-permute-start.24 = (bf16[864,1152]{1,0:T(8,128)(2,1)S(1)}, bf16[864,1152]{1,0:T(8,128)(2,1)}, u32[]{:S(2)}, u32[]{:S(2)}) collective-permute-start(bf16[864,1152]{1,0:T(8,128)(2,1)S(1)} %collective-permute-done.23.refs_7_), channel_id=1, source_target_pairs={{0,1},{1,0},{2,3},{3,2},{4,5},{5,4},{6,7},{7,6},{8,9},{9,8},{10,11... | collective-permute-start | bytes 5971976 | tf_op jit(solution)/shard_map/ppermute | solution.py:469
  124.4 3.7 %collective-permute-done.24.refs_11_ = bf16[864,1152]{1,0:T(8,128)(2,1)} collective-permute-done((bf16[864,1152]{1,0:T(8,128)(2,1)S(1)}, bf16[864,1152]{1,0:T(8,128)(2,1)}, u32[]{:S(2)}, u32[]{:S(2)}) %collective-permute-start.24) | collective-permute-done | bytes 1990688 | tf_op jit(solution)/shard_map/ppermute | solution.py:469
  128.2 15.9 %feed.1 = (bf16[128,2304]{1,0:T(8,128)(2,1)}, bf16[128,2304]{1,0:T(8,128)(2,1)}, bf16[128,2304]{1,0:T(8,128)(2,1)}, bf16[128,2304]{1,0:T(8,128)(2,1)}) custom-call(bf16[128,2304]{1,0:T(8,128)(2,1)} %copy-done.1, bf16[128,2304]{1,0:T(8,128)(2,1)} %copy-done.17, bf16[128,2304]{1,0:T(8,128)(2,1)} %copy-done.18, bf16[128,2304]{1,0:T(8,128)(2,1)} %copy-done.19, ...), custom_call_target="tpu_custom_call" | custom-call | tf_op jit(solution)/shard_map/feed/pallas_call | solution.py:326
  146.4 7.0 %collective-permute-done.25.p1 = bf16[128,2304]{1,0:T(8,128)(2,1)S(1)} collective-permute-done((bf16[128,2304]{1,0:T(8,128)(2,1)}, bf16[128,2304]{1,0:T(8,128)(2,1)S(1)}, u32[]{:S(2)}, u32[]{:S(2)}) %collective-permute-start.25) | collective-permute-done | bytes 589856 | tf_op jit(solution)/shard_map/ppermute | solution.py:480
  155.0 6.3 %collective-permute-done.27.p3 = bf16[128,2304]{1,0:T(8,128)(2,1)S(1)} collective-permute-done((bf16[128,2304]{1,0:T(8,128)(2,1)}, bf16[128,2304]{1,0:T(8,128)(2,1)S(1)}, u32[]{:S(2)}, u32[]{:S(2)}) %collective-permute-start.27) | collective-permute-done | bytes 589856 | tf_op jit(solution)/shard_map/ppermute | solution.py:480
  178.2 4.0 %collective-permute-start.34 = (bf16[128,2304]{1,0:T(8,128)(2,1)S(1)}, bf16[128,2304]{1,0:T(8,128)(2,1)S(1)}, u32[]{:S(2)}, u32[]{:S(2)}) collective-permute-start(bf16[128,2304]{1,0:T(8,128)(2,1)S(1)} %join.3.refs_0_), channel_id=1, source_target_pairs={{0,1},{1,0},{2,3},{3,2},{4,5},{5,4},{6,7},{7,6},{8,9},{9,8},{10,11... | collective-permute-start | bytes 1769480 | tf_op jit(solution)/shard_map/ppermute | solution.py:469
  183.8 3.1 %put_back.1 = bf16[1024,2304]{1,0:T(8,128)(2,1)} custom-call(s32[1]{0:T(128)S(6)} %copy.18.occupied, s32[1,256]{1,0:T(1,128)S(1)} %bitcast.8, bf16[1024,2304]{1,0:T(8,128)(2,1)S(1)} %hold.1.block, bf16[128,2304]{1,0:T(8,128)(2,1)S(1)} %join.3.refs_0_, bf16[128,2304]{1,0:T(8,128)(2,1)S(1)} %collective-permute-done.34.refs_1_), custom_call_target="tpu_custom_call" | custom-call | tf_op jit(solution)/shard_map/put_back/pallas_call | solution.py:454
  (124 shorter events, 59.6 us)
Async XLA Ops:
  2.4 28.9 %collective-permute-start.3 = (bf16[432,1152]{1,0:T(8,128)(2,1)}, bf16[432,1152]{1,0:T(8,128)(2,1)S(1)}, u32[]{:S(2)}, u32[]{:S(2)}) collective-permute-start(bf16[432,1152]{1,0:T(8,128)(2,1)} %get-tuple-element.66), channel_id=1, source_target_pairs={{0,0},{1,64},{32,32},{33,96},{64,1},{65,65},{96,33},{97,97},{2,2},... | collective-permute-start | bytes 2985992 | tf_op jit(solution)/shard_map/ppermute | solution.py:507
  8.6 29.6 %collective-permute-start.4 = (bf16[432,1152]{1,0:T(8,128)(2,1)}, bf16[432,1152]{1,0:T(8,128)(2,1)}, u32[]{:S(2)}, u32[]{:S(2)}) collective-permute-start(bf16[432,1152]{1,0:T(8,128)(2,1)} %get-tuple-element.67), channel_id=1, source_target_pairs={{0,32},{1,96},{32,0},{33,64},{64,33},{65,97},{96,1},{97,65},{2,34}... | collective-permute-start | bytes 2985992 | tf_op jit(solution)/shard_map/ppermute | solution.py:507
  19.9 23.0 %all-to-all-start = ((bf16[4,272,512]{2,1,0:T(8,128)(2,1)}), bf16[4,272,512]{2,1,0:T(8,128)(2,1)S(1)}, u32[]{:S(2)}, u32[]{:S(2)}) async-start(bf16[4,272,512]{2,1,0:T(8,128)(2,1)} %get-tuple-element.64), calls=%async_computation | async-start | bytes 2228224 | tf_op jit(solution)/shard_map/all_to_all | solution.py:510
  25.0 16.0 %collective-permute-start = (bf16[256,512]{1,0:T(8,128)(2,1)S(1)}, bf16[256,512]{1,0:T(8,128)(2,1)S(1)}, u32[]{:S(2)}, u32[]{:S(2)}) collective-permute-start(bf16[256,512]{1,0:T(8,128)(2,1)S(1)} %copy-done.6), channel_id=1, source_target_pairs={{0,32},{32,64},{64,96},{96,0},{1,33},{33,65},{65,97},{97,1},{2,34}... | collective-permute-start | bytes 786440 | tf_op jit(solution)/shard_map/ppermute | solution.py:469
  25.1 17.8 %collective-permute-start.1 = (bf16[256,512]{1,0:T(8,128)(2,1)S(1)}, bf16[256,512]{1,0:T(8,128)(2,1)S(1)}, u32[]{:S(2)}, u32[]{:S(2)}) collective-permute-start(bf16[256,512]{1,0:T(8,128)(2,1)S(1)} %copy-done.6), channel_id=1, source_target_pairs={{0,64},{32,96},{64,0},{96,32},{1,65},{33,97},{65,1},{97,33},{2,66}... | collective-permute-start | bytes 786440 | tf_op jit(solution)/shard_map/ppermute | solution.py:469
  25.3 17.5 %collective-permute-start.2 = (bf16[256,512]{1,0:T(8,128)(2,1)S(1)}, bf16[256,512]{1,0:T(8,128)(2,1)S(1)}, u32[]{:S(2)}, u32[]{:S(2)}) collective-permute-start(bf16[256,512]{1,0:T(8,128)(2,1)S(1)} %copy-done.6), channel_id=1, source_target_pairs={{0,96},{32,0},{64,32},{96,64},{1,97},{33,1},{65,33},{97,65},{2,98}... | collective-permute-start | bytes 786440 | tf_op jit(solution)/shard_map/ppermute | solution.py:469
  42.9 26.8 %collective-permute-start.8 = (bf16[864,1152]{1,0:T(8,128)(2,1)}, bf16[864,1152]{1,0:T(8,128)(2,1)}, u32[]{:S(2)}, u32[]{:S(2)}) collective-permute-start(bf16[864,1152]{1,0:T(8,128)(2,1)} %merge.1.refs_4_), channel_id=1, source_target_pairs={{0,8},{1,25},{8,16},{9,1},{16,24},{17,9},{24,0},{25,17},{2,10},{3,... | collective-permute-start | bytes 5971976 | tf_op jit(solution)/shard_map/ppermute | solution.py:485
  50.0 15.3 %collective-permute-start.7 = (bf16[272,512]{1,0:T(8,128)(2,1)}, bf16[272,512]{1,0:T(8,128)(2,1)}, u32[]{:S(2)}, u32[]{:S(2)}) collective-permute-start(bf16[272,512]{1,0:T(8,128)(2,1)} %attend.6), channel_id=1, source_target_pairs={{0,32},{32,64},{64,96},{96,0},{1,33},{33,65},{65,97},{97,1},{2,34}... | collective-permute-start | bytes 835592 | tf_op jit(solution)/shard_map/ppermute | solution.py:469
  54.9 11.0 %collective-permute-start.6 = (bf16[272,512]{1,0:T(8,128)(2,1)}, bf16[272,512]{1,0:T(8,128)(2,1)}, u32[]{:S(2)}, u32[]{:S(2)}) collective-permute-start(bf16[272,512]{1,0:T(8,128)(2,1)} %attend.5), channel_id=1, source_target_pairs={{0,64},{32,96},{64,0},{96,32},{1,65},{33,97},{65,1},{97,33},{2,66}... | collective-permute-start | bytes 835592 | tf_op jit(solution)/shard_map/ppermute | solution.py:469
  60.6 9.1 %collective-permute-start.5 = (bf16[272,512]{1,0:T(8,128)(2,1)}, bf16[272,512]{1,0:T(8,128)(2,1)}, u32[]{:S(2)}, u32[]{:S(2)}) collective-permute-start(bf16[272,512]{1,0:T(8,128)(2,1)} %attend.4), channel_id=1, source_target_pairs={{0,96},{32,0},{64,32},{96,64},{1,97},{33,1},{65,33},{97,65},{2,98}... | collective-permute-start | bytes 835592 | tf_op jit(solution)/shard_map/ppermute | solution.py:469
  69.6 10.7 %collective-permute-start.10 = (bf16[864,1152]{1,0:T(8,128)(2,1)}, bf16[864,1152]{1,0:T(8,128)(2,1)S(1)}, u32[]{:S(2)}, u32[]{:S(2)}) collective-permute-start(bf16[864,1152]{1,0:T(8,128)(2,1)} %merge.1.refs_4_), channel_id=1, source_target_pairs={{0,1},{1,0},{2,3},{3,2},{4,5},{5,4},{6,7},{7,6},{8,9},{9,8},{10,11... | collective-permute-start | bytes 5971976 | tf_op jit(solution)/shard_map/ppermute | solution.py:469
  72.8 12.5 %collective-permute-start.14 = (bf16[864,1152]{1,0:T(8,128)(2,1)}, bf16[864,1152]{1,0:T(8,128)(2,1)S(1)}, u32[]{:S(2)}, u32[]{:S(2)}) collective-permute-start(bf16[864,1152]{1,0:T(8,128)(2,1)} %collective-permute-done.8.refs_5_), channel_id=1, source_target_pairs={{0,1},{1,0},{2,3},{3,2},{4,5},{5,4},{6,7},{7,6},{8,9},{9,8},{10,11... | collective-permute-start | bytes 5971976 | tf_op jit(solution)/shard_map/ppermute | solution.py:469
  72.8 25.5 %collective-permute-start.18 = (bf16[864,1152]{1,0:T(8,128)(2,1)}, bf16[864,1152]{1,0:T(8,128)(2,1)S(1)}, u32[]{:S(2)}, u32[]{:S(2)}) collective-permute-start(bf16[864,1152]{1,0:T(8,128)(2,1)} %merge.1.refs_4_), channel_id=1, source_target_pairs={{0,24},{1,9},{8,0},{9,17},{16,8},{17,25},{24,16},{25,1},{2,26},{3,... | collective-permute-start | bytes 5971976 | tf_op jit(solution)/shard_map/ppermute | solution.py:485
  81.7 9.2 %collective-permute-start.12 = (bf16[32,2304]{1,0:T(8,128)(2,1)S(1)}, bf16[32,2304]{1,0:T(8,128)(2,1)S(1)}, u32[]{:S(2)}, u32[]{:S(2)}) collective-permute-start(bf16[32,2304]{1,0:T(8,128)(2,1)S(1)} %get-tuple-element.83), channel_id=1, source_target_pairs={{0,4},{2,6},{4,0},{6,2},{1,5},{3,7},{5,1},{7,3},{8,12},{10,14},{12... | collective-permute-start | bytes 442376 | tf_op jit(solution)/shard_map/ppermute | solution.py:469
  91.1 7.1 %collective-permute-start.15 = (bf16[32,2304]{1,0:T(8,128)(2,1)S(1)}, bf16[32,2304]{1,0:T(8,128)(2,1)S(1)}, u32[]{:S(2)}, u32[]{:S(2)}) collective-permute-start(bf16[32,2304]{1,0:T(8,128)(2,1)S(1)} %get-tuple-element.90.refs_0_), channel_id=1, source_target_pairs={{0,2},{1,33},{2,4},{3,35},{4,6},{5,37},{6,0},{7,39},{32,34},{33,65... | collective-permute-start | bytes 442376 | tf_op jit(solution)/shard_map/ppermute | solution.py:480
  93.9 25.5 %collective-permute-start.23 = (bf16[864,1152]{1,0:T(8,128)(2,1)}, bf16[864,1152]{1,0:T(8,128)(2,1)S(1)}, u32[]{:S(2)}, u32[]{:S(2)}) collective-permute-start(bf16[864,1152]{1,0:T(8,128)(2,1)} %collective-permute-done.8.refs_5_), channel_id=1, source_target_pairs={{0,8},{1,25},{8,16},{9,1},{16,24},{17,9},{24,0},{25,17},{2,10},{3,... | collective-permute-start | bytes 5971976 | tf_op jit(solution)/shard_map/ppermute | solution.py:485
  98.9 20.5 %collective-permute-start.22 = (bf16[864,1152]{1,0:T(8,128)(2,1)S(1)}, bf16[864,1152]{1,0:T(8,128)(2,1)S(1)}, u32[]{:S(2)}, u32[]{:S(2)}) collective-permute-start(bf16[864,1152]{1,0:T(8,128)(2,1)S(1)} %collective-permute-done.18.refs_6_), channel_id=1, source_target_pairs={{0,1},{1,0},{2,3},{3,2},{4,5},{5,4},{6,7},{7,6},{8,9},{9,8},{10,11... | collective-permute-start | bytes 5971976 | tf_op jit(solution)/shard_map/ppermute | solution.py:469
  101.4 18.0 %collective-permute-start.19 = (bf16[128,2304]{1,0:T(8,128)(2,1)S(1)}, bf16[128,2304]{1,0:T(8,128)(2,1)S(1)}, u32[]{:S(2)}, u32[]{:S(2)}) collective-permute-start(bf16[128,2304]{1,0:T(8,128)(2,1)S(1)} %join.2.refs_0_), channel_id=1, source_target_pairs={{0,32},{1,3},{2,34},{3,5},{4,36},{5,7},{6,38},{7,1},{32,64},{33,35... | collective-permute-start | bytes 1769480 | tf_op jit(solution)/shard_map/ppermute | solution.py:480
  103.1 16.3 %collective-permute-start.20 = (bf16[128,2304]{1,0:T(8,128)(2,1)S(1)}, bf16[128,2304]{1,0:T(8,128)(2,1)S(1)}, u32[]{:S(2)}, u32[]{:S(2)}) collective-permute-start(bf16[128,2304]{1,0:T(8,128)(2,1)S(1)} %join.2.refs_0_), channel_id=1, source_target_pairs={{0,64},{1,5},{2,66},{3,7},{4,68},{5,1},{6,70},{7,3},{32,96},{33,37... | collective-permute-start | bytes 1769480 | tf_op jit(solution)/shard_map/ppermute | solution.py:480
  105.1 14.3 %collective-permute-start.21 = (bf16[128,2304]{1,0:T(8,128)(2,1)S(1)}, bf16[128,2304]{1,0:T(8,128)(2,1)S(1)}, u32[]{:S(2)}, u32[]{:S(2)}) collective-permute-start(bf16[128,2304]{1,0:T(8,128)(2,1)S(1)} %join.2.refs_0_), channel_id=1, source_target_pairs={{0,96},{1,7},{2,98},{3,1},{4,100},{5,3},{6,102},{7,5},{32,0},{33,3... | collective-permute-start | bytes 1769480 | tf_op jit(solution)/shard_map/ppermute | solution.py:480
  119.4 8.7 %collective-permute-start.24 = (bf16[864,1152]{1,0:T(8,128)(2,1)S(1)}, bf16[864,1152]{1,0:T(8,128)(2,1)}, u32[]{:S(2)}, u32[]{:S(2)}) collective-permute-start(bf16[864,1152]{1,0:T(8,128)(2,1)S(1)} %collective-permute-done.23.refs_7_), channel_id=1, source_target_pairs={{0,1},{1,0},{2,3},{3,2},{4,5},{5,4},{6,7},{7,6},{8,9},{9,8},{10,11... | collective-permute-start | bytes 5971976 | tf_op jit(solution)/shard_map/ppermute | solution.py:469
  144.1 9.3 %collective-permute-start.25 = (bf16[128,2304]{1,0:T(8,128)(2,1)}, bf16[128,2304]{1,0:T(8,128)(2,1)S(1)}, u32[]{:S(2)}, u32[]{:S(2)}) collective-permute-start(bf16[128,2304]{1,0:T(8,128)(2,1)} %get-tuple-element.104), channel_id=1, source_target_pairs={{0,96},{1,7},{2,98},{3,1},{4,100},{5,3},{6,102},{7,5},{32,0},{33,3... | collective-permute-start | bytes 1769480 | tf_op jit(solution)/shard_map/ppermute | solution.py:480
  144.1 10.9 %collective-permute-start.26 = (bf16[128,2304]{1,0:T(8,128)(2,1)}, bf16[128,2304]{1,0:T(8,128)(2,1)S(1)}, u32[]{:S(2)}, u32[]{:S(2)}) collective-permute-start(bf16[128,2304]{1,0:T(8,128)(2,1)} %get-tuple-element.105), channel_id=1, source_target_pairs={{0,64},{1,5},{2,66},{3,7},{4,68},{5,1},{6,70},{7,3},{32,96},{33,37... | collective-permute-start | bytes 1769480 | tf_op jit(solution)/shard_map/ppermute | solution.py:480
  146.1 15.2 %collective-permute-start.27 = (bf16[128,2304]{1,0:T(8,128)(2,1)}, bf16[128,2304]{1,0:T(8,128)(2,1)S(1)}, u32[]{:S(2)}, u32[]{:S(2)}) collective-permute-start(bf16[128,2304]{1,0:T(8,128)(2,1)} %get-tuple-element.106), channel_id=1, source_target_pairs={{0,32},{1,3},{2,34},{3,5},{4,36},{5,7},{6,38},{7,1},{32,64},{33,35... | collective-permute-start | bytes 1769480 | tf_op jit(solution)/shard_map/ppermute | solution.py:480
  (36 other events, 491.8 us)

commit v6 on v5

--- a/solution.py
+++ b/solution.py
@@ -314,12 +314,18 @@
         hidden[:, cols] = (acted[:, cols] * two).astype(BF16)
     for copy in copies[2]:
         copy.wait()
+    stores = []
     for n in range(D // 256):
         rows = slice(n * 256, (n + 1) * 256)
         part = lax.dot_general(hidden[...], down[rows, :], (((1,), (1,)), ((), ())),
                                preferred_element_type=F32).astype(BF16)
+        tokens[:, rows] = part
         for e, out in enumerate(outs):
-            out[:, rows] = part[e * 128:(e + 1) * 128, :]
+            stores.append(pltpu.make_async_copy(tokens.at[e * 128:(e + 1) * 128, rows], out.at[:, rows],
+                                                sems.at[4 * n + e]))
+            stores[-1].start()
+    for store in stores:
+        store.wait()
 
 
 def feed(xs, pieces):
@@ -327,7 +333,7 @@
         feed_body,
         out_shape=(jax.ShapeDtypeStruct((4 * OWN, D), BF16),) * 4,
         in_specs=[hbm_spec()] * 12,
-        out_specs=(vmem_spec(),) * 4,
+        out_specs=(hbm_spec(),) * 4,
         scratch_shapes=[pltpu.VMEM((512, D), BF16), pltpu.VMEM((D, FF_DEV), BF16), pltpu.VMEM((D, FF_DEV), BF16),
                         pltpu.VMEM((D, FF_DEV), BF16), pltpu.VMEM((512, FF_DEV), BF16), pltpu.VMEM((512, FF_DEV), F32),
                         pltpu.SemaphoreType.DMA((52,))],

time: 187 us -> 187 us (level)
  no operation moved by 1% of the time
where the time goes in v6:
time: 187 us; the launch traced here: 186 us
  waiting for transfers between devices  67.8 us (36%)
  starting transfers between devices  60.9 us (33%)
  Pallas kernels  50.5 us (27%)
  local copies, waits for them, and re-layouts  5.94 us (3%)
    ppermute x18, starting transfers between devices, shift(): lax.ppermute(value, axis, [(i, (i + step) % size) for i in range(size)])  32.8 us
    ppermute x12, waiting for transfers between devices, cross(): return lax.ppermute(value, ('y', 'x', 'c'), pairs)  21.5 us
    ppermute x18, waiting for transfers between devices, shift(): lax.ppermute(value, axis, [(i, (i + step) % size) for i in range(size)])  19.6 us
    ppermute x3, waiting for transfers between devices, around(): return lax.ppermute(value, ('z', 'c'), pairs)  16.3 us
    pallas_call x1, Pallas kernels, feed(): pl.pallas_call(feed_body, out_shape=(jax.ShapeDtypeStruct((4 * OWN, D), B...  15.3 us
    pallas_call x4, Pallas kernels, attend(): pl.pallas_call(functools.partial(attend_body, diagonal), out_shape=jax.Sh...  13 us
    ppermute x12, starting transfers between devices, cross(): return lax.ppermute(value, ('y', 'x', 'c'), pairs)  10.8 us
    ppermute x2, waiting for transfers between devices, local(): lax.ppermute(p, ('y', 'c'), weight_pairs(s))  10.5 us
  transfers between devices with their start and end apart: 36, of which 21 were waited for; matrix products, arithmetic and copies ran while one was open for 1% of the time, Pallas kernels for 16%

profile of v6, /device:TPU:1, one launch (start us, length us, event | category | flops | bytes accessed | tf_op | source)
XLA Modules:
  0.0 186.4 jit_solution(16229026730402465335)
XLA Ops:
  2.4 6.2 %collective-permute-start.3 = (bf16[432,1152]{1,0:T(8,128)(2,1)}, bf16[432,1152]{1,0:T(8,128)(2,1)S(1)}, u32[]{:S(2)}, u32[]{:S(2)}) collective-permute-start(bf16[432,1152]{1,0:T(8,128)(2,1)} %get-tuple-element.66), channel_id=1, source_target_pairs={{0,0},{1,64},{32,32},{33,96},{64,1},{65,65},{96,33},{97,97},{2,2},... | collective-permute-start | bytes 2985992 | tf_op jit(solution)/shard_map/ppermute | solution.py:513
  10.4 9.4 %begin.1 = (bf16[256,512]{1,0:T(8,128)(2,1)}, bf16[4,272,512]{2,1,0:T(8,128)(2,1)}, bf16[32,2304]{1,0:T(8,128)(2,1)}) custom-call(s32[1]{0:T(128)S(6)} %copy.18.occupied, bf16[1024,2304]{1,0:T(8,128)(2,1)} %block.1, s32[1,256]{1,0:T(1,128)} %bitcast.7, f32[1,2304]{1,0:T(1,128)} %broadcast_in_dim.36.gain, f32[1,128]{1,0:T(1,128)} %constant.64.clone.frequency, ...), custom_call_target="tpu_custom_call" | custom-call | tf_op jit(solution)/shard_map/begin/pallas_call | solution.py:103
  19.9 5.2 %all-to-all-start = ((bf16[4,272,512]{2,1,0:T(8,128)(2,1)}), bf16[4,272,512]{2,1,0:T(8,128)(2,1)S(1)}, u32[]{:S(2)}, u32[]{:S(2)}) async-start(bf16[4,272,512]{2,1,0:T(8,128)(2,1)} %get-tuple-element.64), calls=%async_computation | async-start | bytes 2228224 | tf_op jit(solution)/shard_map/all_to_all | solution.py:516
  27.7 3.5 %collective-permute-done.3.first = bf16[432,1152]{1,0:T(8,128)(2,1)S(1)} collective-permute-done((bf16[432,1152]{1,0:T(8,128)(2,1)}, bf16[432,1152]{1,0:T(8,128)(2,1)S(1)}, u32[]{:S(2)}, u32[]{:S(2)}) %collective-permute-start.3) | collective-permute-done | bytes 995360 | tf_op jit(solution)/shard_map/ppermute | solution.py:513
  31.3 6.9 %collective-permute-done.4.second = bf16[432,1152]{1,0:T(8,128)(2,1)} collective-permute-done((bf16[432,1152]{1,0:T(8,128)(2,1)}, bf16[432,1152]{1,0:T(8,128)(2,1)}, u32[]{:S(2)}, u32[]{:S(2)}) %collective-permute-start.4) | collective-permute-done | bytes 995360 | tf_op jit(solution)/shard_map/ppermute | solution.py:513
  38.2 2.8 %merge.1.refs_4_ = bf16[864,1152]{1,0:T(8,128)(2,1)} custom-call(bf16[432,1152]{1,0:T(8,128)(2,1)} %copy-done.16, bf16[432,1152]{1,0:T(8,128)(2,1)} %collective-permute-done.4.second), custom_call_target="tpu_custom_call" | custom-call | tf_op jit(solution)/shard_map/merge/pallas_call | solution.py:391
  42.9 3.8 %collective-permute-start.8 = (bf16[864,1152]{1,0:T(8,128)(2,1)}, bf16[864,1152]{1,0:T(8,128)(2,1)}, u32[]{:S(2)}, u32[]{:S(2)}) collective-permute-start(bf16[864,1152]{1,0:T(8,128)(2,1)} %merge.1.refs_4_), channel_id=1, source_target_pairs={{0,8},{1,25},{8,16},{9,1},{16,24},{17,9},{24,0},{25,17},{2,10},{3,... | collective-permute-start | bytes 5971976 | tf_op jit(solution)/shard_map/ppermute | solution.py:491
  46.6 3.4 %attend.6 = bf16[272,512]{1,0:T(8,128)(2,1)} custom-call(s32[4]{0:T(128)S(1)} %broadcast_in_dim.39.at, f32[4]{0:T(128)S(1)} %broadcast_multiply_fusion.scale, bf16[256,512]{1,0:T(8,128)(2,1)S(1)} %collective-permute-done.2.q, bf16[4,272,512]{2,1,0:T(8,128)(2,1)S(1)} %all-to-all-done.kv), custom_call_target="tpu_custom_call" | custom-call | tf_op jit(solution)/shard_map/attend/pallas_call | solution.py:188
  51.5 3.4 %attend.5 = bf16[272,512]{1,0:T(8,128)(2,1)} custom-call(s32[4]{0:T(128)S(1)} %broadcast_in_dim.38.at, f32[4]{0:T(128)S(1)} %broadcast_multiply_fusion.scale, bf16[256,512]{1,0:T(8,128)(2,1)S(1)} %collective-permute-done.1.q, bf16[4,272,512]{2,1,0:T(8,128)(2,1)S(1)} %all-to-all-done.kv), custom_call_target="tpu_custom_call" | custom-call | tf_op jit(solution)/shard_map/attend/pallas_call | solution.py:188
  57.1 3.4 %attend.4 = bf16[272,512]{1,0:T(8,128)(2,1)} custom-call(s32[4]{0:T(128)S(1)} %broadcast_in_dim.37.at, f32[4]{0:T(128)S(1)} %broadcast_multiply_fusion.scale, bf16[256,512]{1,0:T(8,128)(2,1)S(1)} %copy-done.9, bf16[4,272,512]{2,1,0:T(8,128)(2,1)S(1)} %all-to-all-done.kv), custom_call_target="tpu_custom_call" | custom-call | tf_op jit(solution)/shard_map/attend/pallas_call | solution.py:188
  62.5 2.8 %attend.7.p3 = bf16[272,512]{1,0:T(8,128)(2,1)S(1)} custom-call(s32[4]{0:T(128)S(1)} %pad_add_fusion.at, f32[4]{0:T(128)S(1)} %broadcast_multiply_fusion.scale, bf16[256,512]{1,0:T(8,128)(2,1)S(1)} %copy-done.7, bf16[4,272,512]{2,1,0:T(8,128)(2,1)S(1)} %all-to-all-done.kv), custom_call_target="tpu_custom_call" | custom-call | tf_op jit(solution)/shard_map/attend/pallas_call | solution.py:188
  65.9 3.8 %collective-permute-done.5.p0 = bf16[272,512]{1,0:T(8,128)(2,1)} collective-permute-done((bf16[272,512]{1,0:T(8,128)(2,1)}, bf16[272,512]{1,0:T(8,128)(2,1)}, u32[]{:S(2)}, u32[]{:S(2)}) %collective-permute-start.5) | collective-permute-done | bytes 278560 | tf_op jit(solution)/shard_map/ppermute | solution.py:475
  69.6 3.2 %collective-permute-start.10 = (bf16[864,1152]{1,0:T(8,128)(2,1)}, bf16[864,1152]{1,0:T(8,128)(2,1)S(1)}, u32[]{:S(2)}, u32[]{:S(2)}) collective-permute-start(bf16[864,1152]{1,0:T(8,128)(2,1)} %merge.1.refs_4_), channel_id=1, source_target_pairs={{0,1},{1,0},{2,3},{3,2},{4,5},{5,4},{6,7},{7,6},{8,9},{9,8},{10,11... | collective-permute-start | bytes 5971976 | tf_op jit(solution)/shard_map/ppermute | solution.py:475
  72.8 3.2 %mix.1 = (f32[128,2304]{1,0:T(8,128)S(1)}, bf16[128,2304]{1,0:T(8,128)(2,1)S(1)}) custom-call(bf16[272,512]{1,0:T(8,128)(2,1)} %collective-permute-done.5.p0, bf16[272,512]{1,0:T(8,128)(2,1)} %collective-permute-done.6.p1, bf16[272,512]{1,0:T(8,128)(2,1)} %collective-permute-done.7.p2, bf16[272,512]{1,0:T(8,128)(2,1)S(1)} %attend.7.p3, ...), custom_call_target="tpu_custom_call" | custom-call | tf_op jit(solution)/shard_map/mix/pallas_call | solution.py:228
  86.8 4.1 %collective-permute-done.12.r2 = bf16[32,2304]{1,0:T(8,128)(2,1)S(1)} collective-permute-done((bf16[32,2304]{1,0:T(8,128)(2,1)S(1)}, bf16[32,2304]{1,0:T(8,128)(2,1)S(1)}, u32[]{:S(2)}, u32[]{:S(2)}) %collective-permute-start.12) | collective-permute-done | bytes 147488 | tf_op jit(solution)/shard_map/ppermute | solution.py:475
  95.5 2.8 %collective-permute-done.18.refs_6_ = bf16[864,1152]{1,0:T(8,128)(2,1)S(1)} collective-permute-done((bf16[864,1152]{1,0:T(8,128)(2,1)}, bf16[864,1152]{1,0:T(8,128)(2,1)S(1)}, u32[]{:S(2)}, u32[]{:S(2)}) %collective-permute-start.18) | collective-permute-done | bytes 1990688 | tf_op jit(solution)/shard_map/ppermute | solution.py:491
  105.8 13.5 %collective-permute-done.23.refs_7_ = bf16[864,1152]{1,0:T(8,128)(2,1)S(1)} collective-permute-done((bf16[864,1152]{1,0:T(8,128)(2,1)}, bf16[864,1152]{1,0:T(8,128)(2,1)S(1)}, u32[]{:S(2)}, u32[]{:S(2)}) %collective-permute-start.23) | collective-permute-done | bytes 1990688 | tf_op jit(solution)/shard_map/ppermute | solution.py:491
  119.4 4.9 %collective-permute-start.24 = (bf16[864,1152]{1,0:T(8,128)(2,1)S(1)}, bf16[864,1152]{1,0:T(8,128)(2,1)}, u32[]{:S(2)}, u32[]{:S(2)}) collective-permute-start(bf16[864,1152]{1,0:T(8,128)(2,1)S(1)} %collective-permute-done.23.refs_7_), channel_id=1, source_target_pairs={{0,1},{1,0},{2,3},{3,2},{4,5},{5,4},{6,7},{7,6},{8,9},{9,8},{10,11... | collective-permute-start | bytes 5971976 | tf_op jit(solution)/shard_map/ppermute | solution.py:475
  124.4 3.7 %collective-permute-done.24.refs_11_ = bf16[864,1152]{1,0:T(8,128)(2,1)} collective-permute-done((bf16[864,1152]{1,0:T(8,128)(2,1)S(1)}, bf16[864,1152]{1,0:T(8,128)(2,1)}, u32[]{:S(2)}, u32[]{:S(2)}) %collective-permute-start.24) | collective-permute-done | bytes 1990688 | tf_op jit(solution)/shard_map/ppermute | solution.py:475
  128.2 15.3 %feed.1 = (bf16[128,2304]{1,0:T(8,128)(2,1)}, bf16[128,2304]{1,0:T(8,128)(2,1)}, bf16[128,2304]{1,0:T(8,128)(2,1)}, bf16[128,2304]{1,0:T(8,128)(2,1)}) custom-call(bf16[128,2304]{1,0:T(8,128)(2,1)} %copy-done.1, bf16[128,2304]{1,0:T(8,128)(2,1)} %copy-done.17, bf16[128,2304]{1,0:T(8,128)(2,1)} %copy-done.18, bf16[128,2304]{1,0:T(8,128)(2,1)} %copy-done.19, ...), custom_call_target="tpu_custom_call" | custom-call | tf_op jit(solution)/shard_map/feed/pallas_call | solution.py:332
  145.8 7.0 %collective-permute-done.25.p1 = bf16[128,2304]{1,0:T(8,128)(2,1)S(1)} collective-permute-done((bf16[128,2304]{1,0:T(8,128)(2,1)}, bf16[128,2304]{1,0:T(8,128)(2,1)S(1)}, u32[]{:S(2)}, u32[]{:S(2)}) %collective-permute-start.25) | collective-permute-done | bytes 589856 | tf_op jit(solution)/shard_map/ppermute | solution.py:486
  154.4 6.3 %collective-permute-done.27.p3 = bf16[128,2304]{1,0:T(8,128)(2,1)S(1)} collective-permute-done((bf16[128,2304]{1,0:T(8,128)(2,1)}, bf16[128,2304]{1,0:T(8,128)(2,1)S(1)}, u32[]{:S(2)}, u32[]{:S(2)}) %collective-permute-start.27) | collective-permute-done | bytes 589856 | tf_op jit(solution)/shard_map/ppermute | solution.py:486
  177.6 4.0 %collective-permute-start.34 = (bf16[128,2304]{1,0:T(8,128)(2,1)S(1)}, bf16[128,2304]{1,0:T(8,128)(2,1)S(1)}, u32[]{:S(2)}, u32[]{:S(2)}) collective-permute-start(bf16[128,2304]{1,0:T(8,128)(2,1)S(1)} %join.3.refs_0_), channel_id=1, source_target_pairs={{0,1},{1,0},{2,3},{3,2},{4,5},{5,4},{6,7},{7,6},{8,9},{9,8},{10,11... | collective-permute-start | bytes 1769480 | tf_op jit(solution)/shard_map/ppermute | solution.py:475
  183.2 3.1 %put_back.1 = bf16[1024,2304]{1,0:T(8,128)(2,1)} custom-call(s32[1]{0:T(128)S(6)} %copy.18.occupied, s32[1,256]{1,0:T(1,128)S(1)} %bitcast.8, bf16[1024,2304]{1,0:T(8,128)(2,1)S(1)} %hold.1.block, bf16[128,2304]{1,0:T(8,128)(2,1)S(1)} %join.3.refs_0_, bf16[128,2304]{1,0:T(8,128)(2,1)S(1)} %collective-permute-done.34.refs_1_), custom_call_target="tpu_custom_call" | custom-call | tf_op jit(solution)/shard_map/put_back/pallas_call | solution.py:460
  (124 shorter events, 59.5 us)
Async XLA Ops:
  2.4 28.9 %collective-permute-start.3 = (bf16[432,1152]{1,0:T(8,128)(2,1)}, bf16[432,1152]{1,0:T(8,128)(2,1)S(1)}, u32[]{:S(2)}, u32[]{:S(2)}) collective-permute-start(bf16[432,1152]{1,0:T(8,128)(2,1)} %get-tuple-element.66), channel_id=1, source_target_pairs={{0,0},{1,64},{32,32},{33,96},{64,1},{65,65},{96,33},{97,97},{2,2},... | collective-permute-start | bytes 2985992 | tf_op jit(solution)/shard_map/ppermute | solution.py:513
  8.6 29.6 %collective-permute-start.4 = (bf16[432,1152]{1,0:T(8,128)(2,1)}, bf16[432,1152]{1,0:T(8,128)(2,1)}, u32[]{:S(2)}, u32[]{:S(2)}) collective-permute-start(bf16[432,1152]{1,0:T(8,128)(2,1)} %get-tuple-element.67), channel_id=1, source_target_pairs={{0,32},{1,96},{32,0},{33,64},{64,33},{65,97},{96,1},{97,65},{2,34}... | collective-permute-start | bytes 2985992 | tf_op jit(solution)/shard_map/ppermute | solution.py:513
  19.9 23.0 %all-to-all-start = ((bf16[4,272,512]{2,1,0:T(8,128)(2,1)}), bf16[4,272,512]{2,1,0:T(8,128)(2,1)S(1)}, u32[]{:S(2)}, u32[]{:S(2)}) async-start(bf16[4,272,512]{2,1,0:T(8,128)(2,1)} %get-tuple-element.64), calls=%async_computation | async-start | bytes 2228224 | tf_op jit(solution)/shard_map/all_to_all | solution.py:516
  25.0 16.0 %collective-permute-start = (bf16[256,512]{1,0:T(8,128)(2,1)S(1)}, bf16[256,512]{1,0:T(8,128)(2,1)S(1)}, u32[]{:S(2)}, u32[]{:S(2)}) collective-permute-start(bf16[256,512]{1,0:T(8,128)(2,1)S(1)} %copy-done.6), channel_id=1, source_target_pairs={{0,32},{32,64},{64,96},{96,0},{1,33},{33,65},{65,97},{97,1},{2,34}... | collective-permute-start | bytes 786440 | tf_op jit(solution)/shard_map/ppermute | solution.py:475
  25.1 17.8 %collective-permute-start.1 = (bf16[256,512]{1,0:T(8,128)(2,1)S(1)}, bf16[256,512]{1,0:T(8,128)(2,1)S(1)}, u32[]{:S(2)}, u32[]{:S(2)}) collective-permute-start(bf16[256,512]{1,0:T(8,128)(2,1)S(1)} %copy-done.6), channel_id=1, source_target_pairs={{0,64},{32,96},{64,0},{96,32},{1,65},{33,97},{65,1},{97,33},{2,66}... | collective-permute-start | bytes 786440 | tf_op jit(solution)/shard_map/ppermute | solution.py:475
  25.3 17.5 %collective-permute-start.2 = (bf16[256,512]{1,0:T(8,128)(2,1)S(1)}, bf16[256,512]{1,0:T(8,128)(2,1)S(1)}, u32[]{:S(2)}, u32[]{:S(2)}) collective-permute-start(bf16[256,512]{1,0:T(8,128)(2,1)S(1)} %copy-done.6), channel_id=1, source_target_pairs={{0,96},{32,0},{64,32},{96,64},{1,97},{33,1},{65,33},{97,65},{2,98}... | collective-permute-start | bytes 786440 | tf_op jit(solution)/shard_map/ppermute | solution.py:475
  42.9 26.8 %collective-permute-start.8 = (bf16[864,1152]{1,0:T(8,128)(2,1)}, bf16[864,1152]{1,0:T(8,128)(2,1)}, u32[]{:S(2)}, u32[]{:S(2)}) collective-permute-start(bf16[864,1152]{1,0:T(8,128)(2,1)} %merge.1.refs_4_), channel_id=1, source_target_pairs={{0,8},{1,25},{8,16},{9,1},{16,24},{17,9},{24,0},{25,17},{2,10},{3,... | collective-permute-start | bytes 5971976 | tf_op jit(solution)/shard_map/ppermute | solution.py:491
  50.0 15.3 %collective-permute-start.7 = (bf16[272,512]{1,0:T(8,128)(2,1)}, bf16[272,512]{1,0:T(8,128)(2,1)}, u32[]{:S(2)}, u32[]{:S(2)}) collective-permute-start(bf16[272,512]{1,0:T(8,128)(2,1)} %attend.6), channel_id=1, source_target_pairs={{0,32},{32,64},{64,96},{96,0},{1,33},{33,65},{65,97},{97,1},{2,34}... | collective-permute-start | bytes 835592 | tf_op jit(solution)/shard_map/ppermute | solution.py:475
  54.9 11.0 %collective-permute-start.6 = (bf16[272,512]{1,0:T(8,128)(2,1)}, bf16[272,512]{1,0:T(8,128)(2,1)}, u32[]{:S(2)}, u32[]{:S(2)}) collective-permute-start(bf16[272,512]{1,0:T(8,128)(2,1)} %attend.5), channel_id=1, source_target_pairs={{0,64},{32,96},{64,0},{96,32},{1,65},{33,97},{65,1},{97,33},{2,66}... | collective-permute-start | bytes 835592 | tf_op jit(solution)/shard_map/ppermute | solution.py:475
  60.6 9.1 %collective-permute-start.5 = (bf16[272,512]{1,0:T(8,128)(2,1)}, bf16[272,512]{1,0:T(8,128)(2,1)}, u32[]{:S(2)}, u32[]{:S(2)}) collective-permute-start(bf16[272,512]{1,0:T(8,128)(2,1)} %attend.4), channel_id=1, source_target_pairs={{0,96},{32,0},{64,32},{96,64},{1,97},{33,1},{65,33},{97,65},{2,98}... | collective-permute-start | bytes 835592 | tf_op jit(solution)/shard_map/ppermute | solution.py:475
  69.6 10.7 %collective-permute-start.10 = (bf16[864,1152]{1,0:T(8,128)(2,1)}, bf16[864,1152]{1,0:T(8,128)(2,1)S(1)}, u32[]{:S(2)}, u32[]{:S(2)}) collective-permute-start(bf16[864,1152]{1,0:T(8,128)(2,1)} %merge.1.refs_4_), channel_id=1, source_target_pairs={{0,1},{1,0},{2,3},{3,2},{4,5},{5,4},{6,7},{7,6},{8,9},{9,8},{10,11... | collective-permute-start | bytes 5971976 | tf_op jit(solution)/shard_map/ppermute | solution.py:475
  72.8 12.5 %collective-permute-start.14 = (bf16[864,1152]{1,0:T(8,128)(2,1)}, bf16[864,1152]{1,0:T(8,128)(2,1)S(1)}, u32[]{:S(2)}, u32[]{:S(2)}) collective-permute-start(bf16[864,1152]{1,0:T(8,128)(2,1)} %collective-permute-done.8.refs_5_), channel_id=1, source_target_pairs={{0,1},{1,0},{2,3},{3,2},{4,5},{5,4},{6,7},{7,6},{8,9},{9,8},{10,11... | collective-permute-start | bytes 5971976 | tf_op jit(solution)/shard_map/ppermute | solution.py:475
  72.8 25.5 %collective-permute-start.18 = (bf16[864,1152]{1,0:T(8,128)(2,1)}, bf16[864,1152]{1,0:T(8,128)(2,1)S(1)}, u32[]{:S(2)}, u32[]{:S(2)}) collective-permute-start(bf16[864,1152]{1,0:T(8,128)(2,1)} %merge.1.refs_4_), channel_id=1, source_target_pairs={{0,24},{1,9},{8,0},{9,17},{16,8},{17,25},{24,16},{25,1},{2,26},{3,... | collective-permute-start | bytes 5971976 | tf_op jit(solution)/shard_map/ppermute | solution.py:491
  81.7 9.2 %collective-permute-start.12 = (bf16[32,2304]{1,0:T(8,128)(2,1)S(1)}, bf16[32,2304]{1,0:T(8,128)(2,1)S(1)}, u32[]{:S(2)}, u32[]{:S(2)}) collective-permute-start(bf16[32,2304]{1,0:T(8,128)(2,1)S(1)} %get-tuple-element.83), channel_id=1, source_target_pairs={{0,4},{2,6},{4,0},{6,2},{1,5},{3,7},{5,1},{7,3},{8,12},{10,14},{12... | collective-permute-start | bytes 442376 | tf_op jit(solution)/shard_map/ppermute | solution.py:475
  91.1 7.1 %collective-permute-start.15 = (bf16[32,2304]{1,0:T(8,128)(2,1)S(1)}, bf16[32,2304]{1,0:T(8,128)(2,1)S(1)}, u32[]{:S(2)}, u32[]{:S(2)}) collective-permute-start(bf16[32,2304]{1,0:T(8,128)(2,1)S(1)} %get-tuple-element.90.refs_0_), channel_id=1, source_target_pairs={{0,2},{1,33},{2,4},{3,35},{4,6},{5,37},{6,0},{7,39},{32,34},{33,65... | collective-permute-start | bytes 442376 | tf_op jit(solution)/shard_map/ppermute | solution.py:486
  93.9 25.5 %collective-permute-start.23 = (bf16[864,1152]{1,0:T(8,128)(2,1)}, bf16[864,1152]{1,0:T(8,128)(2,1)S(1)}, u32[]{:S(2)}, u32[]{:S(2)}) collective-permute-start(bf16[864,1152]{1,0:T(8,128)(2,1)} %collective-permute-done.8.refs_5_), channel_id=1, source_target_pairs={{0,8},{1,25},{8,16},{9,1},{16,24},{17,9},{24,0},{25,17},{2,10},{3,... | collective-permute-start | bytes 5971976 | tf_op jit(solution)/shard_map/ppermute | solution.py:491
  98.9 20.5 %collective-permute-start.22 = (bf16[864,1152]{1,0:T(8,128)(2,1)S(1)}, bf16[864,1152]{1,0:T(8,128)(2,1)S(1)}, u32[]{:S(2)}, u32[]{:S(2)}) collective-permute-start(bf16[864,1152]{1,0:T(8,128)(2,1)S(1)} %collective-permute-done.18.refs_6_), channel_id=1, source_target_pairs={{0,1},{1,0},{2,3},{3,2},{4,5},{5,4},{6,7},{7,6},{8,9},{9,8},{10,11... | collective-permute-start | bytes 5971976 | tf_op jit(solution)/shard_map/ppermute | solution.py:475
  101.4 18.0 %collective-permute-start.19 = (bf16[128,2304]{1,0:T(8,128)(2,1)S(1)}, bf16[128,2304]{1,0:T(8,128)(2,1)S(1)}, u32[]{:S(2)}, u32[]{:S(2)}) collective-permute-start(bf16[128,2304]{1,0:T(8,128)(2,1)S(1)} %join.2.refs_0_), channel_id=1, source_target_pairs={{0,32},{1,3},{2,34},{3,5},{4,36},{5,7},{6,38},{7,1},{32,64},{33,35... | collective-permute-start | bytes 1769480 | tf_op jit(solution)/shard_map/ppermute | solution.py:486
  103.1 16.3 %collective-permute-start.20 = (bf16[128,2304]{1,0:T(8,128)(2,1)S(1)}, bf16[128,2304]{1,0:T(8,128)(2,1)S(1)}, u32[]{:S(2)}, u32[]{:S(2)}) collective-permute-start(bf16[128,2304]{1,0:T(8,128)(2,1)S(1)} %join.2.refs_0_), channel_id=1, source_target_pairs={{0,64},{1,5},{2,66},{3,7},{4,68},{5,1},{6,70},{7,3},{32,96},{33,37... | collective-permute-start | bytes 1769480 | tf_op jit(solution)/shard_map/ppermute | solution.py:486
  105.1 14.3 %collective-permute-start.21 = (bf16[128,2304]{1,0:T(8,128)(2,1)S(1)}, bf16[128,2304]{1,0:T(8,128)(2,1)S(1)}, u32[]{:S(2)}, u32[]{:S(2)}) collective-permute-start(bf16[128,2304]{1,0:T(8,128)(2,1)S(1)} %join.2.refs_0_), channel_id=1, source_target_pairs={{0,96},{1,7},{2,98},{3,1},{4,100},{5,3},{6,102},{7,5},{32,0},{33,3... | collective-permute-start | bytes 1769480 | tf_op jit(solution)/shard_map/ppermute | solution.py:486
  119.4 8.7 %collective-permute-start.24 = (bf16[864,1152]{1,0:T(8,128)(2,1)S(1)}, bf16[864,1152]{1,0:T(8,128)(2,1)}, u32[]{:S(2)}, u32[]{:S(2)}) collective-permute-start(bf16[864,1152]{1,0:T(8,128)(2,1)S(1)} %collective-permute-done.23.refs_7_), channel_id=1, source_target_pairs={{0,1},{1,0},{2,3},{3,2},{4,5},{5,4},{6,7},{7,6},{8,9},{9,8},{10,11... | collective-permute-start | bytes 5971976 | tf_op jit(solution)/shard_map/ppermute | solution.py:475
  143.5 9.3 %collective-permute-start.25 = (bf16[128,2304]{1,0:T(8,128)(2,1)}, bf16[128,2304]{1,0:T(8,128)(2,1)S(1)}, u32[]{:S(2)}, u32[]{:S(2)}) collective-permute-start(bf16[128,2304]{1,0:T(8,128)(2,1)} %get-tuple-element.104), channel_id=1, source_target_pairs={{0,96},{1,7},{2,98},{3,1},{4,100},{5,3},{6,102},{7,5},{32,0},{33,3... | collective-permute-start | bytes 1769480 | tf_op jit(solution)/shard_map/ppermute | solution.py:486
  143.6 10.9 %collective-permute-start.26 = (bf16[128,2304]{1,0:T(8,128)(2,1)}, bf16[128,2304]{1,0:T(8,128)(2,1)S(1)}, u32[]{:S(2)}, u32[]{:S(2)}) collective-permute-start(bf16[128,2304]{1,0:T(8,128)(2,1)} %get-tuple-element.105), channel_id=1, source_target_pairs={{0,64},{1,5},{2,66},{3,7},{4,68},{5,1},{6,70},{7,3},{32,96},{33,37... | collective-permute-start | bytes 1769480 | tf_op jit(solution)/shard_map/ppermute | solution.py:486
  145.5 15.2 %collective-permute-start.27 = (bf16[128,2304]{1,0:T(8,128)(2,1)}, bf16[128,2304]{1,0:T(8,128)(2,1)S(1)}, u32[]{:S(2)}, u32[]{:S(2)}) collective-permute-start(bf16[128,2304]{1,0:T(8,128)(2,1)} %get-tuple-element.106), channel_id=1, source_target_pairs={{0,32},{1,3},{2,34},{3,5},{4,36},{5,7},{6,38},{7,1},{32,64},{33,35... | collective-permute-start | bytes 1769480 | tf_op jit(solution)/shard_map/ppermute | solution.py:486
  (36 other events, 490.1 us)
